TPU v7x, 256 devices: a whole 4x4x8 slice. The times are simulated.
256 devices in a mesh: layer: 4 (over x), row: 8 (over z_hi, core), col: 8 (over y, z_lo).
Axes of the slice: x: 4, y: 4, z: 8 (z_hi: 4, z_lo: 2; z = z_hi * 2 + z_lo), core: 2. Of those that a mesh axis runs over, the one named last changes fastest.
Arguments:
- even_left: bfloat16 [2, 4, 32, 32, 256, 128], P(None, 'layer', 'row', 'col'), may hold values from -0.09375 to 0.09375
- even_right: bfloat16 [2, 4, 32, 32, 256, 128], P(None, 'layer', 'row', 'col'), may hold values from -0.25 to 0.25
- odd_left: bfloat16 [2, 4, 32, 32, 256, 128], P(None, 'layer', 'col', 'row'), may hold values from -0.09375 to 0.09375
- odd_right: bfloat16 [2, 4, 32, 32, 256, 128], P(None, 'layer', 'col', 'row'), may hold values from -0.25 to 0.25
- even_ranks: int32 [2, 4, 32, 32], P(None, 'layer', 'row', 'col'), may hold values from 16 to 64, as said below
- odd_ranks: int32 [2, 4, 32, 32], P(None, 'layer', 'col', 'row'), may hold values from 16 to 64, as said below
- even_sources: float32 [2, 4, 2, 8192, 128], P(None, 'layer', None, ('row', 'col')), may hold values from -6 to 6
- odd_sources: float32 [2, 4, 2, 8192, 128], P(None, 'layer', None, ('col', 'row')), may hold values from -6 to 6
Outputs:
- even_traces: float32 [4, 2, 8192, 128], P('layer', None, ('row', 'col'))
- odd_traces: float32 [4, 2, 8192, 128], P('layer', None, ('col', 'row'))
Inputs may be any that keep to these rules, and one draw needn't show every extreme that they name: `even_ranks`: every direction and pair has a tile of rank 64 and a tile of rank a quarter of 64. `odd_ranks`: every direction and pair has a tile of rank 64 and a tile of rank a quarter of 64.
All inputs are finite; a program needn't handle non-finite values.
Results may differ from a plain program's by a relative error of at most 0.008.
Values may be sent and summed in bfloat16 or wider, within the bound.
No kernel may reach another device: no remote copies, remote signals or barrier semaphores. Data moves between devices by JAX's collectives and lax.ppermute only.
A program may use at most 128 MiB of HBM per device.

v0:
```python
import jax
import jax.numpy as jnp
from jax import lax
from jax.sharding import PartitionSpec as P


def shifted(shard, axis, by):
    size = lax.axis_size(axis)
    pairs = [(i, i + by) for i in range(size) if 0 <= i + by < size]
    return lax.ppermute(shard, axis, pairs)


def tile_product(gathered, left_factor, right_factor, tile_ranks):
    batch_count = gathered.shape[0]
    tile_rows, tile_cols, tile_size, twice_rank = right_factor.shape
    half_rank = twice_rank // 2
    width = gathered.shape[2]
    half_cols = width // 2
    traces = gathered.reshape(batch_count, tile_cols, tile_size, width)
    products = jnp.einsum(
        "acnr,kcnb->kacrb", right_factor, traces, preferred_element_type=jnp.float32
    )
    real_part = (
        products[:, :, :, :half_rank, :half_cols] - products[:, :, :, half_rank:, half_cols:]
    )
    imag_part = (
        products[:, :, :, :half_rank, half_cols:] + products[:, :, :, half_rank:, :half_cols]
    )
    rank_mask = (lax.iota(jnp.int32, half_rank)[None, None, :] < tile_ranks[:, :, None]).astype(
        jnp.float32
    )
    rank_mask = rank_mask[None, :, :, :, None]
    real_part = real_part * rank_mask
    imag_part = imag_part * rank_mask
    stacked = jnp.concatenate(
        [
            jnp.concatenate([real_part, imag_part], axis=4),
            jnp.concatenate([-imag_part, real_part], axis=4),
        ],
        axis=3,
    ).astype(jnp.bfloat16)
    result = jnp.einsum(
        "acmr,kacrb->kamb", left_factor, stacked, preferred_element_type=jnp.float32
    )
    return result.reshape(batch_count, tile_rows * tile_size, width)


def on_device(
    even_left, even_right, odd_left, odd_right, even_ranks, odd_ranks, even_sources, odd_sources
):
    segments = lax.axis_size("layer")
    batches = even_sources.shape[2]

    def even_product(gathered, direction):
        return tile_product(
            gathered, even_left[direction, 0], even_right[direction, 0], even_ranks[direction, 0]
        )

    def odd_product(gathered, direction):
        return tile_product(
            gathered, odd_left[direction, 0], odd_right[direction, 0], odd_ranks[direction, 0]
        )

    def even_terms(current, direction):
        gathered = lax.all_gather(current.astype(jnp.bfloat16), "row", axis=1, tiled=True)
        return even_product(gathered, direction)

    def odd_terms(current, direction):
        gathered = lax.all_gather(current.astype(jnp.bfloat16), "col", axis=1, tiled=True)
        return odd_product(gathered, direction)

    def even_reduce(terms):
        return lax.psum_scatter(terms, "col", scatter_dimension=1, tiled=True)

    def odd_reduce(terms):
        return lax.psum_scatter(terms, "row", scatter_dimension=1, tiled=True)

    def advance(down_in, up_in, sources):
        down_even_src, down_odd_src, up_even_src, up_odd_src = sources
        down_even = even_reduce(even_terms(down_in, 0)) + down_even_src
        up_odd = odd_reduce(odd_terms(up_in, 1)) + up_odd_src
        down_odd = odd_reduce(odd_terms(down_even, 0)) + down_odd_src
        up_even = even_reduce(even_terms(up_odd, 1)) + up_even_src
        return (down_even, down_odd, up_even, up_odd)

    def pass_on(down_odd, up_even):
        down_next = shifted(down_odd.astype(jnp.bfloat16), "layer", 1).astype(down_odd.dtype)
        up_next = shifted(up_even.astype(jnp.bfloat16), "layer", -1).astype(up_even.dtype)
        return (down_next, up_next)

    sources_all = (even_sources[0, 0], odd_sources[0, 0], even_sources[1, 0], odd_sources[1, 0])

    def whole_chain(sources):
        down_in = jnp.zeros_like(sources[1])
        up_in = jnp.zeros_like(sources[2])
        outcome = None
        for step_index in range(segments):
            outcome = advance(down_in, up_in, sources)
            if step_index + 1 < segments:
                down_in, up_in = pass_on(outcome[1], outcome[2])
        return outcome

    per_batch = [
        whole_chain(tuple((source[batch_index : batch_index + 1] for source in sources_all)))
        for batch_index in range(batches)
    ]
    results = tuple(
        (
            jnp.concatenate([member[position] for member in per_batch], axis=0)
            for position in range(4)
        )
    )
    even_traces = (results[0] + results[2])[None]
    odd_traces = (results[1] + results[3])[None]
    return (even_traces, odd_traces)


def solution(mesh):
    in_specs = (
        P(None, "layer", "row", "col", None, None),
        P(None, "layer", "row", "col", None, None),
        P(None, "layer", "col", "row", None, None),
        P(None, "layer", "col", "row", None, None),
        P(None, "layer", "row", "col"),
        P(None, "layer", "col", "row"),
        P(None, "layer", None, ("row", "col"), None),
        P(None, "layer", None, ("col", "row"), None),
    )
    out_specs = (P("layer", None, ("row", "col"), None), P("layer", None, ("col", "row"), None))
    return jax.shard_map(
        on_device, mesh=mesh, in_specs=in_specs, out_specs=out_specs, check_vma=False
    )
```

profile of v0, /device:TPU:1, one launch (start us, length us, event | category | flops | bytes accessed | tf_op | source)
XLA Modules:
  0.0 1572.0 jit_solution(10573643973686548330)
XLA Ops:
  26.5 28.9 %reduce-scatter.31.cloned.1.call-done = f32[1,128,128]{2,1,0:T(8,128)} async-done(((f32[1,1024,128]{2,1,0:T(8,128)}), f32[1,128,128]{2,1,0:T(8,128)}) %reduce-scatter.31.cloned.1.call-update) | async-done | bytes 65552 | tf_op jit(solution)/shard_map/reduce_scatter | solution.py:73
  56.2 22.6 %all_gather.88 = bf16[1,1024,128]{2,1,0:T(8,128)(2,1)S(1)} all-gather(bf16[1,128,128]{2,1,0:T(8,128)(2,1)S(1)} %get-tuple-element.110), channel_id=1, replica_groups=mesh['layer'=4,'row'=8,'col'=8] {'col'}, dimensions={1}, use_global_device_ids=true | all-gather | bytes 294912 | tf_op jit(solution)/shard_map/all_gather | solution.py:69
  78.8 24.9 %all_gather.94 = bf16[1,1024,128]{2,1,0:T(8,128)(2,1)S(1)} all-gather(bf16[1,128,128]{2,1,0:T(8,128)(2,1)S(1)} %get-tuple-element.111), channel_id=1, replica_groups=mesh['layer'=4,'row'=8,'col'=8] {'col'}, dimensions={1}, use_global_device_ids=true | all-gather | bytes 294912 | tf_op jit(solution)/shard_map/all_gather | solution.py:69
  116.4 43.0 %reduce-scatter.33.cloned.1.call-done = f32[1,128,128]{2,1,0:T(8,128)} async-done(((f32[1,1024,128]{2,1,0:T(8,128)}), f32[1,128,128]{2,1,0:T(8,128)}) %reduce-scatter.33.cloned.1.call-update) | async-done | bytes 65552 | tf_op jit(solution)/shard_map/reduce_scatter | solution.py:76
  159.4 38.3 %reduce-scatter.45.cloned.1.call-done = f32[1,128,128]{2,1,0:T(8,128)} async-done(((f32[1,1024,128]{2,1,0:T(8,128)}), f32[1,128,128]{2,1,0:T(8,128)}) %reduce-scatter.45.cloned.1.call-update) | async-done | bytes 65552 | tf_op jit(solution)/shard_map/reduce_scatter | solution.py:76
  199.4 17.2 %all_gather.100 = bf16[1,1024,128]{2,1,0:T(8,128)(2,1)S(1)} all-gather(bf16[1,128,128]{2,1,0:T(8,128)(2,1)S(1)} %get-tuple-element.108), channel_id=1, replica_groups=mesh['layer'=4,'row'=8,'col'=8] {'row'}, dimensions={1}, use_global_device_ids=true | all-gather | bytes 294912 | tf_op jit(solution)/shard_map/all_gather | solution.py:65
  216.6 14.8 all_gather.107
  250.4 15.9 %all_gather.89 = bf16[1,1024,128]{2,1,0:T(8,128)(2,1)S(1)} all-gather(bf16[1,128,128]{2,1,0:T(8,128)(2,1)} %collective-permute-done), channel_id=1, replica_groups=mesh['layer'=4,'row'=8,'col'=8] {'row'}, dimensions={1}, use_global_device_ids=true | all-gather | bytes 294912 | tf_op jit(solution)/shard_map/all_gather | solution.py:65
  294.9 18.5 %reduce-scatter.73.cloned.1.call-done = f32[1,128,128]{2,1,0:T(8,128)} async-done(((f32[1,1024,128]{2,1,0:T(8,128)}), f32[1,128,128]{2,1,0:T(8,128)}) %reduce-scatter.73.cloned.1.call-update) | async-done | bytes 65552 | tf_op jit(solution)/shard_map/reduce_scatter | solution.py:73
  313.4 41.3 %reduce-scatter.35.cloned.1.call-done = f32[1,128,128]{2,1,0:T(8,128)} async-done(((f32[1,1024,128]{2,1,0:T(8,128)}), f32[1,128,128]{2,1,0:T(8,128)}) %reduce-scatter.35.cloned.1.call-update) | async-done | bytes 65552 | tf_op jit(solution)/shard_map/reduce_scatter | solution.py:73
  354.7 41.5 %reduce-scatter.47.cloned.1.call-done = f32[1,128,128]{2,1,0:T(8,128)} async-done(((f32[1,1024,128]{2,1,0:T(8,128)}), f32[1,128,128]{2,1,0:T(8,128)}) %reduce-scatter.47.cloned.1.call-update) | async-done | bytes 65552 | tf_op jit(solution)/shard_map/reduce_scatter | solution.py:73
  397.8 22.3 %all_gather.90 = bf16[1,1024,128]{2,1,0:T(8,128)(2,1)S(1)} all-gather(bf16[1,128,128]{2,1,0:T(8,128)(2,1)S(1)} %get-tuple-element.151), channel_id=1, replica_groups=mesh['layer'=4,'row'=8,'col'=8] {'col'}, dimensions={1}, use_global_device_ids=true | all-gather | bytes 294912 | tf_op jit(solution)/shard_map/all_gather | solution.py:69
  420.1 23.0 %all_gather.96 = bf16[1,1024,128]{2,1,0:T(8,128)(2,1)S(1)} all-gather(bf16[1,128,128]{2,1,0:T(8,128)(2,1)S(1)} %get-tuple-element.152), channel_id=1, replica_groups=mesh['layer'=4,'row'=8,'col'=8] {'col'}, dimensions={1}, use_global_device_ids=true | all-gather | bytes 294912 | tf_op jit(solution)/shard_map/all_gather | solution.py:69
  458.2 23.0 %all_gather.108 = bf16[1,1024,128]{2,1,0:T(8,128)(2,1)S(1)} all-gather(bf16[1,128,128]{2,1,0:T(8,128)(2,1)} %collective-permute-done.9), channel_id=1, replica_groups=mesh['layer'=4,'row'=8,'col'=8] {'col'}, dimensions={1}, use_global_device_ids=true | all-gather | bytes 294912 | tf_op jit(solution)/shard_map/all_gather | solution.py:69
  481.2 24.3 %all_gather.101 = bf16[1,1024,128]{2,1,0:T(8,128)(2,1)S(1)} all-gather(bf16[1,128,128]{2,1,0:T(8,128)(2,1)S(1)} %collective-permute-done.6), channel_id=1, replica_groups=mesh['layer'=4,'row'=8,'col'=8] {'col'}, dimensions={1}, use_global_device_ids=true | all-gather | bytes 294912 | tf_op jit(solution)/shard_map/all_gather | solution.py:69
  518.0 22.0 %reduce-scatter.49.cloned.1.call-done = f32[1,128,128]{2,1,0:T(8,128)} async-done(((f32[1,1024,128]{2,1,0:T(8,128)}), f32[1,128,128]{2,1,0:T(8,128)}) %reduce-scatter.49.cloned.1.call-update) | async-done | bytes 65552 | tf_op jit(solution)/shard_map/reduce_scatter | solution.py:76
  540.0 37.4 %reduce-scatter.61.cloned.1.call-done = f32[1,128,128]{2,1,0:T(8,128)} async-done(((f32[1,1024,128]{2,1,0:T(8,128)}), f32[1,128,128]{2,1,0:T(8,128)}) %reduce-scatter.61.cloned.1.call-update) | async-done | bytes 65552 | tf_op jit(solution)/shard_map/reduce_scatter | solution.py:76
  577.4 38.2 %reduce-scatter.75.cloned.1.call-done = f32[1,128,128]{2,1,0:T(8,128)} async-done(((f32[1,1024,128]{2,1,0:T(8,128)}), f32[1,128,128]{2,1,0:T(8,128)}) %reduce-scatter.75.cloned.1.call-update) | async-done | bytes 65552 | tf_op jit(solution)/shard_map/reduce_scatter | solution.py:76
  617.3 17.0 %all_gather.102 = bf16[1,1024,128]{2,1,0:T(8,128)(2,1)S(1)} all-gather(bf16[1,128,128]{2,1,0:T(8,128)(2,1)S(1)} %get-tuple-element.144), channel_id=1, replica_groups=mesh['layer'=4,'row'=8,'col'=8] {'row'}, dimensions={1}, use_global_device_ids=true | all-gather | bytes 294912 | tf_op jit(solution)/shard_map/all_gather | solution.py:65
  668.7 15.7 %all_gather.97 = bf16[1,1024,128]{2,1,0:T(8,128)(2,1)S(1)} all-gather(bf16[1,128,128]{2,1,0:T(8,128)(2,1)} %collective-permute-done.4), channel_id=1, replica_groups=mesh['layer'=4,'row'=8,'col'=8] {'row'}, dimensions={1}, use_global_device_ids=true | all-gather | bytes 294912 | tf_op jit(solution)/shard_map/all_gather | solution.py:65
  684.4 14.8 all_gather.91
  713.0 18.1 %reduce-scatter.77.cloned.1.call-done = f32[1,128,128]{2,1,0:T(8,128)} async-done(((f32[1,1024,128]{2,1,0:T(8,128)}), f32[1,128,128]{2,1,0:T(8,128)}) %reduce-scatter.77.cloned.1.call-update) | async-done | bytes 65552 | tf_op jit(solution)/shard_map/reduce_scatter | solution.py:73
  731.2 41.3 %reduce-scatter.39.cloned.1.call-done = f32[1,128,128]{2,1,0:T(8,128)} async-done(((f32[1,1024,128]{2,1,0:T(8,128)}), f32[1,128,128]{2,1,0:T(8,128)}) %reduce-scatter.39.cloned.1.call-update) | async-done | bytes 65552 | tf_op jit(solution)/shard_map/reduce_scatter | solution.py:73
  772.4 41.5 %reduce-scatter.51.cloned.1.call-done = f32[1,128,128]{2,1,0:T(8,128)} async-done(((f32[1,1024,128]{2,1,0:T(8,128)}), f32[1,128,128]{2,1,0:T(8,128)}) %reduce-scatter.51.cloned.1.call-update) | async-done | bytes 65552 | tf_op jit(solution)/shard_map/reduce_scatter | solution.py:73
  815.5 22.4 %all_gather.92 = bf16[1,1024,128]{2,1,0:T(8,128)(2,1)S(1)} all-gather(bf16[1,128,128]{2,1,0:T(8,128)(2,1)S(1)} %get-tuple-element.139), channel_id=1, replica_groups=mesh['layer'=4,'row'=8,'col'=8] {'col'}, dimensions={1}, use_global_device_ids=true | all-gather | bytes 294912 | tf_op jit(solution)/shard_map/all_gather | solution.py:69
  837.9 23.0 %all_gather.98 = bf16[1,1024,128]{2,1,0:T(8,128)(2,1)S(1)} all-gather(bf16[1,128,128]{2,1,0:T(8,128)(2,1)S(1)} %get-tuple-element.140), channel_id=1, replica_groups=mesh['layer'=4,'row'=8,'col'=8] {'col'}, dimensions={1}, use_global_device_ids=true | all-gather | bytes 294912 | tf_op jit(solution)/shard_map/all_gather | solution.py:69
  876.0 23.0 %all_gather.110 = bf16[1,1024,128]{2,1,0:T(8,128)(2,1)S(1)} all-gather(bf16[1,128,128]{2,1,0:T(8,128)(2,1)} %collective-permute-done.10), channel_id=1, replica_groups=mesh['layer'=4,'row'=8,'col'=8] {'col'}, dimensions={1}, use_global_device_ids=true | all-gather | bytes 294912 | tf_op jit(solution)/shard_map/all_gather | solution.py:69
  899.0 24.6 %all_gather.103 = bf16[1,1024,128]{2,1,0:T(8,128)(2,1)S(1)} all-gather(bf16[1,128,128]{2,1,0:T(8,128)(2,1)S(1)} %collective-permute-done.7), channel_id=1, replica_groups=mesh['layer'=4,'row'=8,'col'=8] {'col'}, dimensions={1}, use_global_device_ids=true | all-gather | bytes 294912 | tf_op jit(solution)/shard_map/all_gather | solution.py:69
  936.1 21.9 %reduce-scatter.53.cloned.1.call-done = f32[1,128,128]{2,1,0:T(8,128)} async-done(((f32[1,1024,128]{2,1,0:T(8,128)}), f32[1,128,128]{2,1,0:T(8,128)}) %reduce-scatter.53.cloned.1.call-update) | async-done | bytes 65552 | tf_op jit(solution)/shard_map/reduce_scatter | solution.py:76
  958.0 37.6 %reduce-scatter.65.cloned.1.call-done = f32[1,128,128]{2,1,0:T(8,128)} async-done(((f32[1,1024,128]{2,1,0:T(8,128)}), f32[1,128,128]{2,1,0:T(8,128)}) %reduce-scatter.65.cloned.1.call-update) | async-done | bytes 65552 | tf_op jit(solution)/shard_map/reduce_scatter | solution.py:76
  995.6 38.1 %reduce-scatter.79.cloned.1.call-done = f32[1,128,128]{2,1,0:T(8,128)} async-done(((f32[1,1024,128]{2,1,0:T(8,128)}), f32[1,128,128]{2,1,0:T(8,128)}) %reduce-scatter.79.cloned.1.call-update) | async-done | bytes 65552 | tf_op jit(solution)/shard_map/reduce_scatter | solution.py:76
  1035.5 17.1 %all_gather.104 = bf16[1,1024,128]{2,1,0:T(8,128)(2,1)S(1)} all-gather(bf16[1,128,128]{2,1,0:T(8,128)(2,1)S(1)} %get-tuple-element.132), channel_id=1, replica_groups=mesh['layer'=4,'row'=8,'col'=8] {'row'}, dimensions={1}, use_global_device_ids=true | all-gather | bytes 294912 | tf_op jit(solution)/shard_map/all_gather | solution.py:65
  1086.3 15.9 %all_gather.99 = bf16[1,1024,128]{2,1,0:T(8,128)(2,1)S(1)} all-gather(bf16[1,128,128]{2,1,0:T(8,128)(2,1)} %collective-permute-done.5), channel_id=1, replica_groups=mesh['layer'=4,'row'=8,'col'=8] {'row'}, dimensions={1}, use_global_device_ids=true | all-gather | bytes 294912 | tf_op jit(solution)/shard_map/all_gather | solution.py:65
  1102.2 14.8 all_gather.93
  1130.7 18.7 %reduce-scatter.81.cloned.1.call-done = f32[1,128,128]{2,1,0:T(8,128)} async-done(((f32[1,1024,128]{2,1,0:T(8,128)}), f32[1,128,128]{2,1,0:T(8,128)}) %reduce-scatter.81.cloned.1.call-update) | async-done | bytes 65552 | tf_op jit(solution)/shard_map/reduce_scatter | solution.py:73
  1149.4 41.3 %reduce-scatter.43.cloned.1.call-done = f32[1,128,128]{2,1,0:T(8,128)} async-done(((f32[1,1024,128]{2,1,0:T(8,128)}), f32[1,128,128]{2,1,0:T(8,128)}) %reduce-scatter.43.cloned.1.call-update) | async-done | bytes 65552 | tf_op jit(solution)/shard_map/reduce_scatter | solution.py:73
  1190.7 41.4 %reduce-scatter.55.cloned.1.call-done = f32[1,128,128]{2,1,0:T(8,128)} async-done(((f32[1,1024,128]{2,1,0:T(8,128)}), f32[1,128,128]{2,1,0:T(8,128)}) %reduce-scatter.55.cloned.1.call-update) | async-done | bytes 65552 | tf_op jit(solution)/shard_map/reduce_scatter | solution.py:73
  1233.7 22.3 %all_gather.114 = bf16[1,1024,128]{2,1,0:T(8,128)(2,1)S(1)} all-gather(bf16[1,128,128]{2,1,0:T(8,128)(2,1)S(1)} %get-tuple-element.104), channel_id=1, replica_groups=mesh['layer'=4,'row'=8,'col'=8] {'col'}, dimensions={1}, use_global_device_ids=true | all-gather | bytes 294912 | tf_op jit(solution)/shard_map/all_gather | solution.py:69
  1256.0 22.8 %all_gather.115 = bf16[1,1024,128]{2,1,0:T(8,128)(2,1)S(1)} all-gather(bf16[1,128,128]{2,1,0:T(8,128)(2,1)S(1)} %get-tuple-element.119), channel_id=1, replica_groups=mesh['layer'=4,'row'=8,'col'=8] {'col'}, dimensions={1}, use_global_device_ids=true | all-gather | bytes 294912 | tf_op jit(solution)/shard_map/all_gather | solution.py:69
  1291.4 22.5 %all_gather.112 = bf16[1,1024,128]{2,1,0:T(8,128)(2,1)S(1)} all-gather(bf16[1,128,128]{2,1,0:T(8,128)(2,1)} %collective-permute-done.11), channel_id=1, replica_groups=mesh['layer'=4,'row'=8,'col'=8] {'col'}, dimensions={1}, use_global_device_ids=true | all-gather | bytes 294912 | tf_op jit(solution)/shard_map/all_gather | solution.py:69
  1313.9 24.0 %all_gather.105 = bf16[1,1024,128]{2,1,0:T(8,128)(2,1)S(1)} all-gather(bf16[1,128,128]{2,1,0:T(8,128)(2,1)} %collective-permute-done.8), channel_id=1, replica_groups=mesh['layer'=4,'row'=8,'col'=8] {'col'}, dimensions={1}, use_global_device_ids=true | all-gather | bytes 294912 | tf_op jit(solution)/shard_map/all_gather | solution.py:69
  1345.4 29.6 %reduce-scatter.89.cloned.1.call-done = f32[1,128,128]{2,1,0:T(8,128)} async-done(((f32[1,1024,128]{2,1,0:T(8,128)}), f32[1,128,128]{2,1,0:T(8,128)}) %reduce-scatter.89.cloned.1.call-update) | async-done | bytes 65552 | tf_op jit(solution)/shard_map/reduce_scatter | solution.py:76
  1375.0 37.5 %reduce-scatter.69.cloned.1.call-done = f32[1,128,128]{2,1,0:T(8,128)} async-done(((f32[1,1024,128]{2,1,0:T(8,128)}), f32[1,128,128]{2,1,0:T(8,128)}) %reduce-scatter.69.cloned.1.call-update) | async-done | bytes 65552 | tf_op jit(solution)/shard_map/reduce_scatter | solution.py:76
  1412.5 38.3 %reduce-scatter.83.cloned.1.call-done = f32[1,128,128]{2,1,0:T(8,128)} async-done(((f32[1,1024,128]{2,1,0:T(8,128)}), f32[1,128,128]{2,1,0:T(8,128)}) %reduce-scatter.83.cloned.1.call-update) | async-done | bytes 65552 | tf_op jit(solution)/shard_map/reduce_scatter | solution.py:76
  1452.4 17.4 %all_gather.106 = bf16[1,1024,128]{2,1,0:T(8,128)(2,1)S(1)} all-gather(bf16[1,128,128]{2,1,0:T(8,128)(2,1)S(1)} %get-tuple-element.101), channel_id=1, replica_groups=mesh['layer'=4,'row'=8,'col'=8] {'row'}, dimensions={1}, use_global_device_ids=true | all-gather | bytes 294912 | tf_op jit(solution)/shard_map/all_gather | solution.py:65
  1469.7 15.0 all_gather.113
  1491.0 30.8 %reduce-scatter.71.cloned.1.call-done = f32[1,128,128]{2,1,0:T(8,128)} async-done(((f32[1,1024,128]{2,1,0:T(8,128)}), f32[1,128,128]{2,1,0:T(8,128)}) %reduce-scatter.71.cloned.1.call-update) | async-done | bytes 65552 | tf_op jit(solution)/shard_map/reduce_scatter | solution.py:73
  1521.8 41.4 %reduce-scatter.85.cloned.1.call-done = f32[1,128,128]{2,1,0:T(8,128)} async-done(((f32[1,1024,128]{2,1,0:T(8,128)}), f32[1,128,128]{2,1,0:T(8,128)}) %reduce-scatter.85.cloned.1.call-update) | async-done | bytes 65552 | tf_op jit(solution)/shard_map/reduce_scatter | solution.py:73
  (336 shorter events, 269.2 us)
Async XLA Ops:
  7.2 48.2 %reduce-scatter.31.cloned.1.call-start = ((), (), s32[]{:S(2)}) async-start(), calls=%async_computation.30 | async-start | bytes 589824 | tf_op jit(solution)/shard_map/reduce_scatter | solution.py:73
  15.6 100.9 %reduce-scatter.57.cloned.1.call-start = ((), (), s32[]{:S(2)}) async-start(), calls=%async_computation.43 | async-start | bytes 589824 | tf_op jit(solution)/shard_map/reduce_scatter | solution.py:76
  23.6 31.8 %copy-start.4 = (f32[2,1,2,128,128]{4,3,2,1,0:T(8,128)S(1)}, f32[2,1,2,128,128]{4,3,2,1,0:T(8,128)}, u32[]{:S(2)}) copy-start(f32[2,1,2,128,128]{4,3,2,1,0:T(8,128)} %param.14) | copy-start | bytes 786436
  25.7 133.7 %reduce-scatter.33.cloned.1.call-start = ((), (), s32[]{:S(2)}) async-start(), calls=%async_computation.31 | async-start | bytes 589824 | tf_op jit(solution)/shard_map/reduce_scatter | solution.py:76
  25.9 835.8 %copy-start.31 = (f32[4,4,64]{2,0,1:T(4,128)}, f32[4,4,64]{2,0,1:T(4,128)S(1)}, u32[]{:S(2)}) copy-start(f32[4,4,64]{2,0,1:T(4,128)S(1)} %fusion.311) | copy-start | bytes 12292
  110.3 87.5 %reduce-scatter.45.cloned.1.call-start = ((), (), s32[]{:S(2)}) async-start(), calls=%async_computation.37 | async-start | bytes 589824 | tf_op jit(solution)/shard_map/reduce_scatter | solution.py:76
  114.7 180.1 %reduce-scatter.59.cloned.1.call-start = ((), (), s32[]{:S(2)}) async-start(), calls=%async_computation.44 | async-start | bytes 589824 | tf_op jit(solution)/shard_map/reduce_scatter | solution.py:73
  237.7 75.7 %reduce-scatter.73.cloned.1.call-start = ((), (), s32[]{:S(2)}) async-start(), calls=%async_computation.51 | async-start | bytes 589824 | tf_op jit(solution)/shard_map/reduce_scatter | solution.py:73
  237.8 28.6 %collective-permute-start.3 = (bf16[1,128,128]{2,1,0:T(8,128)(2,1)S(1)}, bf16[1,128,128]{2,1,0:T(8,128)(2,1)S(1)}, u32[]{:S(2)}, u32[]{:S(2)}) collective-permute-start(bf16[1,128,128]{2,1,0:T(8,128)(2,1)S(1)} %get-tuple-element.156), channel_id=1, source_target_pairs={{0,64},{64,128},{128,192},{1,65},{65,129},{129,193},{2,66},{66,130... | collective-permute-start | bytes 98312 | tf_op jit(solution)/shard_map/ppermute | solution.py:10
  241.1 9.4 collective-permute-start
  250.4 104.4 %reduce-scatter.35.cloned.1.call-start = ((), (), s32[]{:S(2)}) async-start(), calls=%async_computation.32 | async-start | bytes 589824 | tf_op jit(solution)/shard_map/reduce_scatter | solution.py:73
  250.4 32.4 %copy-start.1 = (bf16[1,1,4,4,256,128]{4,5,2,3,1,0:T(8,128)(2,1)S(1)}, bf16[1,1,4,4,256,128]{4,5,2,3,1,0:T(8,128)(2,1)}, u32[]{:S(2)}) copy-start(bf16[1,1,4,4,256,128]{4,5,2,3,1,0:T(8,128)(2,1)} %copy-done) | copy-start | bytes 3145732
  288.6 107.6 %reduce-scatter.47.cloned.1.call-start = ((), (), s32[]{:S(2)}) async-start(), calls=%async_computation.38 | async-start | bytes 589824 | tf_op jit(solution)/shard_map/reduce_scatter | solution.py:73
  294.8 223.2 %reduce-scatter.37.cloned.1.call-start = ((), (), s32[]{:S(2)}) async-start(), calls=%async_computation.33 | async-start | bytes 589824 | tf_op jit(solution)/shard_map/reduce_scatter | solution.py:76
  449.3 90.7 %reduce-scatter.49.cloned.1.call-start = ((), (), s32[]{:S(2)}) async-start(), calls=%async_computation.39 | async-start | bytes 589824 | tf_op jit(solution)/shard_map/reduce_scatter | solution.py:76
  449.4 31.8 %collective-permute-start.6 = (bf16[1,128,128]{2,1,0:T(8,128)(2,1)S(1)}, bf16[1,128,128]{2,1,0:T(8,128)(2,1)S(1)}, u32[]{:S(2)}, u32[]{:S(2)}) collective-permute-start(bf16[1,128,128]{2,1,0:T(8,128)(2,1)S(1)} %get-tuple-element.150), channel_id=1, source_target_pairs={{64,0},{128,64},{192,128},{65,1},{129,65},{193,129},{66,2},{130,66... | collective-permute-start | bytes 98312 | tf_op jit(solution)/shard_map/ppermute | solution.py:10
  450.7 7.5 collective-permute-start.9
  458.1 119.3 %reduce-scatter.61.cloned.1.call-start = ((), (), s32[]{:S(2)}) async-start(), calls=%async_computation.45 | async-start | bytes 589824 | tf_op jit(solution)/shard_map/reduce_scatter | solution.py:76
  511.8 103.8 %reduce-scatter.75.cloned.1.call-start = ((), (), s32[]{:S(2)}) async-start(), calls=%async_computation.52 | async-start | bytes 589824 | tf_op jit(solution)/shard_map/reduce_scatter | solution.py:76
  518.0 195.0 %reduce-scatter.63.cloned.1.call-start = ((), (), s32[]{:S(2)}) async-start(), calls=%async_computation.46 | async-start | bytes 589824 | tf_op jit(solution)/shard_map/reduce_scatter | solution.py:73
  655.2 76.0 %reduce-scatter.77.cloned.1.call-start = ((), (), s32[]{:S(2)}) async-start(), calls=%async_computation.53 | async-start | bytes 589824 | tf_op jit(solution)/shard_map/reduce_scatter | solution.py:73
  655.2 29.2 %collective-permute-start.1 = (bf16[1,128,128]{2,1,0:T(8,128)(2,1)S(1)}, bf16[1,128,128]{2,1,0:T(8,128)(2,1)S(1)}, u32[]{:S(2)}, u32[]{:S(2)}) collective-permute-start(bf16[1,128,128]{2,1,0:T(8,128)(2,1)S(1)} %get-tuple-element.145), channel_id=1, source_target_pairs={{0,64},{64,128},{128,192},{1,65},{65,129},{129,193},{2,66},{66,130... | collective-permute-start | bytes 98312 | tf_op jit(solution)/shard_map/ppermute | solution.py:10
  658.8 9.9 collective-permute-start.4
  668.6 103.8 %reduce-scatter.39.cloned.1.call-start = ((), (), s32[]{:S(2)}) async-start(), calls=%async_computation.34 | async-start | bytes 589824 | tf_op jit(solution)/shard_map/reduce_scatter | solution.py:73
  668.7 32.2 %copy-start.2 = (bf16[1,1,4,4,256,128]{4,5,2,3,1,0:T(8,128)(2,1)S(1)}, bf16[1,1,4,4,256,128]{4,5,2,3,1,0:T(8,128)(2,1)}, u32[]{:S(2)}) copy-start(bf16[1,1,4,4,256,128]{4,5,2,3,1,0:T(8,128)(2,1)} %copy-done) | copy-start | bytes 3145732
  706.8 107.1 %reduce-scatter.51.cloned.1.call-start = ((), (), s32[]{:S(2)}) async-start(), calls=%async_computation.40 | async-start | bytes 589824 | tf_op jit(solution)/shard_map/reduce_scatter | solution.py:73
  712.9 223.1 %reduce-scatter.41.cloned.1.call-start = ((), (), s32[]{:S(2)}) async-start(), calls=%async_computation.35 | async-start | bytes 589824 | tf_op jit(solution)/shard_map/reduce_scatter | solution.py:76
  867.2 90.8 %reduce-scatter.53.cloned.1.call-start = ((), (), s32[]{:S(2)}) async-start(), calls=%async_computation.41 | async-start | bytes 589824 | tf_op jit(solution)/shard_map/reduce_scatter | solution.py:76
  867.2 31.8 %collective-permute-start.7 = (bf16[1,128,128]{2,1,0:T(8,128)(2,1)S(1)}, bf16[1,128,128]{2,1,0:T(8,128)(2,1)S(1)}, u32[]{:S(2)}, u32[]{:S(2)}) collective-permute-start(bf16[1,128,128]{2,1,0:T(8,128)(2,1)S(1)} %get-tuple-element.138), channel_id=1, source_target_pairs={{64,0},{128,64},{192,128},{65,1},{129,65},{193,129},{66,2},{130,66... | collective-permute-start | bytes 98312 | tf_op jit(solution)/shard_map/ppermute | solution.py:10
  868.5 7.5 collective-permute-start.10
  875.9 119.7 %reduce-scatter.65.cloned.1.call-start = ((), (), s32[]{:S(2)}) async-start(), calls=%async_computation.47 | async-start | bytes 589824 | tf_op jit(solution)/shard_map/reduce_scatter | solution.py:76
  929.8 103.9 %reduce-scatter.79.cloned.1.call-start = ((), (), s32[]{:S(2)}) async-start(), calls=%async_computation.54 | async-start | bytes 589824 | tf_op jit(solution)/shard_map/reduce_scatter | solution.py:76
  936.0 194.7 %reduce-scatter.67.cloned.1.call-start = ((), (), s32[]{:S(2)}) async-start(), calls=%async_computation.48 | async-start | bytes 589824 | tf_op jit(solution)/shard_map/reduce_scatter | solution.py:73
  1073.6 75.8 %reduce-scatter.81.cloned.1.call-start = ((), (), s32[]{:S(2)}) async-start(), calls=%async_computation.55 | async-start | bytes 589824 | tf_op jit(solution)/shard_map/reduce_scatter | solution.py:73
  1073.7 28.5 %collective-permute-start.2 = (bf16[1,128,128]{2,1,0:T(8,128)(2,1)S(1)}, bf16[1,128,128]{2,1,0:T(8,128)(2,1)S(1)}, u32[]{:S(2)}, u32[]{:S(2)}) collective-permute-start(bf16[1,128,128]{2,1,0:T(8,128)(2,1)S(1)} %get-tuple-element.133), channel_id=1, source_target_pairs={{0,64},{64,128},{128,192},{1,65},{65,129},{129,193},{2,66},{66,130... | collective-permute-start | bytes 98312 | tf_op jit(solution)/shard_map/ppermute | solution.py:10
  1077.0 9.3 collective-permute-start.5
  1086.2 104.5 %reduce-scatter.43.cloned.1.call-start = ((), (), s32[]{:S(2)}) async-start(), calls=%async_computation.36 | async-start | bytes 589824 | tf_op jit(solution)/shard_map/reduce_scatter | solution.py:73
  1086.3 32.4 %copy-start.3 = (bf16[1,1,4,4,256,128]{4,5,2,3,1,0:T(8,128)(2,1)S(1)}, bf16[1,1,4,4,256,128]{4,5,2,3,1,0:T(8,128)(2,1)}, u32[]{:S(2)}) copy-start(bf16[1,1,4,4,256,128]{4,5,2,3,1,0:T(8,128)(2,1)} %copy-done) | copy-start | bytes 3145732
  1124.5 107.6 %reduce-scatter.55.cloned.1.call-start = ((), (), s32[]{:S(2)}) async-start(), calls=%async_computation.42 | async-start | bytes 589824 | tf_op jit(solution)/shard_map/reduce_scatter | solution.py:73
  1130.7 214.8 %reduce-scatter.87.cloned.1.call-start = ((), (), s32[]{:S(2)}) async-start(), calls=%async_computation.58 | async-start | bytes 589824 | tf_op jit(solution)/shard_map/reduce_scatter | solution.py:76
  1284.3 90.7 %reduce-scatter.89.cloned.1.call-start = ((), (), s32[]{:S(2)}) async-start(), calls=%async_computation.59 | async-start | bytes 589824 | tf_op jit(solution)/shard_map/reduce_scatter | solution.py:76
  1284.3 29.6 %collective-permute-start.8 = (bf16[1,128,128]{2,1,0:T(8,128)(2,1)}, bf16[1,128,128]{2,1,0:T(8,128)(2,1)}, u32[]{:S(2)}, u32[]{:S(2)}) collective-permute-start(bf16[1,128,128]{2,1,0:T(8,128)(2,1)} %get-tuple-element.120), channel_id=1, source_target_pairs={{64,0},{128,64},{192,128},{65,1},{129,65},{193,129},{66,2},{130,66... | collective-permute-start | bytes 98312 | tf_op jit(solution)/shard_map/ppermute | solution.py:10
  1285.6 5.8 collective-permute-start.11
  1290.0 122.5 %reduce-scatter.69.cloned.1.call-start = ((), (), s32[]{:S(2)}) async-start(), calls=%async_computation.49 | async-start | bytes 589824 | tf_op jit(solution)/shard_map/reduce_scatter | solution.py:76
  1343.5 107.3 %reduce-scatter.83.cloned.1.call-start = ((), (), s32[]{:S(2)}) async-start(), calls=%async_computation.56 | async-start | bytes 589824 | tf_op jit(solution)/shard_map/reduce_scatter | solution.py:76
  1343.8 106.9 %copy-start.5 = (f32[2,1,2,128,128]{4,3,2,1,0:T(8,128)S(1)}, f32[2,1,2,128,128]{4,3,2,1,0:T(8,128)}, u32[]{:S(2)}) copy-start(f32[2,1,2,128,128]{4,3,2,1,0:T(8,128)} %param.15) | copy-start | bytes 786436
  1345.4 176.4 %reduce-scatter.71.cloned.1.call-start = ((), (), s32[]{:S(2)}) async-start(), calls=%async_computation.50 | async-start | bytes 589824 | tf_op jit(solution)/shard_map/reduce_scatter | solution.py:73
  1488.3 74.9 %reduce-scatter.85.cloned.1.call-start = ((), (), s32[]{:S(2)}) async-start(), calls=%async_computation.57 | async-start | bytes 589824 | tf_op jit(solution)/shard_map/reduce_scatter | solution.py:73
  (33 other events, 85.2 us)
Sparse Core Ops, SparseCore 0:
  15.7 39.5 reduce-scatter.30
  58.0 39.2 reduce-scatter.56
  110.4 49.0 reduce-scatter.32
  162.0 35.7 reduce-scatter.44
  237.8 33.6 reduce-scatter.58
  274.1 39.2 reduce-scatter.72
  315.9 38.7 reduce-scatter.34
  357.4 38.7 reduce-scatter.46
  449.4 51.5 reduce-scatter.36
  503.5 36.4 reduce-scatter.48
  542.6 34.8 reduce-scatter.60
  579.9 35.6 reduce-scatter.74
  655.3 33.9 reduce-scatter.62
  691.8 39.2 reduce-scatter.76
  733.5 38.8 reduce-scatter.38
  775.0 38.8 reduce-scatter.50
  867.3 51.4 reduce-scatter.40
  921.3 36.6 reduce-scatter.52
  960.5 35.0 reduce-scatter.64
  998.2 35.5 reduce-scatter.78
  1073.7 33.3 reduce-scatter.66
  1109.8 39.5 reduce-scatter.80
  1151.9 38.7 reduce-scatter.42
  1193.3 38.8 reduce-scatter.54
  1284.4 51.6 reduce-scatter.86
  1338.6 36.3 reduce-scatter.88
  1377.4 35.0 reduce-scatter.68
  1415.1 35.5 reduce-scatter.82
  1488.5 33.2 reduce-scatter.70
  1524.3 38.8 reduce-scatter.84
where the time goes:
time: 1590 us; the launch traced here: 1570 us
  waiting for transfers between devices  789 us (50%)
  blocking collectives  544 us (34%)
  local copies, waits for them, and re-layouts  70.2 us (4%)
  matrix products  66.5 us (4%)
  other arithmetic  57.2 us (4%)
  starting transfers between devices  29.1 us (2%)
  between operations  16.1 us (1%)
    reduce_scatter x15, waiting for transfers between devices, even_reduce(): return lax.psum_scatter(terms, 'col', scatter_dimension=1, tiled=True)  405 us
    reduce_scatter x15, waiting for transfers between devices, odd_reduce(): return lax.psum_scatter(terms, 'row', scatter_dimension=1, tiled=True)  382 us
    all_gather x14, blocking collectives, odd_terms(): lax.all_gather(current.astype(jnp.bfloat16), 'col', axis=1, tiled=True)  325 us
    all_gather x14, blocking collectives, even_terms(): lax.all_gather(current.astype(jnp.bfloat16), 'row', axis=1, tiled=True)  220 us
    transpose x30, local copies, waits for them, and re-layouts, tile_product(): jnp.einsum('acmr,kacrb->kamb', left_factor, stacked, preferred_element_ty...  56.5 us
    dot_general x30, matrix products, tile_product(): jnp.einsum('acmr,kacrb->kamb', left_factor, stacked, preferred_element_ty...  49.7 us
  transfers between devices with their start and end apart: 42, of which 24 were waited for; matrix products, arithmetic and copies ran while one was open for 8% of the time, Pallas kernels for 0%

commit v1 on v0

v1 whole, which is shorter than its diff:
```python
import functools

import jax
import jax.numpy as jnp
from jax import lax
from jax.experimental import pallas as pl
from jax.experimental.pallas import tpu as pltpu
from jax.sharding import PartitionSpec as P

AXES = ("layer", "row", "col")
BF = jnp.bfloat16
F32 = jnp.float32


USES = (
    ((1, 0), (1, 1), (0, 1), (0, 0)),
    ((0, 0), (1, 0), (1, 1), (0, 1)),
    ((1, 1), (0, 1), (0, 0), (1, 0)),
    ((0, 1), (0, 0), (1, 0), (1, 1)),
)
USE_OF_SLOT = (0, 0, 1, 2, 3, 1, 2)


def sections(slot):
    down, up = (slot + 1) // 2, (6 - slot) // 2
    if slot % 2:
        return down, 0, up, 1
    return up, 1, down, 0


def device(l, zh, core, y, zl):
    return (l * 8 + zh * 2 + core) * 8 + y * 2 + zl


def pairs_of(move, keep):
    found = []
    for l in range(4):
        if l not in keep:
            continue
        for zh in range(4):
            for core in range(2):
                for y in range(4):
                    for zl in range(2):
                        here = device(l, zh, core, y, zl)
                        found.append((here, device(*move(l, zh, core, y, zl))))
    return found


def send(value, move, keep=(0, 1, 2, 3)):
    return lax.ppermute(value, AXES, pairs_of(move, keep))


def order_kernel(pick, ranks, e_left, e_right, o_left, o_right, out, mask, sems):
    lane = lax.broadcasted_iota(jnp.int32, (256, 128), 1) % 64
    line = lax.broadcasted_iota(jnp.int32, (256, 128), 0)
    bound = jnp.zeros((256, 128), jnp.int32)
    for tile in range(16):
        bound = jnp.where(line == tile, ranks[tile], bound)
    direction = pick[1]

    def copies(right, left):
        return (
            pltpu.make_async_copy(right.at[direction], out.at[pl.ds(0, 16)], sems.at[0]),
            pltpu.make_async_copy(left.at[direction], out.at[pl.ds(16, 16)], sems.at[1]),
        )

    @pl.when(pick[0] == 0)
    def _():
        for copy in copies(e_right, e_left):
            copy.start()

    @pl.when(pick[0] != 0)
    def _():
        for copy in copies(o_right, o_left):
            copy.start()

    mask[...] = jnp.where(lane < bound, 1.0, 0.0).astype(BF)
    last = pltpu.make_async_copy(mask, out.at[32], sems.at[2])
    last.start()
    for copy in copies(e_right, e_left):
        copy.wait()
    last.wait()


def ordered(pick, ranks, e_left, e_right, o_left, o_right):
    smem = pl.BlockSpec(memory_space=pltpu.SMEM)
    hbm = pl.BlockSpec(memory_space=pl.ANY)
    return pl.pallas_call(
        order_kernel,
        out_shape=jax.ShapeDtypeStruct((33, 256, 128), BF),
        in_specs=[smem, smem, hbm, hbm, hbm, hbm],
        out_specs=hbm,
        scratch_shapes=[pltpu.VMEM((256, 128), BF), pltpu.SemaphoreType.DMA((3,))],
        compiler_params=pltpu.CompilerParams(vmem_limit_bytes=4 * 2**20),
        name="order_factors",
    )(pick, ranks, e_left, e_right, o_left, o_right)


PIECES = ((32, 1), (0, 8), (8, 8), (16, 8), (24, 8))


def layer_kernel(
    place, buf, other, source, w_own, w_other, keep, away, factors, xs, stacked, sums, sems
):
    even, core, zl, spot = place[0] == 1, place[1], place[2], place[3]

    def piece(w, index):
        start, size = PIECES[index]
        whole = (w_own, w_other)[w]
        return pltpu.make_async_copy(
            whole.at[pl.ds(start, size)], factors.at[w, pl.ds(start, size)], sems.at[w, index]
        )

    for w in range(2):
        for index in range(5):
            piece(w, index).start()

    for w in range(2):
        half = zl if w == 0 else 1 - zl
        for chunk in range(8):
            from_other = jnp.logical_and(even, core != chunk % 2)
            index = jnp.where(even, chunk // 2 * 2 + half, chunk)
            flag = jnp.full((128, 128), from_other.astype(jnp.int32)) != 0
            value = jnp.where(flag, other[index].astype(F32), buf[index].astype(F32)).astype(BF)
            xs[w, chunk // 2, :, chunk % 2 * 128 : chunk % 2 * 128 + 128] = value

    lane = lax.broadcasted_iota(jnp.int32, (1, 128), 1)
    sign = jnp.where(lane < 64, 1.0, -1.0)
    for w in range(2):
        piece(w, 0).wait()
        masks = factors[w, 32, 0:16, :].astype(F32)
        for a_pair in range(2):
            piece(w, 1 + a_pair).wait()
            for c in range(4):
                tiles = (a_pair * 8 + c, a_pair * 8 + 4 + c)
                right = jnp.concatenate([factors[w, tile] for tile in tiles], axis=1)
                product = jnp.dot(xs[w, c], right, preferred_element_type=F32)
                for side in range(2):
                    part = product[:, side * 128 : side * 128 + 128]
                    turned = pltpu.roll(part, 64, 1)
                    turned = jnp.concatenate([-turned[64:], turned[:64]], axis=0)
                    mask = masks[tiles[side] : tiles[side] + 1]
                    value = (part * sign + turned) * mask
                    stacked[w, a_pair * 2 + side, :, c * 128 : c * 128 + 128] = value.astype(BF)
        for a in range(4):
            if a % 2 == 0:
                piece(w, 3 + a // 2).wait()
            total = None
            for c_pair in range(2):
                left = jnp.concatenate(
                    [factors[w, 16 + a * 4 + c_pair * 2 + side] for side in range(2)], axis=1
                )
                term = lax.dot_general(
                    stacked[w, a, :, c_pair * 256 : c_pair * 256 + 256],
                    left,
                    (((1,), (1,)), ((), ())),
                    preferred_element_type=F32,
                )
                total = term if total is None else total + term
            sums[w, a * 2] = total[:, :128]
            sums[w, a * 2 + 1] = total[:, 128:]

    @pl.when(even)
    def _():
        for chunk in range(8):
            keep[chunk] = sums[0, chunk] + sums[1, chunk]
            away[chunk] = jnp.zeros((128, 128), BF)

    @pl.when(jnp.logical_not(even))
    def _():
        for chunk in range(8):
            w = jnp.where(zl == chunk % 2, 0, 1)
            keep[chunk] = sums[w, chunk // 2 * 2 + core]
            away[chunk] = sums[w, chunk // 2 * 2 + 1 - core].astype(BF)

    for side in range(2):
        keep[spot * 2 + side] = keep[spot * 2 + side] + source[side]


def layer(place, buf, other, source, w_own, w_other):
    vmem = pl.BlockSpec(memory_space=pltpu.VMEM)
    hbm = pl.BlockSpec(memory_space=pl.ANY)
    return pl.pallas_call(
        layer_kernel,
        out_shape=(
            jax.ShapeDtypeStruct((8, 128, 128), F32),
            jax.ShapeDtypeStruct((8, 128, 128), BF),
        ),
        in_specs=[pl.BlockSpec(memory_space=pltpu.SMEM), vmem, vmem, vmem, hbm, hbm],
        out_specs=(vmem, vmem),
        scratch_shapes=[
            pltpu.VMEM((2, 33, 256, 128), BF),
            pltpu.VMEM((2, 4, 128, 256), BF),
            pltpu.VMEM((2, 4, 128, 512), BF),
            pltpu.VMEM((2, 8, 128, 128), F32),
            pltpu.SemaphoreType.DMA((2, 5)),
        ],
        compiler_params=pltpu.CompilerParams(vmem_limit_bytes=20 * 2**20),
        cost_estimate=pl.CostEstimate(
            flops=32 * 2 * 128 * 256 * 256, bytes_accessed=6 * 2**20, transcendentals=0
        ),
        name="layer_product",
    )(place, buf, other, source, w_own, w_other)


def on_device(
    even_left, even_right, odd_left, odd_right, even_ranks, odd_ranks, even_sources, odd_sources
):
    section = lax.axis_index("layer")
    row, col = lax.axis_index("row"), lax.axis_index("col")
    zh, core, y, zl = row // 2, row % 2, col // 2, col % 2

    table = jnp.array(USES, jnp.int32)[section]
    flat = [f.reshape(2, 16, 256, 128) for f in (even_left, even_right, odd_left, odd_right)]
    ranks = jnp.stack([even_ranks.reshape(2, 16), odd_ranks.reshape(2, 16)])
    own = []
    for use in range(4):
        pick = table[use]
        own.append(ordered(pick, ranks[pick[0], pick[1]], *flat))
    swap_zl = lambda l, zh, core, y, zl: (l, zh, core, y, 1 - zl)
    swap_core = lambda l, zh, core, y, zl: (l, zh, 1 - core, y, zl)

    sources = jnp.concatenate([even_sources[:, 0], odd_sources[:, 0]])
    sources = jnp.swapaxes(sources, 2, 3)
    mine = lax.dynamic_index_in_dim(sources, zl, 1, keepdims=False)
    theirs = send(lax.dynamic_index_in_dim(sources, 1 - zl, 1, keepdims=False), swap_zl)
    first = zl == 0
    pair = jnp.stack([jnp.where(first, mine, theirs), jnp.where(first, theirs, mine)], axis=1)
    partner = [send(factors, swap_zl) for factors in own]

    def roles(slot):
        even_sec, even_dir, odd_sec, odd_dir = sections(slot)
        even = section == even_sec
        spot = jnp.where(even, y, zh)
        which = jnp.where(even, even_dir, 2 + odd_dir)
        return even, spot, lax.dynamic_index_in_dim(pair, which, 0, keepdims=False)

    def total(value, slot):
        even_sec, _, odd_sec, _ = sections(slot)
        both = (even_sec, odd_sec)

        def flip(bits):
            def move(l, zh, core, y, zl):
                if l == even_sec:
                    return (l, zh, core, y ^ bits, zl)
                return (l, zh ^ bits, core, y, zl)

            return move

        low, high = value[:4], value[4:]
        low_in = send(low.astype(BF), flip(1), both)
        high_in = send(high.astype(BF), flip(3), both)
        low, high = low + low_in.astype(F32), high + high_in.astype(F32)
        low_in = send(low.astype(BF), flip(3), both)
        high_in = send(high.astype(BF), flip(1), both)
        return jnp.concatenate([low + low_in.astype(F32), high + high_in.astype(F32)])

    def next_input(value, slot):
        buf = value.astype(BF)
        even_sec, even_dir, odd_sec, odd_dir = sections(slot)
        if slot in (0, 2, 4):
            step = {even_sec: 1 - 2 * even_dir, odd_sec: 1 - 2 * odd_dir}
            buf = send(
                buf, lambda l, zh, core, y, zl: (l + step[l], zh, core, y, zl), (even_sec, odd_sec)
            )
        other = send(buf, swap_core, (sections(slot + 1)[0],))
        return buf, other

    even, spot, source = roles(-1)
    start = lax.dynamic_update_slice_in_dim(
        jnp.zeros((8, 128, 128), F32), source, spot * 2, 0
    )
    even_sum = jnp.where(section == 0, pair[0], 0.0)
    odd_sum = jnp.where(section == 3, pair[3], 0.0)
    buf, other = next_input(total(start, -1), -1)
    for slot in range(7):
        even_sec, _, odd_sec, _ = sections(slot)
        even, spot, source = roles(slot)
        place = jnp.stack([even.astype(jnp.int32), core, zl, spot])
        use = USE_OF_SLOT[slot]
        keep, away = layer(place, buf, other, source, own[use], partner[use])
        keep = keep + send(away, swap_core, (odd_sec,)).astype(F32)
        result = total(keep, slot)
        part = lax.dynamic_slice_in_dim(result, spot * 2, 2, 0)
        even_sum = even_sum + jnp.where(section == even_sec, part, 0.0)
        odd_sum = odd_sum + jnp.where(section == odd_sec, part, 0.0)
        if slot < 6:
            buf, other = next_input(result, slot)

    both = jnp.stack([even_sum, odd_sum])
    mine = lax.dynamic_index_in_dim(both, zl, 1, keepdims=False)
    theirs = send(lax.dynamic_index_in_dim(both, 1 - zl, 1, keepdims=False), swap_zl)
    whole = jnp.stack([jnp.where(first, mine, theirs), jnp.where(first, theirs, mine)], axis=1)
    whole = jnp.swapaxes(whole, 2, 3)
    return whole[0][None], whole[1][None]


def solution(mesh):
    in_specs = (
        P(None, "layer", "row", "col", None, None),
        P(None, "layer", "row", "col", None, None),
        P(None, "layer", "col", "row", None, None),
        P(None, "layer", "col", "row", None, None),
        P(None, "layer", "row", "col"),
        P(None, "layer", "col", "row"),
        P(None, "layer", None, ("row", "col"), None),
        P(None, "layer", None, ("col", "row"), None),
    )
    out_specs = (P("layer", None, ("row", "col"), None), P("layer", None, ("col", "row"), None))
    return jax.shard_map(
        on_device, mesh=mesh, in_specs=in_specs, out_specs=out_specs, check_vma=False
    )
```

time: 1590 us -> 481 us (0.30)
  blocking collectives: 544 us -> 0 us
  waiting for transfers between devices: 789 us -> 304 us
  starting transfers between devices: 29.1 us -> 98.2 us
  matrix products: 66.5 us -> 0 us
  local copies, waits for them, and re-layouts: 70.2 us -> 18.5 us
  other arithmetic: 57.2 us -> 7.6 us
  Pallas kernels: 0 us -> 33.6 us
    reduce_scatter x30 -> x0, waiting for transfers between devices: 787 us -> none  [the longest x15 405 us: even_reduce(): return lax.psum_scatter(terms, 'col', scatter_dimension=1, tiled=True)]
    all_gather x28 -> x0, blocking collectives: 544 us -> none  [the longest x14 325 us: odd_terms(): lax.all_gather(current.astype(jnp.bfloat16), 'col', axis=1, tiled=True)]
    ppermute x12 -> x55, waiting for transfers between devices: 1.44 us -> 304 us  [send(): return lax.ppermute(value, AXES, pairs_of(move, keep))]
    ppermute x12 -> x55, starting transfers between devices: 27.9 us -> 98.2 us  [send(): return lax.ppermute(value, AXES, pairs_of(move, keep))]
    dot_general x60 -> x0, matrix products: 66.5 us -> none  [the longest x30 49.7 us: tile_product(): jnp.einsum('acmr,kacrb->kamb', left_factor, stacked, preferred_element_ty...]
    transpose x30 -> x0, local copies, waits for them, and re-layouts: 56.5 us -> none  [tile_product(): jnp.einsum('acmr,kacrb->kamb', left_factor, stacked, preferred_element_ty...]
    pallas_call x0 -> x11, Pallas kernels: none -> 33.6 us  [the longest x7 29.1 us: layer(): pl.pallas_call(layer_kernel, out_shape=(jax.ShapeDtypeStruct((8, 128, 128...]
    concatenate x31 -> x1, other arithmetic: 24.1 us -> 0.03 us  [total(): jnp.concatenate([low + low_in.astype(F32), high + high_in.astype(F32)])]
  transfers between devices with their start and end apart: 42 -> 55, of which waited for: 24 -> 25; matrix products, arithmetic and copies ran while one was open for 8% -> 1% of each run, Pallas kernels for 0% -> 2%
where the time goes in v1:
time: 481 us; the launch traced here: 479 us
  waiting for transfers between devices  304 us (63%)
  starting transfers between devices  98.2 us (20%)
  Pallas kernels  33.6 us (7%)
  local copies, waits for them, and re-layouts  18.5 us (4%)
  between operations  17.2 us (4%)
  other arithmetic  7.6 us (2%)
    ppermute x55, waiting for transfers between devices, send(): return lax.ppermute(value, AXES, pairs_of(move, keep))  304 us
    ppermute x55, starting transfers between devices, send(): return lax.ppermute(value, AXES, pairs_of(move, keep))  98.2 us
    pallas_call x7, Pallas kernels, layer(): pl.pallas_call(layer_kernel, out_shape=(jax.ShapeDtypeStruct((8, 128, 128...  29.1 us
    unnamed x101, local copies, waits for them, and re-layouts  15.3 us
  transfers between devices with their start and end apart: 55, of which 25 were waited for; matrix products, arithmetic and copies ran while one was open for 1% of the time, Pallas kernels for 2%

profile of v1, /device:TPU:1, one launch (start us, length us, event | category | flops | bytes accessed | tf_op | source)
XLA Modules:
  0.0 478.7 jit_solution(7524639551654666392)
XLA Ops:
  25.6 2.6 collective-permute-start.6
  28.7 50.8 %collective-permute-done = f32[4,128,128]{2,1,0:T(8,128)} collective-permute-done((f32[4,128,128]{2,1,0:T(8,128)S(1)}, f32[4,128,128]{2,1,0:T(8,128)}, u32[]{:S(2)}, u32[]{:S(2)}) %collective-permute-start) | collective-permute-done | bytes 262176 | tf_op jit(solution)/shard_map/ppermute | solution.py:50
  80.6 4.3 collective-permute-start.1
  84.9 3.8 collective-permute-start.3
  88.7 3.1 collective-permute-done.3
  91.9 3.8 collective-permute-start.2
  95.7 1.9 collective-permute-start.4
  98.8 2.9 collective-permute-done.4
  104.0 3.8 layer_product.7
  107.8 5.8 %collective-permute-start.7 = (bf16[8,128,128]{2,1,0:T(8,128)(2,1)S(1)}, bf16[8,128,128]{2,1,0:T(8,128)(2,1)S(1)}, u32[]{:S(2)}, u32[]{:S(2)}) collective-permute-start(bf16[8,128,128]{2,1,0:T(8,128)(2,1)S(1)} %get-tuple-element.17), channel_id=1, source_target_pairs={{0,8},{1,9},{2,10},{3,11},{4,12},{5,13},{6,14},{7,15},{8,0},{9,1},... | collective-permute-start | bytes 786440 | tf_op jit(solution)/shard_map/ppermute | solution.py:50
  114.9 8.0 %collective-permute-start.10 = (bf16[4,128,128]{2,1,0:T(8,128)(2,1)S(1)}, bf16[4,128,128]{2,1,0:T(8,128)(2,1)S(1)}, u32[]{:S(2)}, u32[]{:S(2)}) collective-permute-start(bf16[4,128,128]{2,1,0:T(8,128)(2,1)S(1)} %get-tuple-element.81), channel_id=1, source_target_pairs={{0,48},{1,49},{2,50},{3,51},{4,52},{5,53},{6,54},{7,55},{8,56},{9,... | collective-permute-start | bytes 393224 | tf_op jit(solution)/shard_map/ppermute | solution.py:50
  123.0 3.1 collective-permute-start.8
  126.0 2.5 collective-permute-done.10
  128.5 2.6 collective-permute-done.8
  131.2 5.0 %collective-permute-start.11 = (bf16[4,128,128]{2,1,0:T(8,128)(2,1)S(1)}, bf16[4,128,128]{2,1,0:T(8,128)(2,1)S(1)}, u32[]{:S(2)}, u32[]{:S(2)}) collective-permute-start(bf16[4,128,128]{2,1,0:T(8,128)(2,1)S(1)} %get-tuple-element.79), channel_id=1, source_target_pairs={{0,16},{1,17},{2,18},{3,19},{4,20},{5,21},{6,22},{7,23},{8,24},{9,... | collective-permute-start | bytes 393224 | tf_op jit(solution)/shard_map/ppermute | solution.py:50
  136.2 2.2 collective-permute-start.9
  138.5 7.6 %collective-permute-done.9 = bf16[4,128,128]{2,1,0:T(8,128)(2,1)S(1)} collective-permute-done((bf16[4,128,128]{2,1,0:T(8,128)(2,1)S(1)}, bf16[4,128,128]{2,1,0:T(8,128)(2,1)S(1)}, u32[]{:S(2)}, u32[]{:S(2)}) %collective-permute-start.9) | collective-permute-done | bytes 131104 | tf_op jit(solution)/shard_map/ppermute | solution.py:50
  147.6 4.9 %collective-permute-done.12.buf = bf16[8,128,128]{2,1,0:T(8,128)(2,1)S(1)} collective-permute-done((bf16[8,128,128]{2,1,0:T(8,128)(2,1)S(1)}, bf16[8,128,128]{2,1,0:T(8,128)(2,1)S(1)}, u32[]{:S(2)}, u32[]{:S(2)}) %collective-permute-start.12) | collective-permute-done | bytes 262176 | tf_op jit(solution)/shard_map/ppermute | solution.py:50
  153.2 1.9 order_factors.5.w_own
  155.3 1.6 copy-done.15
  157.0 3.8 layer_product.8
  166.1 36.5 %collective-permute-done.20.w_other = bf16[33,256,128]{2,1,0:T(8,128)(2,1)} collective-permute-done((bf16[33,256,128]{2,1,0:T(8,128)(2,1)}, bf16[33,256,128]{2,1,0:T(8,128)(2,1)}, u32[]{:S(2)}, u32[]{:S(2)}) %collective-permute-start.20) | collective-permute-done | bytes 2162720 | tf_op jit(solution)/shard_map/ppermute | solution.py:50
  202.5 4.8 %layer_product.9 = (f32[8,128,128]{2,1,0:T(8,128)S(1)}, bf16[8,128,128]{2,1,0:T(8,128)(2,1)S(1)}) custom-call(s32[4]{0:T(128)S(1)} %pad_add_fusion.2.place, bf16[8,128,128]{2,1,0:T(8,128)(2,1)S(1)} %fusion.4.buf, bf16[8,128,128]{2,1,0:T(8,128)(2,1)S(1)} %collective-permute-done.19.other, f32[2,128,128]{2,1,0:T(8,128)S(1)} %get-tuple-element.43.source, ...), custom_call_target="tpu_custom_call" | custom-call | flops 536870912 | bytes 6291456 | tf_op jit(solution)/shard_map/layer_product/pallas_call | solution.py:183
  217.8 39.1 %collective-permute-done.28.w_other = bf16[33,256,128]{2,1,0:T(8,128)(2,1)S(1)} collective-permute-done((bf16[33,256,128]{2,1,0:T(8,128)(2,1)S(1)}, bf16[33,256,128]{2,1,0:T(8,128)(2,1)S(1)}, u32[]{:S(2)}, u32[]{:S(2)}) %collective-permute-start.28) | collective-permute-done | bytes 2162720 | tf_op jit(solution)/shard_map/ppermute | solution.py:50
  256.8 4.1 layer_product.10
  266.1 37.1 %collective-permute-done.35.w_other = bf16[33,256,128]{2,1,0:T(8,128)(2,1)S(1)} collective-permute-done((bf16[33,256,128]{2,1,0:T(8,128)(2,1)S(1)}, bf16[33,256,128]{2,1,0:T(8,128)(2,1)S(1)}, u32[]{:S(2)}, u32[]{:S(2)}) %collective-permute-start.35) | collective-permute-done | bytes 2162720 | tf_op jit(solution)/shard_map/ppermute | solution.py:50
  303.2 4.1 layer_product.11
  312.5 84.3 %collective-permute-done.41.buf = bf16[8,128,128]{2,1,0:T(8,128)(2,1)S(1)} collective-permute-done((bf16[8,128,128]{2,1,0:T(8,128)(2,1)S(1)}, bf16[8,128,128]{2,1,0:T(8,128)(2,1)S(1)}, u32[]{:S(2)}, u32[]{:S(2)}) %collective-permute-start.41) | collective-permute-done | bytes 262176 | tf_op jit(solution)/shard_map/ppermute | solution.py:50
  397.4 4.5 layer_product.12
  402.0 4.9 %collective-permute-start.43 = (bf16[8,128,128]{2,1,0:T(8,128)(2,1)S(1)}, bf16[8,128,128]{2,1,0:T(8,128)(2,1)S(1)}, u32[]{:S(2)}, u32[]{:S(2)}) collective-permute-start(bf16[8,128,128]{2,1,0:T(8,128)(2,1)S(1)} %get-tuple-element.27), channel_id=1, source_target_pairs={{0,8},{1,9},{2,10},{3,11},{4,12},{5,13},{6,14},{7,15},{8,0},{9,1},... | collective-permute-start | bytes 786440 | tf_op jit(solution)/shard_map/ppermute | solution.py:50
  408.1 4.7 collective-permute-start.44
  412.8 4.9 %collective-permute-start.46 = (bf16[4,128,128]{2,1,0:T(8,128)(2,1)S(1)}, bf16[4,128,128]{2,1,0:T(8,128)(2,1)S(1)}, u32[]{:S(2)}, u32[]{:S(2)}) collective-permute-start(bf16[4,128,128]{2,1,0:T(8,128)(2,1)S(1)} %get-tuple-element.51), channel_id=1, source_target_pairs={{0,48},{1,49},{2,50},{3,51},{4,52},{5,53},{6,54},{7,55},{8,56},{9,... | collective-permute-start | bytes 393224 | tf_op jit(solution)/shard_map/ppermute | solution.py:50
  419.2 5.7 %collective-permute-done.46 = bf16[4,128,128]{2,1,0:T(8,128)(2,1)S(1)} collective-permute-done((bf16[4,128,128]{2,1,0:T(8,128)(2,1)S(1)}, bf16[4,128,128]{2,1,0:T(8,128)(2,1)S(1)}, u32[]{:S(2)}, u32[]{:S(2)}) %collective-permute-start.46) | collective-permute-done | bytes 131104 | tf_op jit(solution)/shard_map/ppermute | solution.py:50
  424.9 4.3 collective-permute-start.45
  429.3 1.9 collective-permute-start.47
  431.2 2.2 collective-permute-done.45
  433.4 6.2 %collective-permute-done.47 = bf16[4,128,128]{2,1,0:T(8,128)(2,1)S(1)} collective-permute-done((bf16[4,128,128]{2,1,0:T(8,128)(2,1)S(1)}, bf16[4,128,128]{2,1,0:T(8,128)(2,1)S(1)}, u32[]{:S(2)}, u32[]{:S(2)}) %collective-permute-start.47) | collective-permute-done | bytes 131104 | tf_op jit(solution)/shard_map/ppermute | solution.py:50
  440.4 2.6 collective-permute-start.48
  444.0 1.6 copy-done.17
  445.6 4.1 layer_product.13
  450.6 2.1 collective-permute-start.50
  452.6 3.5 collective-permute-start.52
  457.3 3.1 collective-permute-done.52
  461.2 3.2 collective-permute-start.51
  464.4 1.9 collective-permute-start.53
  466.4 2.1 collective-permute-done.51
  468.4 2.0 collective-permute-done.53
  473.3 3.8 collective-permute-done.54
  (235 shorter events, 56.3 us)
Async XLA Ops:
  25.6 78.3 %collective-permute-start.6 = (bf16[33,256,128]{2,1,0:T(8,128)(2,1)S(1)}, bf16[33,256,128]{2,1,0:T(8,128)(2,1)}, u32[]{:S(2)}, u32[]{:S(2)}) collective-permute-start(bf16[33,256,128]{2,1,0:T(8,128)(2,1)S(1)} %order_factors.4.w_own), channel_id=1, source_target_pairs={{0,1},{1,0},{2,3},{3,2},{4,5},{5,4},{6,7},{7,6},{8,9},{9,8},{10,11... | collective-permute-start | bytes 6488072 | tf_op jit(solution)/shard_map/ppermute | solution.py:50
  28.5 51.0 %collective-permute-start = (f32[4,128,128]{2,1,0:T(8,128)S(1)}, f32[4,128,128]{2,1,0:T(8,128)}, u32[]{:S(2)}, u32[]{:S(2)}) collective-permute-start(f32[4,128,128]{2,1,0:T(8,128)S(1)} %fusion.7), channel_id=1, source_target_pairs={{0,1},{1,0},{2,3},{3,2},{4,5},{5,4},{6,7},{7,6},{8,9},{9,8},{10,11... | collective-permute-start | bytes 786440 | tf_op jit(solution)/shard_map/ppermute | solution.py:50
  80.6 8.1 %collective-permute-start.1 = (bf16[4,128,128]{2,1,0:T(8,128)(2,1)S(1)}, bf16[4,128,128]{2,1,0:T(8,128)(2,1)S(1)}, u32[]{:S(2)}, u32[]{:S(2)}) collective-permute-start(bf16[4,128,128]{2,1,0:T(8,128)(2,1)S(1)} %get-tuple-element.86), channel_id=1, source_target_pairs={{0,2},{1,3},{2,0},{3,1},{4,6},{5,7},{6,4},{7,5},{8,10},{9,11},{10,... | collective-permute-start | bytes 393224 | tf_op jit(solution)/shard_map/ppermute | solution.py:50
  84.9 6.9 %collective-permute-start.3 = (bf16[4,128,128]{2,1,0:T(8,128)(2,1)S(1)}, bf16[4,128,128]{2,1,0:T(8,128)(2,1)S(1)}, u32[]{:S(2)}, u32[]{:S(2)}) collective-permute-start(bf16[4,128,128]{2,1,0:T(8,128)(2,1)S(1)} %get-tuple-element.87), channel_id=1, source_target_pairs={{0,6},{1,7},{2,4},{3,5},{4,2},{5,3},{6,0},{7,1},{8,14},{9,15},{10,... | collective-permute-start | bytes 393224 | tf_op jit(solution)/shard_map/ppermute | solution.py:50
  91.9 6.9 %collective-permute-start.2 = (bf16[4,128,128]{2,1,0:T(8,128)(2,1)S(1)}, bf16[4,128,128]{2,1,0:T(8,128)(2,1)S(1)}, u32[]{:S(2)}, u32[]{:S(2)}) collective-permute-start(bf16[4,128,128]{2,1,0:T(8,128)(2,1)S(1)} %get-tuple-element.84), channel_id=1, source_target_pairs={{0,6},{1,7},{2,4},{3,5},{4,2},{5,3},{6,0},{7,1},{8,14},{9,15},{10,... | collective-permute-start | bytes 393224 | tf_op jit(solution)/shard_map/ppermute | solution.py:50
  95.7 6.0 %collective-permute-start.4 = (bf16[4,128,128]{2,1,0:T(8,128)(2,1)S(1)}, bf16[4,128,128]{2,1,0:T(8,128)(2,1)S(1)}, u32[]{:S(2)}, u32[]{:S(2)}) collective-permute-start(bf16[4,128,128]{2,1,0:T(8,128)(2,1)S(1)} %get-tuple-element.85), channel_id=1, source_target_pairs={{0,2},{1,3},{2,0},{3,1},{4,6},{5,7},{6,4},{7,5},{8,10},{9,11},{10,... | collective-permute-start | bytes 393224 | tf_op jit(solution)/shard_map/ppermute | solution.py:50
  101.9 2.1 collective-permute-start.5
  107.8 7.0 %collective-permute-start.7 = (bf16[8,128,128]{2,1,0:T(8,128)(2,1)S(1)}, bf16[8,128,128]{2,1,0:T(8,128)(2,1)S(1)}, u32[]{:S(2)}, u32[]{:S(2)}) collective-permute-start(bf16[8,128,128]{2,1,0:T(8,128)(2,1)S(1)} %get-tuple-element.17), channel_id=1, source_target_pairs={{0,8},{1,9},{2,10},{3,11},{4,12},{5,13},{6,14},{7,15},{8,0},{9,1},... | collective-permute-start | bytes 786440 | tf_op jit(solution)/shard_map/ppermute | solution.py:50
  114.9 13.6 %collective-permute-start.10 = (bf16[4,128,128]{2,1,0:T(8,128)(2,1)S(1)}, bf16[4,128,128]{2,1,0:T(8,128)(2,1)S(1)}, u32[]{:S(2)}, u32[]{:S(2)}) collective-permute-start(bf16[4,128,128]{2,1,0:T(8,128)(2,1)S(1)} %get-tuple-element.81), channel_id=1, source_target_pairs={{0,48},{1,49},{2,50},{3,51},{4,52},{5,53},{6,54},{7,55},{8,56},{9,... | collective-permute-start | bytes 393224 | tf_op jit(solution)/shard_map/ppermute | solution.py:50
  123.0 8.1 %collective-permute-start.8 = (bf16[4,128,128]{2,1,0:T(8,128)(2,1)S(1)}, bf16[4,128,128]{2,1,0:T(8,128)(2,1)S(1)}, u32[]{:S(2)}, u32[]{:S(2)}) collective-permute-start(bf16[4,128,128]{2,1,0:T(8,128)(2,1)S(1)} %get-tuple-element.80), channel_id=1, source_target_pairs={{0,16},{1,17},{2,18},{3,19},{4,20},{5,21},{6,22},{7,23},{8,24},{9,... | collective-permute-start | bytes 393224 | tf_op jit(solution)/shard_map/ppermute | solution.py:50
  131.2 7.4 %collective-permute-start.11 = (bf16[4,128,128]{2,1,0:T(8,128)(2,1)S(1)}, bf16[4,128,128]{2,1,0:T(8,128)(2,1)S(1)}, u32[]{:S(2)}, u32[]{:S(2)}) collective-permute-start(bf16[4,128,128]{2,1,0:T(8,128)(2,1)S(1)} %get-tuple-element.79), channel_id=1, source_target_pairs={{0,16},{1,17},{2,18},{3,19},{4,20},{5,21},{6,22},{7,23},{8,24},{9,... | collective-permute-start | bytes 393224 | tf_op jit(solution)/shard_map/ppermute | solution.py:50
  136.2 9.9 %collective-permute-start.9 = (bf16[4,128,128]{2,1,0:T(8,128)(2,1)S(1)}, bf16[4,128,128]{2,1,0:T(8,128)(2,1)S(1)}, u32[]{:S(2)}, u32[]{:S(2)}) collective-permute-start(bf16[4,128,128]{2,1,0:T(8,128)(2,1)S(1)} %get-tuple-element.78), channel_id=1, source_target_pairs={{0,48},{1,49},{2,50},{3,51},{4,52},{5,53},{6,54},{7,55},{8,56},{9,... | collective-permute-start | bytes 393224 | tf_op jit(solution)/shard_map/ppermute | solution.py:50
  146.2 6.3 %collective-permute-start.12 = (bf16[8,128,128]{2,1,0:T(8,128)(2,1)S(1)}, bf16[8,128,128]{2,1,0:T(8,128)(2,1)S(1)}, u32[]{:S(2)}, u32[]{:S(2)}) collective-permute-start(bf16[8,128,128]{2,1,0:T(8,128)(2,1)S(1)} %fusion.5), channel_id=1, source_target_pairs={{0,64},{1,65},{2,66},{3,67},{4,68},{5,69},{6,70},{7,71},{8,72},{9,... | collective-permute-start | bytes 786440 | tf_op jit(solution)/shard_map/ppermute | solution.py:50
  152.5 2.8 collective-permute-start.13
  155.2 47.4 %collective-permute-start.20 = (bf16[33,256,128]{2,1,0:T(8,128)(2,1)}, bf16[33,256,128]{2,1,0:T(8,128)(2,1)}, u32[]{:S(2)}, u32[]{:S(2)}) collective-permute-start(bf16[33,256,128]{2,1,0:T(8,128)(2,1)} %order_factors.5.w_own), channel_id=1, source_target_pairs={{0,1},{1,0},{2,3},{3,2},{4,5},{5,4},{6,7},{7,6},{8,9},{9,8},{10,11... | collective-permute-start | bytes 6488072 | tf_op jit(solution)/shard_map/ppermute | solution.py:50
  161.6 1.4 collective-permute-start.15
  162.3 0.7 collective-permute-start.17
  163.0 1.4 collective-permute-start.16
  163.7 0.7 collective-permute-start.18
  165.3 37.2 %collective-permute-start.19 = (bf16[8,128,128]{2,1,0:T(8,128)(2,1)S(1)}, bf16[8,128,128]{2,1,0:T(8,128)(2,1)S(1)}, u32[]{:S(2)}, u32[]{:S(2)}) collective-permute-start(bf16[8,128,128]{2,1,0:T(8,128)(2,1)S(1)} %fusion.4.buf), channel_id=1, source_target_pairs={{128,136},{129,137},{130,138},{131,139},{132,140},{133,141},{134,1... | collective-permute-start | bytes 786440 | tf_op jit(solution)/shard_map/ppermute | solution.py:50
  207.3 3.4 collective-permute-start.21
  210.5 46.3 %collective-permute-start.28 = (bf16[33,256,128]{2,1,0:T(8,128)(2,1)S(1)}, bf16[33,256,128]{2,1,0:T(8,128)(2,1)S(1)}, u32[]{:S(2)}, u32[]{:S(2)}) collective-permute-start(bf16[33,256,128]{2,1,0:T(8,128)(2,1)S(1)} %order_factors.6.w_own), channel_id=1, source_target_pairs={{0,1},{1,0},{2,3},{3,2},{4,5},{5,4},{6,7},{7,6},{8,9},{9,8},{10,11... | collective-permute-start | bytes 6488072 | tf_op jit(solution)/shard_map/ppermute | solution.py:50
  210.9 1.6 collective-permute-start.22
  211.7 0.8 collective-permute-start.24
  212.6 1.4 collective-permute-start.23
  213.3 0.7 collective-permute-start.25
  214.8 42.0 %collective-permute-start.27 = (bf16[8,128,128]{2,1,0:T(8,128)(2,1)S(1)}, bf16[8,128,128]{2,1,0:T(8,128)(2,1)S(1)}, u32[]{:S(2)}, u32[]{:S(2)}) collective-permute-start(bf16[8,128,128]{2,1,0:T(8,128)(2,1)S(1)} %collective-permute-done.26.buf), channel_id=1, source_target_pairs={{128,136},{129,137},{130,138},{131,139},{132,140},{133,141},{134,1... | collective-permute-start | bytes 786440 | tf_op jit(solution)/shard_map/ppermute | solution.py:50
  216.4 86.8 %collective-permute-start.35 = (bf16[33,256,128]{2,1,0:T(8,128)(2,1)S(1)}, bf16[33,256,128]{2,1,0:T(8,128)(2,1)S(1)}, u32[]{:S(2)}, u32[]{:S(2)}) collective-permute-start(bf16[33,256,128]{2,1,0:T(8,128)(2,1)S(1)} %order_factors.7.w_own), channel_id=1, source_target_pairs={{0,1},{1,0},{2,3},{3,2},{4,5},{5,4},{6,7},{7,6},{8,9},{9,8},{10,11... | collective-permute-start | bytes 6488072 | tf_op jit(solution)/shard_map/ppermute | solution.py:50
  261.7 1.4 collective-permute-start.30
  262.4 0.7 collective-permute-start.32
  263.2 1.4 collective-permute-start.31
  263.8 0.7 collective-permute-start.33
  265.4 37.8 %collective-permute-start.34 = (bf16[8,128,128]{2,1,0:T(8,128)(2,1)S(1)}, bf16[8,128,128]{2,1,0:T(8,128)(2,1)S(1)}, u32[]{:S(2)}, u32[]{:S(2)}) collective-permute-start(bf16[8,128,128]{2,1,0:T(8,128)(2,1)S(1)} %fusion.2.buf), channel_id=1, source_target_pairs={{64,72},{65,73},{66,74},{67,75},{68,76},{69,77},{70,78},{71,79},{7... | collective-permute-start | bytes 786440 | tf_op jit(solution)/shard_map/ppermute | solution.py:50
  308.1 1.5 collective-permute-start.37
  309.6 1.4 collective-permute-start.38
  311.2 85.6 %collective-permute-start.41 = (bf16[8,128,128]{2,1,0:T(8,128)(2,1)S(1)}, bf16[8,128,128]{2,1,0:T(8,128)(2,1)S(1)}, u32[]{:S(2)}, u32[]{:S(2)}) collective-permute-start(bf16[8,128,128]{2,1,0:T(8,128)(2,1)S(1)} %fusion.1), channel_id=1, source_target_pairs={{64,0},{65,1},{66,2},{67,3},{68,4},{69,5},{70,6},{71,7},{72,8},{73... | collective-permute-start | bytes 786440 | tf_op jit(solution)/shard_map/ppermute | solution.py:50
  396.7 0.7 collective-permute-start.42
  402.0 6.0 %collective-permute-start.43 = (bf16[8,128,128]{2,1,0:T(8,128)(2,1)S(1)}, bf16[8,128,128]{2,1,0:T(8,128)(2,1)S(1)}, u32[]{:S(2)}, u32[]{:S(2)}) collective-permute-start(bf16[8,128,128]{2,1,0:T(8,128)(2,1)S(1)} %get-tuple-element.27), channel_id=1, source_target_pairs={{0,8},{1,9},{2,10},{3,11},{4,12},{5,13},{6,14},{7,15},{8,0},{9,1},... | collective-permute-start | bytes 786440 | tf_op jit(solution)/shard_map/ppermute | solution.py:50
  408.1 11.1 %collective-permute-start.44 = (bf16[4,128,128]{2,1,0:T(8,128)(2,1)S(1)}, bf16[4,128,128]{2,1,0:T(8,128)(2,1)S(1)}, u32[]{:S(2)}, u32[]{:S(2)}) collective-permute-start(bf16[4,128,128]{2,1,0:T(8,128)(2,1)S(1)} %get-tuple-element.50), channel_id=1, source_target_pairs={{0,16},{1,17},{2,18},{3,19},{4,20},{5,21},{6,22},{7,23},{8,24},{9,... | collective-permute-start | bytes 393224 | tf_op jit(solution)/shard_map/ppermute | solution.py:50
  412.8 12.0 %collective-permute-start.46 = (bf16[4,128,128]{2,1,0:T(8,128)(2,1)S(1)}, bf16[4,128,128]{2,1,0:T(8,128)(2,1)S(1)}, u32[]{:S(2)}, u32[]{:S(2)}) collective-permute-start(bf16[4,128,128]{2,1,0:T(8,128)(2,1)S(1)} %get-tuple-element.51), channel_id=1, source_target_pairs={{0,48},{1,49},{2,50},{3,51},{4,52},{5,53},{6,54},{7,55},{8,56},{9,... | collective-permute-start | bytes 393224 | tf_op jit(solution)/shard_map/ppermute | solution.py:50
  424.9 8.4 %collective-permute-start.45 = (bf16[4,128,128]{2,1,0:T(8,128)(2,1)S(1)}, bf16[4,128,128]{2,1,0:T(8,128)(2,1)S(1)}, u32[]{:S(2)}, u32[]{:S(2)}) collective-permute-start(bf16[4,128,128]{2,1,0:T(8,128)(2,1)S(1)} %get-tuple-element.48), channel_id=1, source_target_pairs={{0,48},{1,49},{2,50},{3,51},{4,52},{5,53},{6,54},{7,55},{8,56},{9,... | collective-permute-start | bytes 393224 | tf_op jit(solution)/shard_map/ppermute | solution.py:50
  429.3 10.3 %collective-permute-start.47 = (bf16[4,128,128]{2,1,0:T(8,128)(2,1)S(1)}, bf16[4,128,128]{2,1,0:T(8,128)(2,1)S(1)}, u32[]{:S(2)}, u32[]{:S(2)}) collective-permute-start(bf16[4,128,128]{2,1,0:T(8,128)(2,1)S(1)} %get-tuple-element.49), channel_id=1, source_target_pairs={{0,16},{1,17},{2,18},{3,19},{4,20},{5,21},{6,22},{7,23},{8,24},{9,... | collective-permute-start | bytes 393224 | tf_op jit(solution)/shard_map/ppermute | solution.py:50
  440.4 3.5 collective-permute-start.48
  450.6 6.7 %collective-permute-start.50 = (bf16[4,128,128]{2,1,0:T(8,128)(2,1)S(1)}, bf16[4,128,128]{2,1,0:T(8,128)(2,1)S(1)}, u32[]{:S(2)}, u32[]{:S(2)}) collective-permute-start(bf16[4,128,128]{2,1,0:T(8,128)(2,1)S(1)} %get-tuple-element.38), channel_id=1, source_target_pairs={{0,2},{1,3},{2,0},{3,1},{4,6},{5,7},{6,4},{7,5},{8,10},{9,11},{10,... | collective-permute-start | bytes 393224 | tf_op jit(solution)/shard_map/ppermute | solution.py:50
  452.6 7.8 %collective-permute-start.52 = (bf16[4,128,128]{2,1,0:T(8,128)(2,1)S(1)}, bf16[4,128,128]{2,1,0:T(8,128)(2,1)S(1)}, u32[]{:S(2)}, u32[]{:S(2)}) collective-permute-start(bf16[4,128,128]{2,1,0:T(8,128)(2,1)S(1)} %get-tuple-element.39), channel_id=1, source_target_pairs={{0,6},{1,7},{2,4},{3,5},{4,2},{5,3},{6,0},{7,1},{8,14},{9,15},{10,... | collective-permute-start | bytes 393224 | tf_op jit(solution)/shard_map/ppermute | solution.py:50
  461.2 7.2 %collective-permute-start.51 = (bf16[4,128,128]{2,1,0:T(8,128)(2,1)}, bf16[4,128,128]{2,1,0:T(8,128)(2,1)}, u32[]{:S(2)}, u32[]{:S(2)}) collective-permute-start(bf16[4,128,128]{2,1,0:T(8,128)(2,1)} %get-tuple-element.36), channel_id=1, source_target_pairs={{0,6},{1,7},{2,4},{3,5},{4,2},{5,3},{6,0},{7,1},{8,14},{9,15},{10,... | collective-permute-start | bytes 393224 | tf_op jit(solution)/shard_map/ppermute | solution.py:50
  464.4 6.0 %collective-permute-start.53 = (bf16[4,128,128]{2,1,0:T(8,128)(2,1)}, bf16[4,128,128]{2,1,0:T(8,128)(2,1)}, u32[]{:S(2)}, u32[]{:S(2)}) collective-permute-start(bf16[4,128,128]{2,1,0:T(8,128)(2,1)} %get-tuple-element.37), channel_id=1, source_target_pairs={{0,2},{1,3},{2,0},{3,1},{4,6},{5,7},{6,4},{7,5},{8,10},{9,11},{10,... | collective-permute-start | bytes 393224 | tf_op jit(solution)/shard_map/ppermute | solution.py:50
  473.2 3.9 collective-permute-start.54
  (55 other events, 1003.9 us)

commit v2 on v0

v2 whole, which is shorter than its diff:
```python
import functools

import jax
import jax.numpy as jnp
from jax import lax
from jax.experimental import pallas as pl
from jax.experimental.pallas import tpu as pltpu
from jax.sharding import PartitionSpec as P

AXES = ("layer", "row", "col")
BF = jnp.bfloat16
F32 = jnp.float32


def down_section(slot):
    return (slot + 1) // 2 if slot <= 6 else -1


def up_section(slot):
    return (7 - slot) // 2


def here():
    row, col = lax.axis_index("row"), lax.axis_index("col")
    return lax.axis_index("layer"), row // 2, row % 2, col // 2, col % 2


def send(value, move, sections):
    pairs = []
    for l in sections:
        for zh in range(4):
            for core in range(2):
                target = move(l, zh, core)
                if target is None:
                    continue
                to_l, to_zh, to_core = target
                for col in range(8):
                    pairs.append(
                        (
                            (l * 8 + zh * 2 + core) * 8 + col,
                            (to_l * 8 + to_zh % 4 * 2 + to_core) * 8 + col,
                        )
                    )
    return lax.ppermute(value, AXES, pairs)


PIECES = ((0, 8), (8, 8))


def product_kernel(odd, choose, ranks, *refs):
    if odd:
        trace, right, left, keep, away, rights, lefts, xs, stacked, sems = refs
    else:
        trace, other, right, left, out, rights, lefts, xs, stacked, sems = refs
    section, zh, core, _, _ = here()
    direction = choose if isinstance(choose, int) else (section == choose[0]).astype(jnp.int32)

    def piece(index):
        source, kept = ((right, rights), (left, lefts))[index // 2]
        start, size = PIECES[index % 2]
        return pltpu.make_async_copy(
            source.at[direction, pl.ds(start, size)], kept.at[pl.ds(start, size)], sems.at[index]
        )

    for index in range(4):
        piece(index).start()

    for chunk in range(8):
        lanes = slice(chunk % 2 * 128, chunk % 2 * 128 + 128)
        if odd:
            xs[chunk // 2, :, lanes] = trace[chunk]
        else:
            place = (zh - chunk // 2 + 4) % 4

            @pl.when(core == chunk % 2)
            def _(chunk=chunk, lanes=lanes, place=place):
                xs[chunk // 2, :, lanes] = trace[place]

            @pl.when(core != chunk % 2)
            def _(chunk=chunk, lanes=lanes, place=place):
                xs[chunk // 2, :, lanes] = other[place]

    lane = lax.broadcasted_iota(jnp.int32, (1, 128), 1)
    sign = jnp.where(lane < 64, 1.0, -1.0)
    for a_pair in range(2):
        piece(a_pair).wait()
        for c in range(4):
            tiles = (a_pair * 8 + c, a_pair * 8 + 4 + c)
            joined = jnp.concatenate([rights[tile] for tile in tiles], axis=1)
            product = jnp.dot(xs[c], joined, preferred_element_type=F32)
            for side in range(2):
                part = product[:, side * 128 : side * 128 + 128]
                turned = pltpu.roll(part, 64, 1)
                turned = jnp.concatenate(
                    [-turned[64:128], turned[:64], -turned[192:], turned[128:192]], axis=0
                )
                mask = jnp.where(lane % 64 < ranks[direction, tiles[side]], 1.0, 0.0)
                value = (part * sign + turned) * mask
                stacked[a_pair * 2 + side, :, c * 128 : c * 128 + 128] = value.astype(BF)
    for a in range(4):
        if a % 2 == 0:
            piece(2 + a // 2).wait()
        total = None
        for c_pair in range(2):
            joined = jnp.concatenate(
                [lefts[a * 4 + c_pair * 2 + side] for side in range(2)], axis=1
            )
            term = lax.dot_general(
                stacked[a, :, c_pair * 256 : c_pair * 256 + 256],
                joined,
                (((1,), (1,)), ((), ())),
                preferred_element_type=F32,
            )
            total = term if total is None else total + term
        first, second = total[:, :128], total[:, 128:]
        if odd:
            place = (a - zh + 4) % 4

            @pl.when(core == 0)
            def _(first=first, second=second, place=place):
                keep[place] = first
                away[place] = second.astype(BF)

            @pl.when(core != 0)
            def _(first=first, second=second, place=place):
                keep[place] = second
                away[place] = first.astype(BF)

        else:
            out[a * 2] = first.astype(BF)
            out[a * 2 + 1] = second.astype(BF)


def product(odd, choose, ranks, traces, right, left):
    smem = pl.BlockSpec(memory_space=pltpu.SMEM)
    vmem = pl.BlockSpec(memory_space=pltpu.VMEM)
    hbm = pl.BlockSpec(memory_space=pltpu.HBM)
    if odd:
        shapes = (
            jax.ShapeDtypeStruct((4, 256, 128), F32),
            jax.ShapeDtypeStruct((4, 256, 128), BF),
        )
    else:
        shapes = jax.ShapeDtypeStruct((8, 256, 128), BF)
    return pl.pallas_call(
        functools.partial(product_kernel, odd, choose),
        out_shape=shapes,
        in_specs=[smem] + [vmem] * len(traces) + [hbm, hbm],
        out_specs=(vmem, vmem) if odd else vmem,
        scratch_shapes=[
            pltpu.VMEM((16, 256, 128), BF),
            pltpu.VMEM((16, 256, 128), BF),
            pltpu.VMEM((4, 256, 256), BF),
            pltpu.VMEM((4, 256, 512), BF),
            pltpu.SemaphoreType.DMA((4,)),
        ],
        compiler_params=pltpu.CompilerParams(vmem_limit_bytes=60 * 2**20),
        cost_estimate=pl.CostEstimate(
            flops=16 * 2 * 256**3, bytes_accessed=3 * 2**20, transcendentals=0
        ),
        name="odd_product" if odd else "even_product",
    )(ranks, *traces, right, left)


def on_device(
    even_left, even_right, odd_left, odd_right, even_ranks, odd_ranks, even_sources, odd_sources
):
    section = lax.axis_index("layer")
    even_left, even_right, odd_left, odd_right = (
        factor.reshape(2, 16, 256, 128) for factor in (even_left, even_right, odd_left, odd_right)
    )
    even_ranks, odd_ranks = even_ranks.reshape(2, 16), odd_ranks.reshape(2, 16)
    even_src = jnp.swapaxes(even_sources[:, 0], 2, 3).reshape(2, 256, 128)
    odd_src = jnp.swapaxes(odd_sources[:, 0], 2, 3).reshape(2, 256, 128)

    def odd_terms(traces, slot):
        return product(True, (up_section(slot),), odd_ranks, traces, odd_right, odd_left)

    def even_terms(traces, choose):
        return product(False, choose, even_ranks, traces, even_right, even_left)

    def swap_core(value):
        return send(value, lambda l, zh, core: (l, zh, 1 - core), range(4))

    def row_sum(keep, away):
        summed = keep + swap_core(away).astype(F32)
        total = summed[0]
        for shift in (1, 2, 3):
            part = summed[shift].astype(BF)
            part = send(part, lambda l, zh, core: (l, zh + shift, core), range(4))
            total = total + part.astype(F32)
        return total

    def row_spread(value, moves):
        value = value.astype(BF)
        parts = []
        for shift in range(4):

            def move(l, zh, core):
                if shift == 0 and moves[l] == l:
                    return None
                return (moves[l], zh + shift, core)

            if shift == 0 and all(l == moves[l] for l in moves):
                parts.append(value)
                continue
            part = send(value, move, tuple(moves))
            if shift == 0:
                for l in moves:
                    if moves[l] == l:
                        part = jnp.where(section == l, value, part)
            parts.append(part)
        buf = jnp.stack(parts)
        return buf, swap_core(buf)

    def col_sum(terms):
        terms = lax.all_to_all(terms, "col", 0, 0, tiled=True)
        return jnp.sum(terms.astype(F32), axis=0)

    def col_spread(value):
        value = jnp.broadcast_to(value.astype(BF)[None], (8, 256, 128))
        return lax.all_to_all(value, "col", 0, 0, tiled=True)

    even_sum = jnp.where(section == 0, even_src[0], 0.0)
    odd_sum = jnp.zeros((256, 128), F32)
    trace = col_spread(even_src[0])
    down_traces = None
    for slot in range(8):
        down, up = down_section(slot), up_section(slot)
        if slot % 2 == 0:
            total = row_sum(*odd_terms((trace,), slot))
            if slot == 0:
                total = jnp.where(section == up, odd_src[1], total + odd_src[0])
            else:
                total = total + jnp.where(section == up, odd_src[1], odd_src[0])
            active = jnp.logical_or(section == down, section == up)
            odd_sum = odd_sum + jnp.where(active, total, 0.0)
            if slot == 2:
                traces = row_spread(total, {up: up})
                down_traces = row_spread(total, {down: down + 1})
            elif slot == 6:
                traces = row_spread(total, {up: up})
            else:
                traces = row_spread(total, {down: down + 1, up: up})
            continue
        if slot == 3:
            terms = even_terms(down_traces, 0), even_terms(traces, 1)
            terms = lax.all_to_all(jnp.concatenate(terms, axis=1), "col", 0, 0, tiled=True)
            terms = jnp.sum(terms.astype(F32), axis=0)
            down_total, up_total = terms[:256] + even_src[0], terms[256:] + even_src[1]
            even_sum = even_sum + jnp.where(section == down, down_total + up_total, 0.0)
        else:
            total = col_sum(even_terms(traces, (up,)))
            total = total + jnp.where(section == up, even_src[1], even_src[0])
            active = jnp.logical_or(section == down, section == up)
            even_sum = even_sum + jnp.where(active, total, 0.0)
            down_total = up_total = total
        if slot < 7:
            moved = send(up_total.astype(BF), lambda l, zh, core: (l - 1, zh, core), (up,))
            trace = col_spread(jnp.where(section == up - 1, moved, down_total.astype(BF)))

    even_traces = jnp.swapaxes(even_sum.reshape(2, 128, 128), 1, 2)
    odd_traces = jnp.swapaxes(odd_sum.reshape(2, 128, 128), 1, 2)
    return even_traces[None], odd_traces[None]


def solution(mesh):
    in_specs = (
        P(None, "layer", "row", "col", None, None),
        P(None, "layer", "row", "col", None, None),
        P(None, "layer", "col", "row", None, None),
        P(None, "layer", "col", "row", None, None),
        P(None, "layer", "row", "col"),
        P(None, "layer", "col", "row"),
        P(None, "layer", None, ("row", "col"), None),
        P(None, "layer", None, ("col", "row"), None),
    )
    out_specs = (P("layer", None, ("row", "col"), None), P("layer", None, ("col", "row"), None))
    return jax.shard_map(
        on_device, mesh=mesh, in_specs=in_specs, out_specs=out_specs, check_vma=False
    )
```

time: 1590 us -> 328 us (0.21); the launches traced: 1570 us -> 327 us
  waiting for transfers between devices: 789 us -> 113 us
  blocking collectives: 544 us -> 66.4 us
  matrix products: 66.5 us -> 0 us
  local copies, waits for them, and re-layouts: 70.2 us -> 9.63 us
  starting transfers between devices: 29.1 us -> 84.8 us
  other arithmetic: 57.2 us -> 6.61 us
  Pallas kernels: 0 us -> 44.8 us
    reduce_scatter x30 -> x0, waiting for transfers between devices: 787 us -> none  [the longest x15 405 us: even_reduce(): return lax.psum_scatter(terms, 'col', scatter_dimension=1, tiled=True)]
    all_gather x28 -> x0, blocking collectives: 544 us -> none  [the longest x14 325 us: odd_terms(): lax.all_gather(current.astype(jnp.bfloat16), 'col', axis=1, tiled=True)]
    ppermute x12 -> x42, waiting for transfers between devices: 1.44 us -> 86.4 us  [send(): return lax.ppermute(value, AXES, pairs)]
    dot_general x60 -> x0, matrix products: 66.5 us -> none  [the longest x30 49.7 us: tile_product(): jnp.einsum('acmr,kacrb->kamb', left_factor, stacked, preferred_element_ty...]
    all_to_all x0 -> x5, blocking collectives: none -> 66.4 us  [the longest x3 35.2 us: col_spread(): return lax.all_to_all(value, 'col', 0, 0, tiled=True)]
    transpose x30 -> x0, local copies, waits for them, and re-layouts: 56.5 us -> none  [tile_product(): jnp.einsum('acmr,kacrb->kamb', left_factor, stacked, preferred_element_ty...]
    pallas_call x0 -> x9, Pallas kernels: none -> 44.8 us  [product(): pl.pallas_call(functools.partial(product_kernel, odd, choose), out_shape=...]
    ppermute x12 -> x42, starting transfers between devices: 27.9 us -> 71.4 us  [send(): return lax.ppermute(value, AXES, pairs)]
  transfers between devices with their start and end apart: 42 -> 45, of which waited for: 24 -> 26; matrix products, arithmetic and copies ran while one was open for 8% -> 1% of each run, Pallas kernels for 0% -> 1%
where the time goes in v2:
time: 328 us; the launch traced here: 327 us
  waiting for transfers between devices  113 us (34%)
  starting transfers between devices  84.8 us (26%)
  blocking collectives  66.4 us (20%)
  Pallas kernels  44.8 us (14%)
  local copies, waits for them, and re-layouts  9.63 us (3%)
  other arithmetic  6.61 us (2%)
    ppermute x42, waiting for transfers between devices, send(): return lax.ppermute(value, AXES, pairs)  86.4 us
    ppermute x42, starting transfers between devices, send(): return lax.ppermute(value, AXES, pairs)  71.4 us
    pallas_call x9, Pallas kernels, product(): pl.pallas_call(functools.partial(product_kernel, odd, choose), out_shape=...  44.8 us
    all_to_all x3, blocking collectives, col_spread(): return lax.all_to_all(value, 'col', 0, 0, tiled=True)  35.2 us
    all_to_all x2, waiting for transfers between devices, col_sum(): terms = lax.all_to_all(terms, 'col', 0, 0, tiled=True)  18.1 us
    all_to_all x1, blocking collectives, on_device(): lax.all_to_all(jnp.concatenate(terms, axis=1), 'col', 0, 0, tiled=True)  17.9 us
    all_to_all x1, blocking collectives, col_sum(): terms = lax.all_to_all(terms, 'col', 0, 0, tiled=True)  13.2 us
    all_to_all x1, waiting for transfers between devices, col_spread(): return lax.all_to_all(value, 'col', 0, 0, tiled=True)  8.52 us
  transfers between devices with their start and end apart: 45, of which 26 were waited for; matrix products, arithmetic and copies ran while one was open for 1% of the time, Pallas kernels for 1%

profile of v2, /device:TPU:1, one launch (start us, length us, event | category | flops | bytes accessed | tf_op | source)
XLA Modules:
  0.0 326.6 jit_solution(8072719493517194979)
XLA Ops:
  2.6 6.4 %all-to-all-start = ((bf16[8,256,128]{2,1,0:T(8,128)(2,1)}), bf16[8,256,128]{2,1,0:T(8,128)(2,1)S(1)}, u32[]{:S(2)}, u32[]{:S(2)}) async-start(bf16[8,256,128]{2,1,0:T(8,128)(2,1)} %broadcast_in_dim.43), calls=%async_computation | async-start | bytes 1048576 | tf_op jit(solution)/shard_map/all_to_all | solution.py:222
  9.7 8.5 %all-to-all-done.refs_0_ = bf16[8,256,128]{2,1,0:T(8,128)(2,1)S(1)} async-done(((bf16[8,256,128]{2,1,0:T(8,128)(2,1)}), bf16[8,256,128]{2,1,0:T(8,128)(2,1)S(1)}, u32[]{:S(2)}, u32[]{:S(2)}) %all-to-all-start) | async-done | bytes 524320 | tf_op jit(solution)/shard_map/all_to_all | solution.py:222
  19.0 5.4 %odd_product.4 = (f32[4,256,128]{2,1,0:T(8,128)}, bf16[4,256,128]{2,1,0:T(8,128)(2,1)}) custom-call(s32[2,16]{1,0:T(2,128)} %reshape.59.ranks, bf16[8,256,128]{2,1,0:T(8,128)(2,1)} %copy-done, bf16[2,16,256,128]{3,2,1,0:T(8,128)(2,1)} %bitcast.198, bf16[2,16,256,128]{3,2,1,0:T(8,128)(2,1)} %bitcast.202), custom_call_target="tpu_custom_call" | custom-call | flops 536870912 | bytes 3145728 | tf_op jit(solution)/shard_map/odd_product/pallas_call | solution.py:145
  24.4 1.9 collective-permute-start
  28.9 3.1 collective-permute-start.1
  31.9 4.2 %collective-permute-start.2 = (bf16[256,128]{1,0:T(8,128)(2,1)S(1)}, bf16[256,128]{1,0:T(8,128)(2,1)S(1)}, u32[]{:S(2)}, u32[]{:S(2)}) collective-permute-start(bf16[256,128]{1,0:T(8,128)(2,1)S(1)} %get-tuple-element.45), channel_id=1, source_target_pairs={{0,32},{1,33},{2,34},{3,35},{4,36},{5,37},{6,38},{7,39},{8,40},{9,... | collective-permute-start | bytes 196616 | tf_op jit(solution)/shard_map/ppermute | solution.py:44
  36.2 2.4 collective-permute-start.3
  38.8 2.4 collective-permute-done.2
  41.2 1.9 collective-permute-done.3
  43.2 3.1 collective-permute-start.4
  46.3 2.2 collective-permute-start.5
  48.5 4.1 %collective-permute-start.6 = (bf16[256,128]{1,0:T(8,128)(2,1)S(1)}, bf16[256,128]{1,0:T(8,128)(2,1)S(1)}, u32[]{:S(2)}, u32[]{:S(2)}) collective-permute-start(bf16[256,128]{1,0:T(8,128)(2,1)S(1)} %get-tuple-element.30), channel_id=1, source_target_pairs={{0,96},{1,97},{2,98},{3,99},{4,100},{5,101},{6,102},{7,103},{8,104... | collective-permute-start | bytes 196616 | tf_op jit(solution)/shard_map/ppermute | solution.py:44
  54.1 2.9 collective-permute-done.7
  59.8 4.6 %even_product.5 = bf16[8,256,128]{2,1,0:T(8,128)(2,1)} custom-call(s32[2,16]{1,0:T(2,128)} %reshape.58.ranks, bf16[4,256,128]{2,1,0:T(8,128)(2,1)} %copy-done.4, bf16[4,256,128]{2,1,0:T(8,128)(2,1)} %copy-done.9, bf16[2,16,256,128]{3,2,1,0:T(8,128)(2,1)} %bitcast.188, bf16[2,16,256,128]{3,2,1,0:T(8,128)(2,1)} %bitcast.193), custom_call_target="tpu_custom_call" | custom-call | flops 536870912 | bytes 3145728 | tf_op jit(solution)/shard_map/even_product/pallas_call | solution.py:145
  64.4 3.5 %all-to-all-start.1 = ((bf16[8,256,128]{2,1,0:T(8,128)(2,1)}), bf16[8,256,128]{2,1,0:T(8,128)(2,1)S(1)}, u32[]{:S(2)}, u32[]{:S(2)}) async-start(bf16[8,256,128]{2,1,0:T(8,128)(2,1)} %even_product.5), calls=%async_computation.1 | async-start | bytes 1048576 | tf_op jit(solution)/shard_map/all_to_all | solution.py:217
  68.1 9.4 %all-to-all-done.1 = bf16[8,256,128]{2,1,0:T(8,128)(2,1)S(1)} async-done(((bf16[8,256,128]{2,1,0:T(8,128)(2,1)}), bf16[8,256,128]{2,1,0:T(8,128)(2,1)S(1)}, u32[]{:S(2)}, u32[]{:S(2)}) %all-to-all-start.1) | async-done | bytes 524320 | tf_op jit(solution)/shard_map/all_to_all | solution.py:217
  78.3 12.1 %all_to_all.40.refs_0_ = bf16[8,256,128]{2,1,0:T(8,128)(2,1)} all-to-all(bf16[8,256,128]{2,1,0:T(8,128)(2,1)S(1)} %broadcast_in_dim.44), channel_id=1, replica_groups=mesh['layer'=4,'row'=8,'col'=8] {'col'}, dimensions={0} | all-to-all | bytes 1048576 | tf_op jit(solution)/shard_map/all_to_all | solution.py:222
  90.4 5.4 %odd_product.5 = (f32[4,256,128]{2,1,0:T(8,128)}, bf16[4,256,128]{2,1,0:T(8,128)(2,1)}) custom-call(s32[2,16]{1,0:T(2,128)} %reshape.59.ranks, bf16[8,256,128]{2,1,0:T(8,128)(2,1)} %all_to_all.40.refs_0_, bf16[2,16,256,128]{3,2,1,0:T(8,128)(2,1)} %bitcast.199, bf16[2,16,256,128]{3,2,1,0:T(8,128)(2,1)} %bitcast.203), custom_call_target="tpu_custom_call" | custom-call | flops 536870912 | bytes 3145728 | tf_op jit(solution)/shard_map/odd_product/pallas_call | solution.py:145
  95.9 2.3 collective-permute-start.10
  102.1 2.3 collective-permute-start.12
  105.6 1.8 collective-permute-done.11
  107.4 1.8 collective-permute-done.12
  109.2 4.2 %collective-permute-done.13 = bf16[256,128]{1,0:T(8,128)(2,1)S(1)} collective-permute-done((bf16[256,128]{1,0:T(8,128)(2,1)S(1)}, bf16[256,128]{1,0:T(8,128)(2,1)S(1)}, u32[]{:S(2)}, u32[]{:S(2)}) %collective-permute-start.13) | collective-permute-done | bytes 65568 | tf_op jit(solution)/shard_map/ppermute | solution.py:44
  120.7 4.6 %even_product.6 = bf16[8,256,128]{2,1,0:T(8,128)(2,1)} custom-call(s32[2,16]{1,0:T(2,128)} %reshape.58.ranks, bf16[4,256,128]{2,1,0:T(8,128)(2,1)} %copy-done.2, bf16[4,256,128]{2,1,0:T(8,128)(2,1)} %copy-done.7, bf16[2,16,256,128]{3,2,1,0:T(8,128)(2,1)} %bitcast.189, bf16[2,16,256,128]{3,2,1,0:T(8,128)(2,1)} %bitcast.194), custom_call_target="tpu_custom_call" | custom-call | flops 536870912 | bytes 3145728 | tf_op jit(solution)/shard_map/even_product/pallas_call | solution.py:145
  126.1 4.6 %even_product.7 = bf16[8,256,128]{2,1,0:T(8,128)(2,1)} custom-call(s32[2,16]{1,0:T(2,128)} %reshape.58.ranks, bf16[4,256,128]{2,1,0:T(8,128)(2,1)} %copy-done.3, bf16[4,256,128]{2,1,0:T(8,128)(2,1)} %copy-done.8, bf16[2,16,256,128]{3,2,1,0:T(8,128)(2,1)} %bitcast.190, bf16[2,16,256,128]{3,2,1,0:T(8,128)(2,1)} %bitcast.195), custom_call_target="tpu_custom_call" | custom-call | flops 536870912 | bytes 3145728 | tf_op jit(solution)/shard_map/even_product/pallas_call | solution.py:145
  131.8 17.9 %all_to_all.41 = bf16[8,512,128]{2,1,0:T(8,128)(2,1)S(1)} all-to-all(bf16[8,512,128]{2,1,0:T(8,128)(2,1)S(1)} %pad_maximum_fusion), channel_id=1, replica_groups=mesh['layer'=4,'row'=8,'col'=8] {'col'}, dimensions={0} | all-to-all | bytes 2097152 | tf_op jit(solution)/shard_map/all_to_all | solution.py:248
  150.7 12.0 %all_to_all.42.refs_0_ = bf16[8,256,128]{2,1,0:T(8,128)(2,1)} all-to-all(bf16[8,256,128]{2,1,0:T(8,128)(2,1)S(1)} %broadcast_in_dim.45), channel_id=1, replica_groups=mesh['layer'=4,'row'=8,'col'=8] {'col'}, dimensions={0} | all-to-all | bytes 1048576 | tf_op jit(solution)/shard_map/all_to_all | solution.py:222
  162.7 5.4 %odd_product.6 = (f32[4,256,128]{2,1,0:T(8,128)}, bf16[4,256,128]{2,1,0:T(8,128)(2,1)}) custom-call(s32[2,16]{1,0:T(2,128)} %reshape.59.ranks, bf16[8,256,128]{2,1,0:T(8,128)(2,1)} %all_to_all.42.refs_0_, bf16[2,16,256,128]{3,2,1,0:T(8,128)(2,1)} %bitcast.200, bf16[2,16,256,128]{3,2,1,0:T(8,128)(2,1)} %bitcast.204), custom_call_target="tpu_custom_call" | custom-call | flops 536870912 | bytes 3145728 | tf_op jit(solution)/shard_map/odd_product/pallas_call | solution.py:145
  168.1 2.2 collective-permute-start.24
  174.3 2.4 collective-permute-start.26
  181.4 4.2 %collective-permute-done.27 = bf16[256,128]{1,0:T(8,128)(2,1)S(1)} collective-permute-done((bf16[256,128]{1,0:T(8,128)(2,1)S(1)}, bf16[256,128]{1,0:T(8,128)(2,1)S(1)}, u32[]{:S(2)}, u32[]{:S(2)}) %collective-permute-start.27) | collective-permute-done | bytes 65568 | tf_op jit(solution)/shard_map/ppermute | solution.py:44
  190.9 4.6 %even_product.8 = bf16[8,256,128]{2,1,0:T(8,128)(2,1)} custom-call(s32[2,16]{1,0:T(2,128)} %reshape.58.ranks, bf16[4,256,128]{2,1,0:T(8,128)(2,1)} %copy-done.6, bf16[4,256,128]{2,1,0:T(8,128)(2,1)} %copy-done.11, bf16[2,16,256,128]{3,2,1,0:T(8,128)(2,1)} %bitcast.191, bf16[2,16,256,128]{3,2,1,0:T(8,128)(2,1)} %bitcast.196), custom_call_target="tpu_custom_call" | custom-call | flops 536870912 | bytes 3145728 | tf_op jit(solution)/shard_map/even_product/pallas_call | solution.py:145
  195.5 13.2 %all_to_all.43 = bf16[8,256,128]{2,1,0:T(8,128)(2,1)S(1)} all-to-all(bf16[8,256,128]{2,1,0:T(8,128)(2,1)} %even_product.8), channel_id=1, replica_groups=mesh['layer'=4,'row'=8,'col'=8] {'col'}, dimensions={0} | all-to-all | bytes 1048576 | tf_op jit(solution)/shard_map/all_to_all | solution.py:217
  210.2 43.6 %collective-permute-done.33 = bf16[256,128]{1,0:T(8,128)(2,1)S(1)} collective-permute-done((bf16[256,128]{1,0:T(8,128)(2,1)S(1)}, bf16[256,128]{1,0:T(8,128)(2,1)S(1)}, u32[]{:S(2)}, u32[]{:S(2)}) %collective-permute-start.33) | collective-permute-done | bytes 65568 | tf_op jit(solution)/shard_map/ppermute | solution.py:44
  253.9 11.1 %all_to_all.44.refs_0_ = bf16[8,256,128]{2,1,0:T(8,128)(2,1)} all-to-all(bf16[8,256,128]{2,1,0:T(8,128)(2,1)S(1)} %broadcast_in_dim.46), channel_id=1, replica_groups=mesh['layer'=4,'row'=8,'col'=8] {'col'}, dimensions={0} | all-to-all | bytes 1048576 | tf_op jit(solution)/shard_map/all_to_all | solution.py:222
  265.0 5.4 %odd_product.7 = (f32[4,256,128]{2,1,0:T(8,128)}, bf16[4,256,128]{2,1,0:T(8,128)(2,1)}) custom-call(s32[2,16]{1,0:T(2,128)} %reshape.59.ranks, bf16[8,256,128]{2,1,0:T(8,128)(2,1)} %all_to_all.44.refs_0_, bf16[2,16,256,128]{3,2,1,0:T(8,128)(2,1)} %bitcast.201, bf16[2,16,256,128]{3,2,1,0:T(8,128)(2,1)} %bitcast.205), custom_call_target="tpu_custom_call" | custom-call | flops 536870912 | bytes 3145728 | tf_op jit(solution)/shard_map/odd_product/pallas_call | solution.py:145
  270.4 3.1 collective-permute-start.34
  276.0 2.5 collective-permute-start.35
  278.5 2.6 collective-permute-start.36
  282.2 3.5 %collective-permute-done.36 = bf16[256,128]{1,0:T(8,128)(2,1)S(1)} collective-permute-done((bf16[256,128]{1,0:T(8,128)(2,1)S(1)}, bf16[256,128]{1,0:T(8,128)(2,1)S(1)}, u32[]{:S(2)}, u32[]{:S(2)}) %collective-permute-start.36) | collective-permute-done | bytes 65568 | tf_op jit(solution)/shard_map/ppermute | solution.py:44
  285.6 3.3 %collective-permute-done.37 = bf16[256,128]{1,0:T(8,128)(2,1)S(1)} collective-permute-done((bf16[256,128]{1,0:T(8,128)(2,1)S(1)}, bf16[256,128]{1,0:T(8,128)(2,1)S(1)}, u32[]{:S(2)}, u32[]{:S(2)}) %collective-permute-start.37) | collective-permute-done | bytes 65568 | tf_op jit(solution)/shard_map/ppermute | solution.py:44
  289.0 4.1 %collective-permute-start.38 = (bf16[256,128]{1,0:T(8,128)(2,1)S(1)}, bf16[256,128]{1,0:T(8,128)(2,1)S(1)}, u32[]{:S(2)}, u32[]{:S(2)}) collective-permute-start(bf16[256,128]{1,0:T(8,128)(2,1)S(1)} %get-tuple-element.19), channel_id=1, source_target_pairs={{0,16},{1,17},{2,18},{3,19},{4,20},{5,21},{6,22},{7,23},{8,24},{9,... | collective-permute-start | bytes 196616 | tf_op jit(solution)/shard_map/ppermute | solution.py:44
  293.1 4.7 %collective-permute-start.39 = (bf16[256,128]{1,0:T(8,128)(2,1)S(1)}, bf16[256,128]{1,0:T(8,128)(2,1)S(1)}, u32[]{:S(2)}, u32[]{:S(2)}) collective-permute-start(bf16[256,128]{1,0:T(8,128)(2,1)S(1)} %get-tuple-element.19), channel_id=1, source_target_pairs={{0,32},{1,33},{2,34},{3,35},{4,36},{5,37},{6,38},{7,39},{8,40},{9,... | collective-permute-start | bytes 196616 | tf_op jit(solution)/shard_map/ppermute | solution.py:44
  297.8 3.0 collective-permute-start.40
  302.1 2.8 collective-permute-done.40
  308.0 4.6 %even_product.9 = bf16[8,256,128]{2,1,0:T(8,128)(2,1)} custom-call(s32[2,16]{1,0:T(2,128)} %reshape.58.ranks, bf16[4,256,128]{2,1,0:T(8,128)(2,1)} %copy-done.5, bf16[4,256,128]{2,1,0:T(8,128)(2,1)} %copy-done.10, bf16[2,16,256,128]{3,2,1,0:T(8,128)(2,1)} %bitcast.192, bf16[2,16,256,128]{3,2,1,0:T(8,128)(2,1)} %bitcast.197), custom_call_target="tpu_custom_call" | custom-call | flops 536870912 | bytes 3145728 | tf_op jit(solution)/shard_map/even_product/pallas_call | solution.py:145
  312.6 3.5 %all-to-all-start.7 = ((bf16[8,256,128]{2,1,0:T(8,128)(2,1)}), bf16[8,256,128]{2,1,0:T(8,128)(2,1)S(1)}, u32[]{:S(2)}, u32[]{:S(2)}) async-start(bf16[8,256,128]{2,1,0:T(8,128)(2,1)} %even_product.9), calls=%async_computation.7 | async-start | bytes 1048576 | tf_op jit(solution)/shard_map/all_to_all | solution.py:217
  316.9 8.7 %all-to-all-done.7 = bf16[8,256,128]{2,1,0:T(8,128)(2,1)S(1)} async-done(((bf16[8,256,128]{2,1,0:T(8,128)(2,1)}), bf16[8,256,128]{2,1,0:T(8,128)(2,1)S(1)}, u32[]{:S(2)}, u32[]{:S(2)}) %all-to-all-start.7) | async-done | bytes 524320 | tf_op jit(solution)/shard_map/all_to_all | solution.py:217
  (132 shorter events, 51.4 us)
Async XLA Ops:
  0.6 8.4 %copy-start.13 = (s32[2,1,4,4]{3,2,1,0:T(4,128)S(1)}, s32[2,1,4,4]{3,2,1,0:T(4,128)}, u32[]{:S(2)}) copy-start(s32[2,1,4,4]{3,2,1,0:T(4,128)} %param.13) | copy-start | bytes 388
  2.6 15.5 %all-to-all-start = ((bf16[8,256,128]{2,1,0:T(8,128)(2,1)}), bf16[8,256,128]{2,1,0:T(8,128)(2,1)S(1)}, u32[]{:S(2)}, u32[]{:S(2)}) async-start(bf16[8,256,128]{2,1,0:T(8,128)(2,1)} %broadcast_in_dim.43), calls=%async_computation | async-start | bytes 1048576 | tf_op jit(solution)/shard_map/all_to_all | solution.py:222
  24.4 14.1 %copy-start.12 = (f32[2,1,2,128,128]{4,3,2,1,0:T(8,128)S(1)}, f32[2,1,2,128,128]{4,3,2,1,0:T(8,128)}, u32[]{:S(2)}) copy-start(f32[2,1,2,128,128]{4,3,2,1,0:T(8,128)} %param.15) | copy-start | bytes 786436
  24.4 3.3 %collective-permute-start = (bf16[4,256,128]{2,1,0:T(8,128)(2,1)}, bf16[4,256,128]{2,1,0:T(8,128)(2,1)S(1)}, u32[]{:S(2)}, u32[]{:S(2)}) collective-permute-start(bf16[4,256,128]{2,1,0:T(8,128)(2,1)} %get-tuple-element.11), channel_id=1, source_target_pairs={{0,8},{1,9},{2,10},{3,11},{4,12},{5,13},{6,14},{7,15},{8,0},{9,1},... | collective-permute-start | bytes 786440 | tf_op jit(solution)/shard_map/ppermute | solution.py:44
  27.7 30.2 %copy-start.14 = (s32[2,1,4,4]{3,2,1,0:T(4,128)S(1)}, s32[2,1,4,4]{3,2,1,0:T(4,128)}, u32[]{:S(2)}) copy-start(s32[2,1,4,4]{3,2,1,0:T(4,128)} %param.12) | copy-start | bytes 388
  28.9 9.9 %collective-permute-start.1 = (bf16[256,128]{1,0:T(8,128)(2,1)S(1)}, bf16[256,128]{1,0:T(8,128)(2,1)S(1)}, u32[]{:S(2)}, u32[]{:S(2)}) collective-permute-start(bf16[256,128]{1,0:T(8,128)(2,1)S(1)} %get-tuple-element.43), channel_id=1, source_target_pairs={{0,16},{1,17},{2,18},{3,19},{4,20},{5,21},{6,22},{7,23},{8,24},{9,... | collective-permute-start | bytes 196616 | tf_op jit(solution)/shard_map/ppermute | solution.py:44
  31.9 9.3 %collective-permute-start.2 = (bf16[256,128]{1,0:T(8,128)(2,1)S(1)}, bf16[256,128]{1,0:T(8,128)(2,1)S(1)}, u32[]{:S(2)}, u32[]{:S(2)}) collective-permute-start(bf16[256,128]{1,0:T(8,128)(2,1)S(1)} %get-tuple-element.45), channel_id=1, source_target_pairs={{0,32},{1,33},{2,34},{3,35},{4,36},{5,37},{6,38},{7,39},{8,40},{9,... | collective-permute-start | bytes 196616 | tf_op jit(solution)/shard_map/ppermute | solution.py:44
  36.2 7.0 %collective-permute-start.3 = (bf16[256,128]{1,0:T(8,128)(2,1)S(1)}, bf16[256,128]{1,0:T(8,128)(2,1)S(1)}, u32[]{:S(2)}, u32[]{:S(2)}) collective-permute-start(bf16[256,128]{1,0:T(8,128)(2,1)S(1)} %get-tuple-element.44), channel_id=1, source_target_pairs={{0,48},{1,49},{2,50},{3,51},{4,52},{5,53},{6,54},{7,55},{8,56},{9,... | collective-permute-start | bytes 196616 | tf_op jit(solution)/shard_map/ppermute | solution.py:44
  43.2 10.8 %collective-permute-start.4 = (bf16[256,128]{1,0:T(8,128)(2,1)S(1)}, bf16[256,128]{1,0:T(8,128)(2,1)S(1)}, u32[]{:S(2)}, u32[]{:S(2)}) collective-permute-start(bf16[256,128]{1,0:T(8,128)(2,1)S(1)} %get-tuple-element.30), channel_id=1, source_target_pairs={{0,64},{1,65},{2,66},{3,67},{4,68},{5,69},{6,70},{7,71},{8,72},{9,... | collective-permute-start | bytes 196616 | tf_op jit(solution)/shard_map/ppermute | solution.py:44
  46.3 7.7 %collective-permute-start.5 = (bf16[256,128]{1,0:T(8,128)(2,1)S(1)}, bf16[256,128]{1,0:T(8,128)(2,1)S(1)}, u32[]{:S(2)}, u32[]{:S(2)}) collective-permute-start(bf16[256,128]{1,0:T(8,128)(2,1)S(1)} %get-tuple-element.30), channel_id=1, source_target_pairs={{0,80},{1,81},{2,82},{3,83},{4,84},{5,85},{6,86},{7,87},{8,88},{9,... | collective-permute-start | bytes 196616 | tf_op jit(solution)/shard_map/ppermute | solution.py:44
  48.5 5.5 %collective-permute-start.6 = (bf16[256,128]{1,0:T(8,128)(2,1)S(1)}, bf16[256,128]{1,0:T(8,128)(2,1)S(1)}, u32[]{:S(2)}, u32[]{:S(2)}) collective-permute-start(bf16[256,128]{1,0:T(8,128)(2,1)S(1)} %get-tuple-element.30), channel_id=1, source_target_pairs={{0,96},{1,97},{2,98},{3,99},{4,100},{5,101},{6,102},{7,103},{8,104... | collective-permute-start | bytes 196616 | tf_op jit(solution)/shard_map/ppermute | solution.py:44
  52.6 4.3 %collective-permute-start.7 = (bf16[256,128]{1,0:T(8,128)(2,1)S(1)}, bf16[256,128]{1,0:T(8,128)(2,1)S(1)}, u32[]{:S(2)}, u32[]{:S(2)}) collective-permute-start(bf16[256,128]{1,0:T(8,128)(2,1)S(1)} %get-tuple-element.30), channel_id=1, source_target_pairs={{0,112},{1,113},{2,114},{3,115},{4,116},{5,117},{6,118},{7,119},{8... | collective-permute-start | bytes 196616 | tf_op jit(solution)/shard_map/ppermute | solution.py:44
  57.0 2.1 collective-permute-start.8
  64.4 13.0 %all-to-all-start.1 = ((bf16[8,256,128]{2,1,0:T(8,128)(2,1)}), bf16[8,256,128]{2,1,0:T(8,128)(2,1)S(1)}, u32[]{:S(2)}, u32[]{:S(2)}) async-start(bf16[8,256,128]{2,1,0:T(8,128)(2,1)} %even_product.5), calls=%async_computation.1 | async-start | bytes 1048576 | tf_op jit(solution)/shard_map/all_to_all | solution.py:217
  77.5 0.7 collective-permute-start.9
  95.9 3.6 %collective-permute-start.10 = (bf16[4,256,128]{2,1,0:T(8,128)(2,1)}, bf16[4,256,128]{2,1,0:T(8,128)(2,1)S(1)}, u32[]{:S(2)}, u32[]{:S(2)}) collective-permute-start(bf16[4,256,128]{2,1,0:T(8,128)(2,1)} %get-tuple-element.13), channel_id=1, source_target_pairs={{0,8},{1,9},{2,10},{3,11},{4,12},{5,13},{6,14},{7,15},{8,0},{9,1},... | collective-permute-start | bytes 786440 | tf_op jit(solution)/shard_map/ppermute | solution.py:44
  100.6 6.8 %collective-permute-start.11 = (bf16[256,128]{1,0:T(8,128)(2,1)S(1)}, bf16[256,128]{1,0:T(8,128)(2,1)S(1)}, u32[]{:S(2)}, u32[]{:S(2)}) collective-permute-start(bf16[256,128]{1,0:T(8,128)(2,1)S(1)} %get-tuple-element.40), channel_id=1, source_target_pairs={{0,16},{1,17},{2,18},{3,19},{4,20},{5,21},{6,22},{7,23},{8,24},{9,... | collective-permute-start | bytes 196616 | tf_op jit(solution)/shard_map/ppermute | solution.py:44
  102.1 7.1 %collective-permute-start.12 = (bf16[256,128]{1,0:T(8,128)(2,1)S(1)}, bf16[256,128]{1,0:T(8,128)(2,1)S(1)}, u32[]{:S(2)}, u32[]{:S(2)}) collective-permute-start(bf16[256,128]{1,0:T(8,128)(2,1)S(1)} %get-tuple-element.42), channel_id=1, source_target_pairs={{0,32},{1,33},{2,34},{3,35},{4,36},{5,37},{6,38},{7,39},{8,40},{9,... | collective-permute-start | bytes 196616 | tf_op jit(solution)/shard_map/ppermute | solution.py:44
  104.4 9.1 %collective-permute-start.13 = (bf16[256,128]{1,0:T(8,128)(2,1)S(1)}, bf16[256,128]{1,0:T(8,128)(2,1)S(1)}, u32[]{:S(2)}, u32[]{:S(2)}) collective-permute-start(bf16[256,128]{1,0:T(8,128)(2,1)S(1)} %get-tuple-element.41), channel_id=1, source_target_pairs={{0,48},{1,49},{2,50},{3,51},{4,52},{5,53},{6,54},{7,55},{8,56},{9,... | collective-permute-start | bytes 196616 | tf_op jit(solution)/shard_map/ppermute | solution.py:44
  113.5 3.4 %collective-permute-start.14 = (bf16[256,128]{1,0:T(8,128)(2,1)S(1)}, bf16[256,128]{1,0:T(8,128)(2,1)S(1)}, u32[]{:S(2)}, u32[]{:S(2)}) collective-permute-start(bf16[256,128]{1,0:T(8,128)(2,1)S(1)} %get-tuple-element.26), channel_id=1, source_target_pairs={{64,128},{65,129},{66,130},{67,131},{68,132},{69,133},{70,134},{71... | collective-permute-start | bytes 196616 | tf_op jit(solution)/shard_map/ppermute | solution.py:44
  114.2 3.4 %collective-permute-start.15 = (bf16[256,128]{1,0:T(8,128)(2,1)S(1)}, bf16[256,128]{1,0:T(8,128)(2,1)S(1)}, u32[]{:S(2)}, u32[]{:S(2)}) collective-permute-start(bf16[256,128]{1,0:T(8,128)(2,1)S(1)} %get-tuple-element.26), channel_id=1, source_target_pairs={{64,144},{65,145},{66,146},{67,147},{68,148},{69,149},{70,150},{71... | collective-permute-start | bytes 196616 | tf_op jit(solution)/shard_map/ppermute | solution.py:44
  114.8 3.4 %collective-permute-start.16 = (bf16[256,128]{1,0:T(8,128)(2,1)S(1)}, bf16[256,128]{1,0:T(8,128)(2,1)S(1)}, u32[]{:S(2)}, u32[]{:S(2)}) collective-permute-start(bf16[256,128]{1,0:T(8,128)(2,1)S(1)} %get-tuple-element.26), channel_id=1, source_target_pairs={{64,160},{65,161},{66,162},{67,163},{68,164},{69,165},{70,166},{71... | collective-permute-start | bytes 196616 | tf_op jit(solution)/shard_map/ppermute | solution.py:44
  115.5 2.7 collective-permute-start.17
  116.2 2.7 collective-permute-start.19
  116.9 2.0 collective-permute-start.20
  117.5 1.3 collective-permute-start.21
  118.3 1.7 collective-permute-start.18
  118.9 6.4 %collective-permute-start.22 = (bf16[4,256,128]{2,1,0:T(8,128)(2,1)S(1)}, bf16[4,256,128]{2,1,0:T(8,128)(2,1)S(1)}, u32[]{:S(2)}, u32[]{:S(2)}) collective-permute-start(bf16[4,256,128]{2,1,0:T(8,128)(2,1)S(1)} %pad_maximum_fusion.3.refs_0_), channel_id=1, source_target_pairs={{0,8},{1,9},{2,10},{3,11},{4,12},{5,13},{6,14},{7,15},{8,0},{9,1},... | collective-permute-start | bytes 786440 | tf_op jit(solution)/shard_map/ppermute | solution.py:44
  149.9 0.7 collective-permute-start.23
  168.1 3.6 %collective-permute-start.24 = (bf16[4,256,128]{2,1,0:T(8,128)(2,1)}, bf16[4,256,128]{2,1,0:T(8,128)(2,1)S(1)}, u32[]{:S(2)}, u32[]{:S(2)}) collective-permute-start(bf16[4,256,128]{2,1,0:T(8,128)(2,1)} %get-tuple-element.15), channel_id=1, source_target_pairs={{0,8},{1,9},{2,10},{3,11},{4,12},{5,13},{6,14},{7,15},{8,0},{9,1},... | collective-permute-start | bytes 786440 | tf_op jit(solution)/shard_map/ppermute | solution.py:44
  172.8 7.0 %collective-permute-start.25 = (bf16[256,128]{1,0:T(8,128)(2,1)S(1)}, bf16[256,128]{1,0:T(8,128)(2,1)S(1)}, u32[]{:S(2)}, u32[]{:S(2)}) collective-permute-start(bf16[256,128]{1,0:T(8,128)(2,1)S(1)} %get-tuple-element.37), channel_id=1, source_target_pairs={{0,16},{1,17},{2,18},{3,19},{4,20},{5,21},{6,22},{7,23},{8,24},{9,... | collective-permute-start | bytes 196616 | tf_op jit(solution)/shard_map/ppermute | solution.py:44
  174.3 7.1 %collective-permute-start.26 = (bf16[256,128]{1,0:T(8,128)(2,1)S(1)}, bf16[256,128]{1,0:T(8,128)(2,1)S(1)}, u32[]{:S(2)}, u32[]{:S(2)}) collective-permute-start(bf16[256,128]{1,0:T(8,128)(2,1)S(1)} %get-tuple-element.39), channel_id=1, source_target_pairs={{0,32},{1,33},{2,34},{3,35},{4,36},{5,37},{6,38},{7,39},{8,40},{9,... | collective-permute-start | bytes 196616 | tf_op jit(solution)/shard_map/ppermute | solution.py:44
  176.7 8.8 %collective-permute-start.27 = (bf16[256,128]{1,0:T(8,128)(2,1)S(1)}, bf16[256,128]{1,0:T(8,128)(2,1)S(1)}, u32[]{:S(2)}, u32[]{:S(2)}) collective-permute-start(bf16[256,128]{1,0:T(8,128)(2,1)S(1)} %get-tuple-element.38), channel_id=1, source_target_pairs={{0,48},{1,49},{2,50},{3,51},{4,52},{5,53},{6,54},{7,55},{8,56},{9,... | collective-permute-start | bytes 196616 | tf_op jit(solution)/shard_map/ppermute | solution.py:44
  185.6 2.7 collective-permute-start.28
  186.3 2.0 collective-permute-start.29
  187.0 1.4 collective-permute-start.30
  187.7 0.7 collective-permute-start.31
  188.4 1.7 collective-permute-start.32
  208.9 44.9 %collective-permute-start.33 = (bf16[256,128]{1,0:T(8,128)(2,1)S(1)}, bf16[256,128]{1,0:T(8,128)(2,1)S(1)}, u32[]{:S(2)}, u32[]{:S(2)}) collective-permute-start(bf16[256,128]{1,0:T(8,128)(2,1)S(1)} %fusion.25), channel_id=1, source_target_pairs={{64,0},{65,1},{66,2},{67,3},{68,4},{69,5},{70,6},{71,7},{72,8},{73... | collective-permute-start | bytes 196616 | tf_op jit(solution)/shard_map/ppermute | solution.py:44
  270.4 4.4 %collective-permute-start.34 = (bf16[4,256,128]{2,1,0:T(8,128)(2,1)}, bf16[4,256,128]{2,1,0:T(8,128)(2,1)S(1)}, u32[]{:S(2)}, u32[]{:S(2)}) collective-permute-start(bf16[4,256,128]{2,1,0:T(8,128)(2,1)} %get-tuple-element.17), channel_id=1, source_target_pairs={{0,8},{1,9},{2,10},{3,11},{4,12},{5,13},{6,14},{7,15},{8,0},{9,1},... | collective-permute-start | bytes 786440 | tf_op jit(solution)/shard_map/ppermute | solution.py:44
  276.0 6.2 %collective-permute-start.35 = (bf16[256,128]{1,0:T(8,128)(2,1)S(1)}, bf16[256,128]{1,0:T(8,128)(2,1)S(1)}, u32[]{:S(2)}, u32[]{:S(2)}) collective-permute-start(bf16[256,128]{1,0:T(8,128)(2,1)S(1)} %get-tuple-element.34), channel_id=1, source_target_pairs={{0,16},{1,17},{2,18},{3,19},{4,20},{5,21},{6,22},{7,23},{8,24},{9,... | collective-permute-start | bytes 196616 | tf_op jit(solution)/shard_map/ppermute | solution.py:44
  278.5 7.1 %collective-permute-start.36 = (bf16[256,128]{1,0:T(8,128)(2,1)S(1)}, bf16[256,128]{1,0:T(8,128)(2,1)S(1)}, u32[]{:S(2)}, u32[]{:S(2)}) collective-permute-start(bf16[256,128]{1,0:T(8,128)(2,1)S(1)} %get-tuple-element.36), channel_id=1, source_target_pairs={{0,32},{1,33},{2,34},{3,35},{4,36},{5,37},{6,38},{7,39},{8,40},{9,... | collective-permute-start | bytes 196616 | tf_op jit(solution)/shard_map/ppermute | solution.py:44
  281.2 7.8 %collective-permute-start.37 = (bf16[256,128]{1,0:T(8,128)(2,1)S(1)}, bf16[256,128]{1,0:T(8,128)(2,1)S(1)}, u32[]{:S(2)}, u32[]{:S(2)}) collective-permute-start(bf16[256,128]{1,0:T(8,128)(2,1)S(1)} %get-tuple-element.35), channel_id=1, source_target_pairs={{0,48},{1,49},{2,50},{3,51},{4,52},{5,53},{6,54},{7,55},{8,56},{9,... | collective-permute-start | bytes 196616 | tf_op jit(solution)/shard_map/ppermute | solution.py:44
  289.0 11.8 %collective-permute-start.38 = (bf16[256,128]{1,0:T(8,128)(2,1)S(1)}, bf16[256,128]{1,0:T(8,128)(2,1)S(1)}, u32[]{:S(2)}, u32[]{:S(2)}) collective-permute-start(bf16[256,128]{1,0:T(8,128)(2,1)S(1)} %get-tuple-element.19), channel_id=1, source_target_pairs={{0,16},{1,17},{2,18},{3,19},{4,20},{5,21},{6,22},{7,23},{8,24},{9,... | collective-permute-start | bytes 196616 | tf_op jit(solution)/shard_map/ppermute | solution.py:44
  293.1 9.0 %collective-permute-start.39 = (bf16[256,128]{1,0:T(8,128)(2,1)S(1)}, bf16[256,128]{1,0:T(8,128)(2,1)S(1)}, u32[]{:S(2)}, u32[]{:S(2)}) collective-permute-start(bf16[256,128]{1,0:T(8,128)(2,1)S(1)} %get-tuple-element.19), channel_id=1, source_target_pairs={{0,32},{1,33},{2,34},{3,35},{4,36},{5,37},{6,38},{7,39},{8,40},{9,... | collective-permute-start | bytes 196616 | tf_op jit(solution)/shard_map/ppermute | solution.py:44
  297.8 7.1 %collective-permute-start.40 = (bf16[256,128]{1,0:T(8,128)(2,1)S(1)}, bf16[256,128]{1,0:T(8,128)(2,1)S(1)}, u32[]{:S(2)}, u32[]{:S(2)}) collective-permute-start(bf16[256,128]{1,0:T(8,128)(2,1)S(1)} %get-tuple-element.19), channel_id=1, source_target_pairs={{0,48},{1,49},{2,50},{3,51},{4,52},{5,53},{6,54},{7,55},{8,56},{9,... | collective-permute-start | bytes 196616 | tf_op jit(solution)/shard_map/ppermute | solution.py:44
  304.9 2.4 collective-permute-start.41
  312.6 13.0 %all-to-all-start.7 = ((bf16[8,256,128]{2,1,0:T(8,128)(2,1)}), bf16[8,256,128]{2,1,0:T(8,128)(2,1)S(1)}, u32[]{:S(2)}, u32[]{:S(2)}) async-start(bf16[8,256,128]{2,1,0:T(8,128)(2,1)} %even_product.9), calls=%async_computation.7 | async-start | bytes 1048576 | tf_op jit(solution)/shard_map/all_to_all | solution.py:217
  (12 other events, 24.0 us)

commit v3 on v2

--- a/solution.py
+++ b/solution.py
@@ -44,33 +44,35 @@
     return lax.ppermute(value, AXES, pairs)
 
 
-PIECES = ((0, 8), (8, 8))
-
-
-def product_kernel(odd, choose, ranks, *refs):
+def product_kernel(odd, choose, turn, ranks, *refs):
     if odd:
-        trace, right, left, keep, away, rights, lefts, xs, stacked, sems = refs
+        trace, right, left, keep, away, xs, stacked, lefts, rights, sems = refs
     else:
-        trace, other, right, left, out, rights, lefts, xs, stacked, sems = refs
+        trace, other, right, left, out, xs, stacked, lefts, sems = refs
     section, zh, core, _, _ = here()
     direction = choose if isinstance(choose, int) else (section == choose[0]).astype(jnp.int32)
 
     def piece(index):
-        source, kept = ((right, rights), (left, lefts))[index // 2]
-        start, size = PIECES[index % 2]
+        source, kept = ((left, lefts), (right, rights))[index // 2]
+        start, size = index % 2 * 8, 8
         return pltpu.make_async_copy(
             source.at[direction, pl.ds(start, size)], kept.at[pl.ds(start, size)], sems.at[index]
         )
 
-    for index in range(4):
-        piece(index).start()
+    if odd:
+        piece(2).start()
+        piece(3).start()
+    else:
+        rights = None
+        piece(0).start()
+        piece(1).start()
 
     for chunk in range(8):
         lanes = slice(chunk % 2 * 128, chunk % 2 * 128 + 128)
         if odd:
             xs[chunk // 2, :, lanes] = trace[chunk]
         else:
-            place = (zh - chunk // 2 + 4) % 4
+            place = (zh - chunk // 2 + 4) % 4 if turn else chunk // 2
 
             @pl.when(core == chunk % 2)
             def _(chunk=chunk, lanes=lanes, place=place):
@@ -83,23 +85,28 @@
     lane = lax.broadcasted_iota(jnp.int32, (1, 128), 1)
     sign = jnp.where(lane < 64, 1.0, -1.0)
     for a_pair in range(2):
-        piece(a_pair).wait()
+        if odd:
+            piece(2 + a_pair).wait()
+            piece(a_pair).start()
         for c in range(4):
             tiles = (a_pair * 8 + c, a_pair * 8 + 4 + c)
-            joined = jnp.concatenate([rights[tile] for tile in tiles], axis=1)
+            joined = jnp.concatenate([rights[tile] if odd else right[direction, tile] for tile in tiles], axis=1)
             product = jnp.dot(xs[c], joined, preferred_element_type=F32)
             for side in range(2):
                 part = product[:, side * 128 : side * 128 + 128]
                 turned = pltpu.roll(part, 64, 1)
-                turned = jnp.concatenate(
-                    [-turned[64:128], turned[:64], -turned[192:], turned[128:192]], axis=0
-                )
-                mask = jnp.where(lane % 64 < ranks[direction, tiles[side]], 1.0, 0.0)
-                value = (part * sign + turned) * mask
-                stacked[a_pair * 2 + side, :, c * 128 : c * 128 + 128] = value.astype(BF)
+                mask = jnp.where(lane % 64 < ranks[direction, 0, a_pair * 2 + side, c], 1.0, 0.0)
+                part, turned = part * (sign * mask), turned * mask
+                lanes = slice(c * 128, c * 128 + 128)
+                for start in (0, 128):
+                    real, imag = slice(start, start + 64), slice(start + 64, start + 128)
+                    value = part[real] - turned[imag]
+                    stacked[a_pair * 2 + side, real, lanes] = value.astype(BF)
+                    value = part[imag] + turned[real]
+                    stacked[a_pair * 2 + side, imag, lanes] = value.astype(BF)
     for a in range(4):
         if a % 2 == 0:
-            piece(2 + a // 2).wait()
+            piece(a // 2).wait()
         total = None
         for c_pair in range(2):
             joined = jnp.concatenate(
@@ -114,7 +121,7 @@
             total = term if total is None else total + term
         first, second = total[:, :128], total[:, 128:]
         if odd:
-            place = (a - zh + 4) % 4
+            place = (a - zh + 4) % 4 if turn else a
 
             @pl.when(core == 0)
             def _(first=first, second=second, place=place):
@@ -131,11 +138,13 @@
             out[a * 2 + 1] = second.astype(BF)
 
 
-def product(odd, choose, ranks, traces, right, left):
+def product(odd, choose, ranks, traces, right, left, turn=True):
     smem = pl.BlockSpec(memory_space=pltpu.SMEM)
     vmem = pl.BlockSpec(memory_space=pltpu.VMEM)
     hbm = pl.BlockSpec(memory_space=pltpu.HBM)
+    left = pltpu.with_memory_space_constraint(left, pltpu.HBM)
     if odd:
+        right = pltpu.with_memory_space_constraint(right, pltpu.HBM)
         shapes = (
             jax.ShapeDtypeStruct((4, 256, 128), F32),
             jax.ShapeDtypeStruct((4, 256, 128), BF),
@@ -143,18 +152,17 @@
     else:
         shapes = jax.ShapeDtypeStruct((8, 256, 128), BF)
     return pl.pallas_call(
-        functools.partial(product_kernel, odd, choose),
+        functools.partial(product_kernel, odd, choose, turn),
         out_shape=shapes,
-        in_specs=[smem] + [vmem] * len(traces) + [hbm, hbm],
+        in_specs=[smem] + [vmem] * len(traces) + [hbm if odd else vmem, hbm],
         out_specs=(vmem, vmem) if odd else vmem,
         scratch_shapes=[
-            pltpu.VMEM((16, 256, 128), BF),
-            pltpu.VMEM((16, 256, 128), BF),
             pltpu.VMEM((4, 256, 256), BF),
             pltpu.VMEM((4, 256, 512), BF),
-            pltpu.SemaphoreType.DMA((4,)),
-        ],
-        compiler_params=pltpu.CompilerParams(vmem_limit_bytes=60 * 2**20),
+        ]
+        + [pltpu.VMEM((16, 256, 128), BF)] * (2 if odd else 1)
+        + [pltpu.SemaphoreType.DMA((4,))],
+        compiler_params=pltpu.CompilerParams(vmem_limit_bytes=20 * 2**20),
         cost_estimate=pl.CostEstimate(
             flops=16 * 2 * 256**3, bytes_accessed=3 * 2**20, transcendentals=0
         ),
@@ -169,15 +177,15 @@
     even_left, even_right, odd_left, odd_right = (
         factor.reshape(2, 16, 256, 128) for factor in (even_left, even_right, odd_left, odd_right)
     )
-    even_ranks, odd_ranks = even_ranks.reshape(2, 16), odd_ranks.reshape(2, 16)
     even_src = jnp.swapaxes(even_sources[:, 0], 2, 3).reshape(2, 256, 128)
     odd_src = jnp.swapaxes(odd_sources[:, 0], 2, 3).reshape(2, 256, 128)
 
     def odd_terms(traces, slot):
-        return product(True, (up_section(slot),), odd_ranks, traces, odd_right, odd_left)
-
-    def even_terms(traces, choose):
-        return product(False, choose, even_ranks, traces, even_right, even_left)
+        choose = (up_section(slot),)
+        return product(True, choose, odd_ranks, traces, odd_right, odd_left, slot < 6)
+
+    def even_terms(traces, choose, turn=True):
+        return product(False, choose, even_ranks, traces, even_right, even_left, turn)
 
     def swap_core(value):
         return send(value, lambda l, zh, core: (l, zh, 1 - core), range(4))
@@ -190,6 +198,20 @@
             part = send(part, lambda l, zh, core: (l, zh + shift, core), range(4))
             total = total + part.astype(F32)
         return total
+
+    def row_whole(keep, away, source):
+        value = keep + swap_core(away).astype(F32)
+        own = zh_mask * source[None]
+        value = value + own
+        flips = [lambda l, zh, core, bits=bits: (l, zh ^ bits, core) for bits in (1, 3)]
+        low, high = value[:2], value[2:]
+        for first, second in (flips, flips[::-1]):
+            low_in = send(low.astype(BF), first, range(4))
+            high_in = send(high.astype(BF), second, range(4))
+            low, high = low + low_in.astype(F32), high + high_in.astype(F32)
+        value = jnp.concatenate([low, high])
+        buf = value.astype(BF)
+        return jnp.sum(value * zh_mask, axis=0), (buf, swap_core(buf))
 
     def row_spread(value, moves):
         value = value.astype(BF)
@@ -221,6 +243,7 @@
         value = jnp.broadcast_to(value.astype(BF)[None], (8, 256, 128))
         return lax.all_to_all(value, "col", 0, 0, tiled=True)
 
+    zh_mask = (lax.iota(jnp.int32, 4) == here()[1]).astype(F32)[:, None, None]
     even_sum = jnp.where(section == 0, even_src[0], 0.0)
     odd_sum = jnp.zeros((256, 128), F32)
     trace = col_spread(even_src[0])
@@ -228,6 +251,12 @@
     for slot in range(8):
         down, up = down_section(slot), up_section(slot)
         if slot % 2 == 0:
+            if slot == 6:
+                source = jnp.where(section == up, odd_src[1], odd_src[0])
+                total, traces = row_whole(*odd_terms((trace,), slot), source)
+                active = jnp.logical_or(section == down, section == up)
+                odd_sum = odd_sum + jnp.where(active, total, 0.0)
+                continue
             total = row_sum(*odd_terms((trace,), slot))
             if slot == 0:
                 total = jnp.where(section == up, odd_src[1], total + odd_src[0])
@@ -238,8 +267,6 @@
             if slot == 2:
                 traces = row_spread(total, {up: up})
                 down_traces = row_spread(total, {down: down + 1})
-            elif slot == 6:
-                traces = row_spread(total, {up: up})
             else:
                 traces = row_spread(total, {down: down + 1, up: up})
             continue
@@ -250,7 +277,7 @@
             down_total, up_total = terms[:256] + even_src[0], terms[256:] + even_src[1]
             even_sum = even_sum + jnp.where(section == down, down_total + up_total, 0.0)
         else:
-            total = col_sum(even_terms(traces, (up,)))
+            total = col_sum(even_terms(traces, (up,), slot < 7))
             total = total + jnp.where(section == up, even_src[1], even_src[0])
             active = jnp.logical_or(section == down, section == up)
             even_sum = even_sum + jnp.where(active, total, 0.0)

time: 328 us -> 299 us (0.912)
  starting transfers between devices: 84.8 us -> 68.9 us
  Pallas kernels: 44.8 us -> 30.9 us
  blocking collectives: 66.4 us -> 79.5 us
  waiting for transfers between devices: 113 us -> 105 us
  local copies, waits for them, and re-layouts: 9.63 us -> 6.18 us
    all_to_all x3 -> x4, blocking collectives: 35.2 us -> 49.4 us  [col_spread(): return lax.all_to_all(value, 'col', 0, 0, tiled=True)]
    pallas_call x9, Pallas kernels: 44.8 us -> 30.9 us  [product(): pl.pallas_call(functools.partial(product_kernel, odd, choose, turn), out_...]
    ppermute x42 -> x40, starting transfers between devices: 71.4 us -> 61.8 us  [send(): return lax.ppermute(value, AXES, pairs)]
    all_to_all x1 -> x0, waiting for transfers between devices: 8.52 us -> none  [col_spread(): return lax.all_to_all(value, 'col', 0, 0, tiled=True)]
    all_to_all x1 -> x0, starting transfers between devices: 6.37 us -> none  [col_spread(): return lax.all_to_all(value, 'col', 0, 0, tiled=True)]
    unnamed x30 -> x12, local copies, waits for them, and re-layouts: 4.3 us -> 0.03 us
    another operation x4 -> x3, other arithmetic: 4.48 us -> 0.24 us
    ppermute x42 -> x40, waiting for transfers between devices: 86.4 us -> 88.9 us  [send(): return lax.ppermute(value, AXES, pairs)]
  transfers between devices with their start and end apart: 45 -> 42, of which waited for: 26 -> 24; matrix products, arithmetic and copies ran while one was open for 1% -> 1% of each run, Pallas kernels for 1% -> 1%
where the time goes in v3:
time: 299 us; the launch traced here: 297 us
  waiting for transfers between devices  105 us (35%)
  blocking collectives  79.5 us (27%)
  starting transfers between devices  68.9 us (23%)
  Pallas kernels  30.9 us (10%)
  local copies, waits for them, and re-layouts  6.18 us (2%)
  other arithmetic  5.57 us (2%)
    ppermute x40, waiting for transfers between devices, send(): return lax.ppermute(value, AXES, pairs)  88.9 us
    ppermute x40, starting transfers between devices, send(): return lax.ppermute(value, AXES, pairs)  61.8 us
    all_to_all x4, blocking collectives, col_spread(): return lax.all_to_all(value, 'col', 0, 0, tiled=True)  49.4 us
    pallas_call x9, Pallas kernels, product(): pl.pallas_call(functools.partial(product_kernel, odd, choose, turn), out_...  30.9 us
    all_to_all x1, blocking collectives, on_device(): lax.all_to_all(jnp.concatenate(terms, axis=1), 'col', 0, 0, tiled=True)  17.9 us
    all_to_all x2, waiting for transfers between devices, col_sum(): terms = lax.all_to_all(terms, 'col', 0, 0, tiled=True)  16.1 us
    all_to_all x1, blocking collectives, col_sum(): terms = lax.all_to_all(terms, 'col', 0, 0, tiled=True)  12.2 us
    all_to_all x2, starting transfers between devices, col_sum(): terms = lax.all_to_all(terms, 'col', 0, 0, tiled=True)  7.14 us
  transfers between devices with their start and end apart: 42, of which 24 were waited for; matrix products, arithmetic and copies ran while one was open for 1% of the time, Pallas kernels for 1%

profile of v3, /device:TPU:1, one launch (start us, length us, event | category | flops | bytes accessed | tf_op | source)
XLA Modules:
  0.0 297.3 jit_solution(17540853265230643463)
XLA Ops:
  0.6 1.6 fusion.37
  2.5 15.4 %all_to_all.40.refs_0_ = bf16[8,256,128]{2,1,0:T(8,128)(2,1)S(1)} all-to-all(bf16[8,256,128]{2,1,0:T(8,128)(2,1)S(1)} %broadcast_in_dim.45), channel_id=1, replica_groups=mesh['layer'=4,'row'=8,'col'=8] {'col'}, dimensions={0} | all-to-all | bytes 1048576 | tf_op jit(solution)/shard_map/all_to_all | solution.py:244
  17.9 4.4 %odd_product.4 = (f32[4,256,128]{2,1,0:T(8,128)S(1)}, bf16[4,256,128]{2,1,0:T(8,128)(2,1)S(1)}) custom-call(s32[2,1,4,4]{3,2,1,0:T(4,128)S(1)} %copy-done.2, bf16[8,256,128]{2,1,0:T(8,128)(2,1)S(1)} %all_to_all.40.refs_0_, bf16[2,16,256,128]{3,2,1,0:T(8,128)(2,1)} %bitcast.173, bf16[2,16,256,128]{3,2,1,0:T(8,128)(2,1)} %bitcast.177), custom_call_target="tpu_custom_call" | custom-call | flops 536870912 | bytes 3145728 | tf_op jit(solution)/shard_map/odd_product/pallas_call | solution.py:154
  22.3 1.9 collective-permute-start
  26.2 3.0 %collective-permute-start.1 = (bf16[256,128]{1,0:T(8,128)(2,1)}, bf16[256,128]{1,0:T(8,128)(2,1)S(1)}, u32[]{:S(2)}, u32[]{:S(2)}) collective-permute-start(bf16[256,128]{1,0:T(8,128)(2,1)} %get-tuple-element.43), channel_id=1, source_target_pairs={{0,16},{1,17},{2,18},{3,19},{4,20},{5,21},{6,22},{7,23},{8,24},{9,... | collective-permute-start | bytes 196616 | tf_op jit(solution)/shard_map/ppermute | solution.py:44
  29.1 4.2 %collective-permute-start.2 = (bf16[256,128]{1,0:T(8,128)(2,1)}, bf16[256,128]{1,0:T(8,128)(2,1)S(1)}, u32[]{:S(2)}, u32[]{:S(2)}) collective-permute-start(bf16[256,128]{1,0:T(8,128)(2,1)} %get-tuple-element.45), channel_id=1, source_target_pairs={{0,32},{1,33},{2,34},{3,35},{4,36},{5,37},{6,38},{7,39},{8,40},{9,... | collective-permute-start | bytes 196616 | tf_op jit(solution)/shard_map/ppermute | solution.py:44
  33.4 2.4 collective-permute-start.3
  36.0 2.6 collective-permute-done.2
  38.6 1.7 collective-permute-done.3
  41.1 3.1 %collective-permute-start.4 = (bf16[256,128]{1,0:T(8,128)(2,1)S(1)}, bf16[256,128]{1,0:T(8,128)(2,1)S(1)}, u32[]{:S(2)}, u32[]{:S(2)}) collective-permute-start(bf16[256,128]{1,0:T(8,128)(2,1)S(1)} %get-tuple-element.26), channel_id=1, source_target_pairs={{0,64},{1,65},{2,66},{3,67},{4,68},{5,69},{6,70},{7,71},{8,72},{9,... | collective-permute-start | bytes 196616 | tf_op jit(solution)/shard_map/ppermute | solution.py:44
  44.2 2.4 collective-permute-start.5
  46.6 4.1 %collective-permute-start.6 = (bf16[256,128]{1,0:T(8,128)(2,1)S(1)}, bf16[256,128]{1,0:T(8,128)(2,1)S(1)}, u32[]{:S(2)}, u32[]{:S(2)}) collective-permute-start(bf16[256,128]{1,0:T(8,128)(2,1)S(1)} %get-tuple-element.26), channel_id=1, source_target_pairs={{0,96},{1,97},{2,98},{3,99},{4,100},{5,101},{6,102},{7,103},{8,104... | collective-permute-start | bytes 196616 | tf_op jit(solution)/shard_map/ppermute | solution.py:44
  52.1 2.6 collective-permute-done.7
  57.0 3.2 %even_product.5 = bf16[8,256,128]{2,1,0:T(8,128)(2,1)} custom-call(s32[2,1,4,4]{3,2,1,0:T(4,128)S(1)} %copy-done.1, bf16[4,256,128]{2,1,0:T(8,128)(2,1)S(1)} %pad_maximum_fusion.2.refs_0_, bf16[4,256,128]{2,1,0:T(8,128)(2,1)S(1)} %collective-permute-done.8.refs_1_, bf16[2,16,256,128]{3,2,1,0:T(8,128)(2,1)S(1)} %bitcast.163, bf16[2,16,256,128]{3,2,1,0:T(8,128)(2,1)} %bitcast.168), custom_call_target="tpu_custom_call" | custom-call | flops 536870912 | bytes 3145728 | tf_op jit(solution)/shard_map/even_product/pallas_call | solution.py:154
  60.2 3.5 %all-to-all-start.1 = ((bf16[8,256,128]{2,1,0:T(8,128)(2,1)}), bf16[8,256,128]{2,1,0:T(8,128)(2,1)S(1)}, u32[]{:S(2)}, u32[]{:S(2)}) async-start(bf16[8,256,128]{2,1,0:T(8,128)(2,1)} %even_product.5), calls=%async_computation.1 | async-start | bytes 1048576 | tf_op jit(solution)/shard_map/all_to_all | solution.py:239
  64.7 8.5 %all-to-all-done.1 = bf16[8,256,128]{2,1,0:T(8,128)(2,1)S(1)} async-done(((bf16[8,256,128]{2,1,0:T(8,128)(2,1)}), bf16[8,256,128]{2,1,0:T(8,128)(2,1)S(1)}, u32[]{:S(2)}, u32[]{:S(2)}) %all-to-all-start.1) | async-done | bytes 524320 | tf_op jit(solution)/shard_map/all_to_all | solution.py:239
  74.1 12.4 %all_to_all.41.refs_0_ = bf16[8,256,128]{2,1,0:T(8,128)(2,1)S(1)} all-to-all(bf16[8,256,128]{2,1,0:T(8,128)(2,1)S(1)} %broadcast_in_dim.46), channel_id=1, replica_groups=mesh['layer'=4,'row'=8,'col'=8] {'col'}, dimensions={0} | all-to-all | bytes 1048576 | tf_op jit(solution)/shard_map/all_to_all | solution.py:244
  86.4 4.4 %odd_product.5 = (f32[4,256,128]{2,1,0:T(8,128)S(1)}, bf16[4,256,128]{2,1,0:T(8,128)(2,1)S(1)}) custom-call(s32[2,1,4,4]{3,2,1,0:T(4,128)S(1)} %copy-done.2, bf16[8,256,128]{2,1,0:T(8,128)(2,1)S(1)} %all_to_all.41.refs_0_, bf16[2,16,256,128]{3,2,1,0:T(8,128)(2,1)} %bitcast.174, bf16[2,16,256,128]{3,2,1,0:T(8,128)(2,1)} %bitcast.178), custom_call_target="tpu_custom_call" | custom-call | flops 536870912 | bytes 3145728 | tf_op jit(solution)/shard_map/odd_product/pallas_call | solution.py:154
  90.8 2.0 collective-permute-start.10
  95.8 2.7 collective-permute-start.12
  99.6 2.1 collective-permute-done.11
  101.7 1.5 collective-permute-done.12
  103.2 4.4 %collective-permute-done.13 = bf16[256,128]{1,0:T(8,128)(2,1)S(1)} collective-permute-done((bf16[256,128]{1,0:T(8,128)(2,1)}, bf16[256,128]{1,0:T(8,128)(2,1)S(1)}, u32[]{:S(2)}, u32[]{:S(2)}) %collective-permute-start.13) | collective-permute-done | bytes 65568 | tf_op jit(solution)/shard_map/ppermute | solution.py:44
  114.9 2.3 even_product.6
  117.2 2.3 even_product.7
  119.7 17.9 %all_to_all.42 = bf16[8,512,128]{2,1,0:T(8,128)(2,1)S(1)} all-to-all(bf16[8,512,128]{2,1,0:T(8,128)(2,1)S(1)} %pad_maximum_fusion), channel_id=1, replica_groups=mesh['layer'=4,'row'=8,'col'=8] {'col'}, dimensions={0} | all-to-all | bytes 2097152 | tf_op jit(solution)/shard_map/all_to_all | solution.py:275
  138.5 11.2 %all_to_all.43.refs_0_ = bf16[8,256,128]{2,1,0:T(8,128)(2,1)S(1)} all-to-all(bf16[8,256,128]{2,1,0:T(8,128)(2,1)S(1)} %broadcast_in_dim.47), channel_id=1, replica_groups=mesh['layer'=4,'row'=8,'col'=8] {'col'}, dimensions={0} | all-to-all | bytes 1048576 | tf_op jit(solution)/shard_map/all_to_all | solution.py:244
  149.7 4.4 %odd_product.6 = (f32[4,256,128]{2,1,0:T(8,128)S(1)}, bf16[4,256,128]{2,1,0:T(8,128)(2,1)S(1)}) custom-call(s32[2,1,4,4]{3,2,1,0:T(4,128)S(1)} %copy-done.2, bf16[8,256,128]{2,1,0:T(8,128)(2,1)S(1)} %all_to_all.43.refs_0_, bf16[2,16,256,128]{3,2,1,0:T(8,128)(2,1)} %bitcast.175, bf16[2,16,256,128]{3,2,1,0:T(8,128)(2,1)} %bitcast.179), custom_call_target="tpu_custom_call" | custom-call | flops 536870912 | bytes 3145728 | tf_op jit(solution)/shard_map/odd_product/pallas_call | solution.py:154
  154.1 2.3 collective-permute-start.24
  158.9 2.9 collective-permute-start.26
  163.1 1.8 collective-permute-done.25
  166.2 4.3 %collective-permute-done.27 = bf16[256,128]{1,0:T(8,128)(2,1)S(1)} collective-permute-done((bf16[256,128]{1,0:T(8,128)(2,1)S(1)}, bf16[256,128]{1,0:T(8,128)(2,1)S(1)}, u32[]{:S(2)}, u32[]{:S(2)}) %collective-permute-start.27) | collective-permute-done | bytes 65568 | tf_op jit(solution)/shard_map/ppermute | solution.py:44
  175.7 2.4 even_product.8
  178.1 12.2 %all_to_all.44 = bf16[8,256,128]{2,1,0:T(8,128)(2,1)S(1)} all-to-all(bf16[8,256,128]{2,1,0:T(8,128)(2,1)S(1)} %even_product.8), channel_id=1, replica_groups=mesh['layer'=4,'row'=8,'col'=8] {'col'}, dimensions={0} | all-to-all | bytes 1048576 | tf_op jit(solution)/shard_map/all_to_all | solution.py:239
  190.5 1.5 collective-permute-start.33
  192.0 43.2 %collective-permute-done.33 = bf16[256,128]{1,0:T(8,128)(2,1)S(1)} collective-permute-done((bf16[256,128]{1,0:T(8,128)(2,1)S(1)}, bf16[256,128]{1,0:T(8,128)(2,1)S(1)}, u32[]{:S(2)}, u32[]{:S(2)}) %collective-permute-start.33) | collective-permute-done | bytes 65568 | tf_op jit(solution)/shard_map/ppermute | solution.py:44
  235.3 10.4 %all_to_all.45.refs_0_ = bf16[8,256,128]{2,1,0:T(8,128)(2,1)S(1)} all-to-all(bf16[8,256,128]{2,1,0:T(8,128)(2,1)S(1)} %broadcast_in_dim.48), channel_id=1, replica_groups=mesh['layer'=4,'row'=8,'col'=8] {'col'}, dimensions={0} | all-to-all | bytes 1048576 | tf_op jit(solution)/shard_map/all_to_all | solution.py:244
  245.7 4.4 %odd_product.7 = (f32[4,256,128]{2,1,0:T(8,128)S(1)}, bf16[4,256,128]{2,1,0:T(8,128)(2,1)S(1)}) custom-call(s32[2,1,4,4]{3,2,1,0:T(4,128)S(1)} %copy-done.2, bf16[8,256,128]{2,1,0:T(8,128)(2,1)S(1)} %all_to_all.45.refs_0_, bf16[2,16,256,128]{3,2,1,0:T(8,128)(2,1)} %bitcast.176, bf16[2,16,256,128]{3,2,1,0:T(8,128)(2,1)} %bitcast.180), custom_call_target="tpu_custom_call" | custom-call | flops 536870912 | bytes 3145728 | tf_op jit(solution)/shard_map/odd_product/pallas_call | solution.py:154
  250.1 3.5 %collective-permute-start.34 = (bf16[4,256,128]{2,1,0:T(8,128)(2,1)S(1)}, bf16[4,256,128]{2,1,0:T(8,128)(2,1)}, u32[]{:S(2)}, u32[]{:S(2)}) collective-permute-start(bf16[4,256,128]{2,1,0:T(8,128)(2,1)S(1)} %get-tuple-element.17), channel_id=1, source_target_pairs={{0,8},{1,9},{2,10},{3,11},{4,12},{5,13},{6,14},{7,15},{8,0},{9,1},... | collective-permute-start | bytes 786440 | tf_op jit(solution)/shard_map/ppermute | solution.py:44
  256.0 2.7 collective-permute-start.35
  259.4 6.0 %collective-permute-done.35 = bf16[2,256,128]{2,1,0:T(8,128)(2,1)S(1)} collective-permute-done((bf16[2,256,128]{2,1,0:T(8,128)(2,1)S(1)}, bf16[2,256,128]{2,1,0:T(8,128)(2,1)S(1)}, u32[]{:S(2)}, u32[]{:S(2)}) %collective-permute-start.35) | collective-permute-done | bytes 131104 | tf_op jit(solution)/shard_map/ppermute | solution.py:44
  265.5 3.4 %collective-permute-start.36 = (bf16[2,256,128]{2,1,0:T(8,128)(2,1)S(1)}, bf16[2,256,128]{2,1,0:T(8,128)(2,1)S(1)}, u32[]{:S(2)}, u32[]{:S(2)}) collective-permute-start(bf16[2,256,128]{2,1,0:T(8,128)(2,1)S(1)} %get-tuple-element.32), channel_id=1, source_target_pairs={{0,48},{1,49},{2,50},{3,51},{4,52},{5,53},{6,54},{7,55},{8,56},{9,... | collective-permute-start | bytes 393224 | tf_op jit(solution)/shard_map/ppermute | solution.py:44
  268.9 4.9 %collective-permute-done.36 = bf16[2,256,128]{2,1,0:T(8,128)(2,1)S(1)} collective-permute-done((bf16[2,256,128]{2,1,0:T(8,128)(2,1)S(1)}, bf16[2,256,128]{2,1,0:T(8,128)(2,1)S(1)}, u32[]{:S(2)}, u32[]{:S(2)}) %collective-permute-start.36) | collective-permute-done | bytes 131104 | tf_op jit(solution)/shard_map/ppermute | solution.py:44
  273.8 3.1 %collective-permute-done.38 = bf16[2,256,128]{2,1,0:T(8,128)(2,1)S(1)} collective-permute-done((bf16[2,256,128]{2,1,0:T(8,128)(2,1)S(1)}, bf16[2,256,128]{2,1,0:T(8,128)(2,1)S(1)}, u32[]{:S(2)}, u32[]{:S(2)}) %collective-permute-start.38) | collective-permute-done | bytes 131104 | tf_op jit(solution)/shard_map/ppermute | solution.py:44
  277.0 2.0 collective-permute-start.39
  280.1 3.1 %even_product.9 = bf16[8,256,128]{2,1,0:T(8,128)(2,1)} custom-call(s32[2,1,4,4]{3,2,1,0:T(4,128)S(1)} %copy-done.1, bf16[4,256,128]{2,1,0:T(8,128)(2,1)S(1)} %fusion.refs_0_, bf16[4,256,128]{2,1,0:T(8,128)(2,1)S(1)} %collective-permute-done.39.refs_1_, bf16[2,16,256,128]{3,2,1,0:T(8,128)(2,1)S(1)} %bitcast.167, bf16[2,16,256,128]{3,2,1,0:T(8,128)(2,1)} %bitcast.172), custom_call_target="tpu_custom_call" | custom-call | flops 536870912 | bytes 3145728 | tf_op jit(solution)/shard_map/even_product/pallas_call | solution.py:154
  283.3 3.6 %all-to-all-start.7 = ((bf16[8,256,128]{2,1,0:T(8,128)(2,1)}), bf16[8,256,128]{2,1,0:T(8,128)(2,1)S(1)}, u32[]{:S(2)}, u32[]{:S(2)}) async-start(bf16[8,256,128]{2,1,0:T(8,128)(2,1)} %even_product.9), calls=%async_computation.7 | async-start | bytes 1048576 | tf_op jit(solution)/shard_map/all_to_all | solution.py:239
  288.8 7.6 %all-to-all-done.7 = bf16[8,256,128]{2,1,0:T(8,128)(2,1)S(1)} async-done(((bf16[8,256,128]{2,1,0:T(8,128)(2,1)}), bf16[8,256,128]{2,1,0:T(8,128)(2,1)S(1)}, u32[]{:S(2)}, u32[]{:S(2)}) %all-to-all-start.7) | async-done | bytes 524320 | tf_op jit(solution)/shard_map/all_to_all | solution.py:239
  (111 shorter events, 38.5 us)
Async XLA Ops:
  0.6 17.2 %copy-start.2 = (s32[2,1,4,4]{3,2,1,0:T(4,128)S(1)}, s32[2,1,4,4]{3,2,1,0:T(4,128)}, u32[]{:S(2)}) copy-start(s32[2,1,4,4]{3,2,1,0:T(4,128)} %ranks.16) | copy-start | bytes 388
  22.3 13.5 %copy-start.5 = (f32[2,1,2,128,128]{4,3,2,1,0:T(8,128)S(1)}, f32[2,1,2,128,128]{4,3,2,1,0:T(8,128)}, u32[]{:S(2)}) copy-start(f32[2,1,2,128,128]{4,3,2,1,0:T(8,128)} %param.15) | copy-start | bytes 786436
  22.3 3.1 %collective-permute-start = (bf16[4,256,128]{2,1,0:T(8,128)(2,1)S(1)}, bf16[4,256,128]{2,1,0:T(8,128)(2,1)S(1)}, u32[]{:S(2)}, u32[]{:S(2)}) collective-permute-start(bf16[4,256,128]{2,1,0:T(8,128)(2,1)S(1)} %get-tuple-element.11), channel_id=1, source_target_pairs={{0,8},{1,9},{2,10},{3,11},{4,12},{5,13},{6,14},{7,15},{8,0},{9,1},... | collective-permute-start | bytes 786440 | tf_op jit(solution)/shard_map/ppermute | solution.py:44
  25.4 31.6 %copy-start = (bf16[2,1,4,4,256,128]{5,4,3,2,1,0:T(8,128)(2,1)S(1)}, bf16[2,1,4,4,256,128]{5,4,3,2,1,0:T(8,128)(2,1)}, u32[]{:S(2)}) copy-start(bf16[2,1,4,4,256,128]{5,4,3,2,1,0:T(8,128)(2,1)} %param.9) | copy-start | bytes 6291460
  25.4 31.6 %copy-start.1 = (s32[2,1,4,4]{3,2,1,0:T(4,128)S(1)}, s32[2,1,4,4]{3,2,1,0:T(4,128)}, u32[]{:S(2)}) copy-start(s32[2,1,4,4]{3,2,1,0:T(4,128)} %ranks.17) | copy-start | bytes 388
  26.2 9.8 %collective-permute-start.1 = (bf16[256,128]{1,0:T(8,128)(2,1)}, bf16[256,128]{1,0:T(8,128)(2,1)S(1)}, u32[]{:S(2)}, u32[]{:S(2)}) collective-permute-start(bf16[256,128]{1,0:T(8,128)(2,1)} %get-tuple-element.43), channel_id=1, source_target_pairs={{0,16},{1,17},{2,18},{3,19},{4,20},{5,21},{6,22},{7,23},{8,24},{9,... | collective-permute-start | bytes 196616 | tf_op jit(solution)/shard_map/ppermute | solution.py:44
  29.1 9.5 %collective-permute-start.2 = (bf16[256,128]{1,0:T(8,128)(2,1)}, bf16[256,128]{1,0:T(8,128)(2,1)S(1)}, u32[]{:S(2)}, u32[]{:S(2)}) collective-permute-start(bf16[256,128]{1,0:T(8,128)(2,1)} %get-tuple-element.45), channel_id=1, source_target_pairs={{0,32},{1,33},{2,34},{3,35},{4,36},{5,37},{6,38},{7,39},{8,40},{9,... | collective-permute-start | bytes 196616 | tf_op jit(solution)/shard_map/ppermute | solution.py:44
  33.4 7.0 %collective-permute-start.3 = (bf16[256,128]{1,0:T(8,128)(2,1)}, bf16[256,128]{1,0:T(8,128)(2,1)S(1)}, u32[]{:S(2)}, u32[]{:S(2)}) collective-permute-start(bf16[256,128]{1,0:T(8,128)(2,1)} %get-tuple-element.44), channel_id=1, source_target_pairs={{0,48},{1,49},{2,50},{3,51},{4,52},{5,53},{6,54},{7,55},{8,56},{9,... | collective-permute-start | bytes 196616 | tf_op jit(solution)/shard_map/ppermute | solution.py:44
  41.1 10.9 %collective-permute-start.4 = (bf16[256,128]{1,0:T(8,128)(2,1)S(1)}, bf16[256,128]{1,0:T(8,128)(2,1)S(1)}, u32[]{:S(2)}, u32[]{:S(2)}) collective-permute-start(bf16[256,128]{1,0:T(8,128)(2,1)S(1)} %get-tuple-element.26), channel_id=1, source_target_pairs={{0,64},{1,65},{2,66},{3,67},{4,68},{5,69},{6,70},{7,71},{8,72},{9,... | collective-permute-start | bytes 196616 | tf_op jit(solution)/shard_map/ppermute | solution.py:44
  44.2 7.8 %collective-permute-start.5 = (bf16[256,128]{1,0:T(8,128)(2,1)S(1)}, bf16[256,128]{1,0:T(8,128)(2,1)S(1)}, u32[]{:S(2)}, u32[]{:S(2)}) collective-permute-start(bf16[256,128]{1,0:T(8,128)(2,1)S(1)} %get-tuple-element.26), channel_id=1, source_target_pairs={{0,80},{1,81},{2,82},{3,83},{4,84},{5,85},{6,86},{7,87},{8,88},{9,... | collective-permute-start | bytes 196616 | tf_op jit(solution)/shard_map/ppermute | solution.py:44
  46.6 5.5 %collective-permute-start.6 = (bf16[256,128]{1,0:T(8,128)(2,1)S(1)}, bf16[256,128]{1,0:T(8,128)(2,1)S(1)}, u32[]{:S(2)}, u32[]{:S(2)}) collective-permute-start(bf16[256,128]{1,0:T(8,128)(2,1)S(1)} %get-tuple-element.26), channel_id=1, source_target_pairs={{0,96},{1,97},{2,98},{3,99},{4,100},{5,101},{6,102},{7,103},{8,104... | collective-permute-start | bytes 196616 | tf_op jit(solution)/shard_map/ppermute | solution.py:44
  50.7 4.0 %collective-permute-start.7 = (bf16[256,128]{1,0:T(8,128)(2,1)S(1)}, bf16[256,128]{1,0:T(8,128)(2,1)S(1)}, u32[]{:S(2)}, u32[]{:S(2)}) collective-permute-start(bf16[256,128]{1,0:T(8,128)(2,1)S(1)} %get-tuple-element.26), channel_id=1, source_target_pairs={{0,112},{1,113},{2,114},{3,115},{4,116},{5,117},{6,118},{7,119},{8... | collective-permute-start | bytes 196616 | tf_op jit(solution)/shard_map/ppermute | solution.py:44
  54.7 2.3 collective-permute-start.8
  60.2 13.0 %all-to-all-start.1 = ((bf16[8,256,128]{2,1,0:T(8,128)(2,1)}), bf16[8,256,128]{2,1,0:T(8,128)(2,1)S(1)}, u32[]{:S(2)}, u32[]{:S(2)}) async-start(bf16[8,256,128]{2,1,0:T(8,128)(2,1)} %even_product.5), calls=%async_computation.1 | async-start | bytes 1048576 | tf_op jit(solution)/shard_map/all_to_all | solution.py:239
  73.3 0.7 collective-permute-start.9
  90.8 3.1 %collective-permute-start.10 = (bf16[4,256,128]{2,1,0:T(8,128)(2,1)S(1)}, bf16[4,256,128]{2,1,0:T(8,128)(2,1)S(1)}, u32[]{:S(2)}, u32[]{:S(2)}) collective-permute-start(bf16[4,256,128]{2,1,0:T(8,128)(2,1)S(1)} %get-tuple-element.13), channel_id=1, source_target_pairs={{0,8},{1,9},{2,10},{3,11},{4,12},{5,13},{6,14},{7,15},{8,0},{9,1},... | collective-permute-start | bytes 786440 | tf_op jit(solution)/shard_map/ppermute | solution.py:44
  94.7 7.0 %collective-permute-start.11 = (bf16[256,128]{1,0:T(8,128)(2,1)}, bf16[256,128]{1,0:T(8,128)(2,1)S(1)}, u32[]{:S(2)}, u32[]{:S(2)}) collective-permute-start(bf16[256,128]{1,0:T(8,128)(2,1)} %get-tuple-element.40), channel_id=1, source_target_pairs={{0,16},{1,17},{2,18},{3,19},{4,20},{5,21},{6,22},{7,23},{8,24},{9,... | collective-permute-start | bytes 196616 | tf_op jit(solution)/shard_map/ppermute | solution.py:44
  95.8 7.4 %collective-permute-start.12 = (bf16[256,128]{1,0:T(8,128)(2,1)}, bf16[256,128]{1,0:T(8,128)(2,1)S(1)}, u32[]{:S(2)}, u32[]{:S(2)}) collective-permute-start(bf16[256,128]{1,0:T(8,128)(2,1)} %get-tuple-element.42), channel_id=1, source_target_pairs={{0,32},{1,33},{2,34},{3,35},{4,36},{5,37},{6,38},{7,39},{8,40},{9,... | collective-permute-start | bytes 196616 | tf_op jit(solution)/shard_map/ppermute | solution.py:44
  98.5 9.2 %collective-permute-start.13 = (bf16[256,128]{1,0:T(8,128)(2,1)}, bf16[256,128]{1,0:T(8,128)(2,1)S(1)}, u32[]{:S(2)}, u32[]{:S(2)}) collective-permute-start(bf16[256,128]{1,0:T(8,128)(2,1)} %get-tuple-element.41), channel_id=1, source_target_pairs={{0,48},{1,49},{2,50},{3,51},{4,52},{5,53},{6,54},{7,55},{8,56},{9,... | collective-permute-start | bytes 196616 | tf_op jit(solution)/shard_map/ppermute | solution.py:44
  108.4 3.4 %collective-permute-start.14 = (bf16[256,128]{1,0:T(8,128)(2,1)S(1)}, bf16[256,128]{1,0:T(8,128)(2,1)S(1)}, u32[]{:S(2)}, u32[]{:S(2)}) collective-permute-start(bf16[256,128]{1,0:T(8,128)(2,1)S(1)} %get-tuple-element.22), channel_id=1, source_target_pairs={{64,128},{65,129},{66,130},{67,131},{68,132},{69,133},{70,134},{71... | collective-permute-start | bytes 196616 | tf_op jit(solution)/shard_map/ppermute | solution.py:44
  109.0 3.4 %collective-permute-start.15 = (bf16[256,128]{1,0:T(8,128)(2,1)S(1)}, bf16[256,128]{1,0:T(8,128)(2,1)S(1)}, u32[]{:S(2)}, u32[]{:S(2)}) collective-permute-start(bf16[256,128]{1,0:T(8,128)(2,1)S(1)} %get-tuple-element.22), channel_id=1, source_target_pairs={{64,144},{65,145},{66,146},{67,147},{68,148},{69,149},{70,150},{71... | collective-permute-start | bytes 196616 | tf_op jit(solution)/shard_map/ppermute | solution.py:44
  109.7 3.4 %collective-permute-start.16 = (bf16[256,128]{1,0:T(8,128)(2,1)S(1)}, bf16[256,128]{1,0:T(8,128)(2,1)S(1)}, u32[]{:S(2)}, u32[]{:S(2)}) collective-permute-start(bf16[256,128]{1,0:T(8,128)(2,1)S(1)} %get-tuple-element.22), channel_id=1, source_target_pairs={{64,160},{65,161},{66,162},{67,163},{68,164},{69,165},{70,166},{71... | collective-permute-start | bytes 196616 | tf_op jit(solution)/shard_map/ppermute | solution.py:44
  110.4 2.7 collective-permute-start.17
  111.0 2.7 collective-permute-start.19
  111.7 2.0 collective-permute-start.20
  112.4 1.3 collective-permute-start.21
  113.1 1.7 collective-permute-start.18
  113.8 3.5 %collective-permute-start.22 = (bf16[4,256,128]{2,1,0:T(8,128)(2,1)S(1)}, bf16[4,256,128]{2,1,0:T(8,128)(2,1)S(1)}, u32[]{:S(2)}, u32[]{:S(2)}) collective-permute-start(bf16[4,256,128]{2,1,0:T(8,128)(2,1)S(1)} %pad_maximum_fusion.4.refs_0_), channel_id=1, source_target_pairs={{0,8},{1,9},{2,10},{3,11},{4,12},{5,13},{6,14},{7,15},{8,0},{9,1},... | collective-permute-start | bytes 786440 | tf_op jit(solution)/shard_map/ppermute | solution.py:44
  137.7 0.7 collective-permute-start.23
  154.1 3.5 %collective-permute-start.24 = (bf16[4,256,128]{2,1,0:T(8,128)(2,1)S(1)}, bf16[4,256,128]{2,1,0:T(8,128)(2,1)S(1)}, u32[]{:S(2)}, u32[]{:S(2)}) collective-permute-start(bf16[4,256,128]{2,1,0:T(8,128)(2,1)S(1)} %get-tuple-element.15), channel_id=1, source_target_pairs={{0,8},{1,9},{2,10},{3,11},{4,12},{5,13},{6,14},{7,15},{8,0},{9,1},... | collective-permute-start | bytes 786440 | tf_op jit(solution)/shard_map/ppermute | solution.py:44
  157.7 7.2 %collective-permute-start.25 = (bf16[256,128]{1,0:T(8,128)(2,1)S(1)}, bf16[256,128]{1,0:T(8,128)(2,1)S(1)}, u32[]{:S(2)}, u32[]{:S(2)}) collective-permute-start(bf16[256,128]{1,0:T(8,128)(2,1)S(1)} %get-tuple-element.37), channel_id=1, source_target_pairs={{0,16},{1,17},{2,18},{3,19},{4,20},{5,21},{6,22},{7,23},{8,24},{9,... | collective-permute-start | bytes 196616 | tf_op jit(solution)/shard_map/ppermute | solution.py:44
  158.9 7.4 %collective-permute-start.26 = (bf16[256,128]{1,0:T(8,128)(2,1)S(1)}, bf16[256,128]{1,0:T(8,128)(2,1)S(1)}, u32[]{:S(2)}, u32[]{:S(2)}) collective-permute-start(bf16[256,128]{1,0:T(8,128)(2,1)S(1)} %get-tuple-element.39), channel_id=1, source_target_pairs={{0,32},{1,33},{2,34},{3,35},{4,36},{5,37},{6,38},{7,39},{8,40},{9,... | collective-permute-start | bytes 196616 | tf_op jit(solution)/shard_map/ppermute | solution.py:44
  161.7 8.7 %collective-permute-start.27 = (bf16[256,128]{1,0:T(8,128)(2,1)S(1)}, bf16[256,128]{1,0:T(8,128)(2,1)S(1)}, u32[]{:S(2)}, u32[]{:S(2)}) collective-permute-start(bf16[256,128]{1,0:T(8,128)(2,1)S(1)} %get-tuple-element.38), channel_id=1, source_target_pairs={{0,48},{1,49},{2,50},{3,51},{4,52},{5,53},{6,54},{7,55},{8,56},{9,... | collective-permute-start | bytes 196616 | tf_op jit(solution)/shard_map/ppermute | solution.py:44
  171.2 2.7 collective-permute-start.28
  171.8 2.0 collective-permute-start.29
  172.5 1.4 collective-permute-start.30
  173.2 0.7 collective-permute-start.31
  174.0 1.7 collective-permute-start.32
  190.4 44.9 %copy-start.3 = (f32[256,128]{1,0:T(8,128)}, f32[256,128]{1,0:T(8,128)S(1)}, u32[]{:S(2)}) copy-start(f32[256,128]{1,0:T(8,128)S(1)} %convert_reduce_fusion.2) | copy-start | bytes 393220
  190.5 44.8 %collective-permute-start.33 = (bf16[256,128]{1,0:T(8,128)(2,1)S(1)}, bf16[256,128]{1,0:T(8,128)(2,1)S(1)}, u32[]{:S(2)}, u32[]{:S(2)}) collective-permute-start(bf16[256,128]{1,0:T(8,128)(2,1)S(1)} %fusion.24), channel_id=1, source_target_pairs={{64,0},{65,1},{66,2},{67,3},{68,4},{69,5},{70,6},{71,7},{72,8},{73... | collective-permute-start | bytes 196616 | tf_op jit(solution)/shard_map/ppermute | solution.py:44
  250.1 4.8 %collective-permute-start.34 = (bf16[4,256,128]{2,1,0:T(8,128)(2,1)S(1)}, bf16[4,256,128]{2,1,0:T(8,128)(2,1)}, u32[]{:S(2)}, u32[]{:S(2)}) collective-permute-start(bf16[4,256,128]{2,1,0:T(8,128)(2,1)S(1)} %get-tuple-element.17), channel_id=1, source_target_pairs={{0,8},{1,9},{2,10},{3,11},{4,12},{5,13},{6,14},{7,15},{8,0},{9,1},... | collective-permute-start | bytes 786440 | tf_op jit(solution)/shard_map/ppermute | solution.py:44
  256.0 9.3 %collective-permute-start.35 = (bf16[2,256,128]{2,1,0:T(8,128)(2,1)S(1)}, bf16[2,256,128]{2,1,0:T(8,128)(2,1)S(1)}, u32[]{:S(2)}, u32[]{:S(2)}) collective-permute-start(bf16[2,256,128]{2,1,0:T(8,128)(2,1)S(1)} %get-tuple-element.34), channel_id=1, source_target_pairs={{0,16},{1,17},{2,18},{3,19},{4,20},{5,21},{6,22},{7,23},{8,24},{9,... | collective-permute-start | bytes 393224 | tf_op jit(solution)/shard_map/ppermute | solution.py:44
  258.8 6.6 %collective-permute-start.37 = (bf16[2,256,128]{2,1,0:T(8,128)(2,1)S(1)}, bf16[2,256,128]{2,1,0:T(8,128)(2,1)S(1)}, u32[]{:S(2)}, u32[]{:S(2)}) collective-permute-start(bf16[2,256,128]{2,1,0:T(8,128)(2,1)S(1)} %get-tuple-element.35), channel_id=1, source_target_pairs={{0,48},{1,49},{2,50},{3,51},{4,52},{5,53},{6,54},{7,55},{8,56},{9,... | collective-permute-start | bytes 393224 | tf_op jit(solution)/shard_map/ppermute | solution.py:44
  265.5 8.3 %collective-permute-start.36 = (bf16[2,256,128]{2,1,0:T(8,128)(2,1)S(1)}, bf16[2,256,128]{2,1,0:T(8,128)(2,1)S(1)}, u32[]{:S(2)}, u32[]{:S(2)}) collective-permute-start(bf16[2,256,128]{2,1,0:T(8,128)(2,1)S(1)} %get-tuple-element.32), channel_id=1, source_target_pairs={{0,48},{1,49},{2,50},{3,51},{4,52},{5,53},{6,54},{7,55},{8,56},{9,... | collective-permute-start | bytes 393224 | tf_op jit(solution)/shard_map/ppermute | solution.py:44
  268.9 8.0 %collective-permute-start.38 = (bf16[2,256,128]{2,1,0:T(8,128)(2,1)S(1)}, bf16[2,256,128]{2,1,0:T(8,128)(2,1)S(1)}, u32[]{:S(2)}, u32[]{:S(2)}) collective-permute-start(bf16[2,256,128]{2,1,0:T(8,128)(2,1)S(1)} %get-tuple-element.33), channel_id=1, source_target_pairs={{0,16},{1,17},{2,18},{3,19},{4,20},{5,21},{6,22},{7,23},{8,24},{9,... | collective-permute-start | bytes 393224 | tf_op jit(solution)/shard_map/ppermute | solution.py:44
  277.0 3.1 %collective-permute-start.39 = (bf16[4,256,128]{2,1,0:T(8,128)(2,1)S(1)}, bf16[4,256,128]{2,1,0:T(8,128)(2,1)S(1)}, u32[]{:S(2)}, u32[]{:S(2)}) collective-permute-start(bf16[4,256,128]{2,1,0:T(8,128)(2,1)S(1)} %fusion.refs_0_), channel_id=1, source_target_pairs={{0,8},{1,9},{2,10},{3,11},{4,12},{5,13},{6,14},{7,15},{8,0},{9,1},... | collective-permute-start | bytes 786440 | tf_op jit(solution)/shard_map/ppermute | solution.py:44
  283.3 13.2 %copy-start.4 = (f32[256,128]{1,0:T(8,128)S(1)}, f32[256,128]{1,0:T(8,128)}, u32[]{:S(2)}) copy-start(f32[256,128]{1,0:T(8,128)} %copy-done.3) | copy-start | bytes 393220
  283.3 13.1 %all-to-all-start.7 = ((bf16[8,256,128]{2,1,0:T(8,128)(2,1)}), bf16[8,256,128]{2,1,0:T(8,128)(2,1)S(1)}, u32[]{:S(2)}, u32[]{:S(2)}) async-start(bf16[8,256,128]{2,1,0:T(8,128)(2,1)} %even_product.9), calls=%async_computation.7 | async-start | bytes 1048576 | tf_op jit(solution)/shard_map/all_to_all | solution.py:239

commit v4 on v3

--- a/solution.py
+++ b/solution.py
@@ -44,12 +44,12 @@
     return lax.ppermute(value, AXES, pairs)
 
 
-def product_kernel(odd, choose, turn, ranks, *refs):
+def product_kernel(odd, choose, ranks, *refs):
     if odd:
         trace, right, left, keep, away, xs, stacked, lefts, rights, sems = refs
     else:
         trace, other, right, left, out, xs, stacked, lefts, sems = refs
-    section, zh, core, _, _ = here()
+    section, _, core, _, _ = here()
     direction = choose if isinstance(choose, int) else (section == choose[0]).astype(jnp.int32)
 
     def piece(index):
@@ -72,7 +72,7 @@
         if odd:
             xs[chunk // 2, :, lanes] = trace[chunk]
         else:
-            place = (zh - chunk // 2 + 4) % 4 if turn else chunk // 2
+            place = chunk // 2
 
             @pl.when(core == chunk % 2)
             def _(chunk=chunk, lanes=lanes, place=place):
@@ -121,7 +121,7 @@
             total = term if total is None else total + term
         first, second = total[:, :128], total[:, 128:]
         if odd:
-            place = (a - zh + 4) % 4 if turn else a
+            place = a
 
             @pl.when(core == 0)
             def _(first=first, second=second, place=place):
@@ -138,7 +138,7 @@
             out[a * 2 + 1] = second.astype(BF)
 
 
-def product(odd, choose, ranks, traces, right, left, turn=True):
+def product(odd, choose, ranks, traces, right, left):
     smem = pl.BlockSpec(memory_space=pltpu.SMEM)
     vmem = pl.BlockSpec(memory_space=pltpu.VMEM)
     hbm = pl.BlockSpec(memory_space=pltpu.HBM)
@@ -152,7 +152,7 @@
     else:
         shapes = jax.ShapeDtypeStruct((8, 256, 128), BF)
     return pl.pallas_call(
-        functools.partial(product_kernel, odd, choose, turn),
+        functools.partial(product_kernel, odd, choose),
         out_shape=shapes,
         in_specs=[smem] + [vmem] * len(traces) + [hbm if odd else vmem, hbm],
         out_specs=(vmem, vmem) if odd else vmem,
@@ -182,58 +182,63 @@
 
     def odd_terms(traces, slot):
         choose = (up_section(slot),)
-        return product(True, choose, odd_ranks, traces, odd_right, odd_left, slot < 6)
-
-    def even_terms(traces, choose, turn=True):
-        return product(False, choose, even_ranks, traces, even_right, even_left, turn)
+        return product(True, choose, odd_ranks, traces, odd_right, odd_left)
+
+    def even_terms(traces, choose):
+        return product(False, choose, even_ranks, traces, even_right, even_left)
 
     def swap_core(value):
         return send(value, lambda l, zh, core: (l, zh, 1 - core), range(4))
 
-    def row_sum(keep, away):
-        summed = keep + swap_core(away).astype(F32)
-        total = summed[0]
-        for shift in (1, 2, 3):
-            part = summed[shift].astype(BF)
-            part = send(part, lambda l, zh, core: (l, zh + shift, core), range(4))
-            total = total + part.astype(F32)
-        return total
-
-    def row_whole(keep, away, source):
+    def row_total(keep, away, source, slot):
+        down, up = down_section(slot), up_section(slot)
         value = keep + swap_core(away).astype(F32)
-        own = zh_mask * source[None]
-        value = value + own
-        flips = [lambda l, zh, core, bits=bits: (l, zh ^ bits, core) for bits in (1, 3)]
+        if slot == 0:
+            value = jnp.where(section == up, 0.0, value)
+        value = value + jnp.where(own_rows, source[None], 0.0)
         low, high = value[:2], value[2:]
-        for first, second in (flips, flips[::-1]):
-            low_in = send(low.astype(BF), first, range(4))
-            high_in = send(high.astype(BF), second, range(4))
-            low, high = low + low_in.astype(F32), high + high_in.astype(F32)
-        value = jnp.concatenate([low, high])
-        buf = value.astype(BF)
-        return jnp.sum(value * zh_mask, axis=0), (buf, swap_core(buf))
-
-    def row_spread(value, moves):
-        value = value.astype(BF)
-        parts = []
-        for shift in range(4):
-
+
+        def flip(bits):
+            return lambda l, zh, core: (l, zh ^ bits, core)
+
+        low_in = send(low.astype(BF), flip(1), range(4))
+        high_in = send(high.astype(BF), flip(3), range(4))
+        low, high = low + low_in.astype(F32), high + high_in.astype(F32)
+        low_out, high_out = low.astype(BF), high.astype(BF)
+        hops = slot < 6
+
+        def outcome(value):
+            buf = value.astype(BF)
+            return jnp.sum(jnp.where(own_rows, value, 0.0), axis=0), (buf, swap_core(buf))
+
+        def joined(low, high):
+            return jnp.concatenate([low, high])
+
+        if not hops:
+            low_in = send(low_out, flip(3), range(4)).astype(F32)
+            high_in = send(high_out, flip(1), range(4)).astype(F32)
+            both = outcome(joined(low + low_in, high + high_in))
+            return both, both
+
+        def target(bits, sections):
             def move(l, zh, core):
-                if shift == 0 and moves[l] == l:
-                    return None
-                return (moves[l], zh + shift, core)
-
-            if shift == 0 and all(l == moves[l] for l in moves):
-                parts.append(value)
-                continue
-            part = send(value, move, tuple(moves))
-            if shift == 0:
-                for l in moves:
-                    if moves[l] == l:
-                        part = jnp.where(section == l, value, part)
-            parts.append(part)
-        buf = jnp.stack(parts)
-        return buf, swap_core(buf)
+                return (l + 1 if l == down else l, zh ^ bits, core)
+
+            return lambda part: send(part, move, sections).astype(F32)
+
+        if down + 1 == up:
+            up_low = low + target(3, (up,))(low_out)
+            up_high = high + target(1, (up,))(high_out)
+            down_low = target(3, (down,))(low_out) + target(0, (down,))(low_out)
+            down_high = target(1, (down,))(high_out) + target(0, (down,))(high_out)
+            return outcome(joined(down_low, down_high)), outcome(joined(up_low, up_high))
+        stays = section == up
+        low_in = target(3, (down, up))(low_out)
+        high_in = target(1, (down, up))(high_out)
+        low = low_in + jnp.where(stays, low, target(0, (down,))(low_out))
+        high = high_in + jnp.where(stays, high, target(0, (down,))(high_out))
+        both = outcome(joined(low, high))
+        return both, both
 
     def col_sum(terms):
         terms = lax.all_to_all(terms, "col", 0, 0, tiled=True)
@@ -243,32 +248,21 @@
         value = jnp.broadcast_to(value.astype(BF)[None], (8, 256, 128))
         return lax.all_to_all(value, "col", 0, 0, tiled=True)
 
-    zh_mask = (lax.iota(jnp.int32, 4) == here()[1]).astype(F32)[:, None, None]
+    own_rows = (lax.iota(jnp.int32, 4) == here()[1])[:, None, None]
     even_sum = jnp.where(section == 0, even_src[0], 0.0)
-    odd_sum = jnp.zeros((256, 128), F32)
+    odd_sum = ahead = jnp.zeros((256, 128), F32)
     trace = col_spread(even_src[0])
-    down_traces = None
     for slot in range(8):
         down, up = down_section(slot), up_section(slot)
         if slot % 2 == 0:
+            source = jnp.where(section == up, odd_src[1], odd_src[0])
+            keep, away = odd_terms((trace,), slot)
+            (down_rows, down_traces), (up_rows, traces) = row_total(keep, away, source, slot)
+            odd_sum = odd_sum + jnp.where(section == up, up_rows, 0.0)
             if slot == 6:
-                source = jnp.where(section == up, odd_src[1], odd_src[0])
-                total, traces = row_whole(*odd_terms((trace,), slot), source)
-                active = jnp.logical_or(section == down, section == up)
-                odd_sum = odd_sum + jnp.where(active, total, 0.0)
-                continue
-            total = row_sum(*odd_terms((trace,), slot))
-            if slot == 0:
-                total = jnp.where(section == up, odd_src[1], total + odd_src[0])
+                odd_sum = odd_sum + jnp.where(section == down, down_rows, 0.0)
             else:
-                total = total + jnp.where(section == up, odd_src[1], odd_src[0])
-            active = jnp.logical_or(section == down, section == up)
-            odd_sum = odd_sum + jnp.where(active, total, 0.0)
-            if slot == 2:
-                traces = row_spread(total, {up: up})
-                down_traces = row_spread(total, {down: down + 1})
-            else:
-                traces = row_spread(total, {down: down + 1, up: up})
+                ahead = ahead + jnp.where(section == down + 1, down_rows, 0.0)
             continue
         if slot == 3:
             terms = even_terms(down_traces, 0), even_terms(traces, 1)
@@ -277,7 +271,7 @@
             down_total, up_total = terms[:256] + even_src[0], terms[256:] + even_src[1]
             even_sum = even_sum + jnp.where(section == down, down_total + up_total, 0.0)
         else:
-            total = col_sum(even_terms(traces, (up,), slot < 7))
+            total = col_sum(even_terms(traces, (up,)))
             total = total + jnp.where(section == up, even_src[1], even_src[0])
             active = jnp.logical_or(section == down, section == up)
             even_sum = even_sum + jnp.where(active, total, 0.0)
@@ -286,6 +280,7 @@
             moved = send(up_total.astype(BF), lambda l, zh, core: (l - 1, zh, core), (up,))
             trace = col_spread(jnp.where(section == up - 1, moved, down_total.astype(BF)))
 
+    odd_sum = odd_sum + send(ahead, lambda l, zh, core: (l - 1, zh, core), (1, 2, 3))
     even_traces = jnp.swapaxes(even_sum.reshape(2, 128, 128), 1, 2)
     odd_traces = jnp.swapaxes(odd_sum.reshape(2, 128, 128), 1, 2)
     return even_traces[None], odd_traces[None]

time: 299 us -> 282 us (0.943)
  waiting for transfers between devices: 105 us -> 97.3 us
  blocking collectives: 79.5 us -> 76.3 us
    all_to_all x2 -> x1, waiting for transfers between devices: 16.1 us -> 0.06 us  [col_sum(): terms = lax.all_to_all(terms, 'col', 0, 0, tiled=True)]
    all_to_all x4 -> x3, blocking collectives: 49.4 us -> 33.4 us  [col_spread(): return lax.all_to_all(value, 'col', 0, 0, tiled=True)]
    all_to_all x1 -> x2, blocking collectives: 12.2 us -> 25.1 us  [col_sum(): terms = lax.all_to_all(terms, 'col', 0, 0, tiled=True)]
    all_to_all x0 -> x1, waiting for transfers between devices: none -> 9.17 us  [col_spread(): return lax.all_to_all(value, 'col', 0, 0, tiled=True)]
    all_to_all x0 -> x1, starting transfers between devices: none -> 6.37 us  [col_spread(): return lax.all_to_all(value, 'col', 0, 0, tiled=True)]
    ppermute x40 -> x37, starting transfers between devices: 61.8 us -> 55.7 us  [send(): return lax.ppermute(value, AXES, pairs)]
    all_to_all x2 -> x1, starting transfers between devices: 7.14 us -> 4.15 us  [col_sum(): terms = lax.all_to_all(terms, 'col', 0, 0, tiled=True)]
    ppermute x40 -> x37, waiting for transfers between devices: 88.9 us -> 88.1 us  [send(): return lax.ppermute(value, AXES, pairs)]
  transfers between devices with their start and end apart: 42 -> 39, of which waited for: 24 -> 23; matrix products, arithmetic and copies ran while one was open for 1% -> 1% of each run, Pallas kernels for 1% -> 1%
where the time goes in v4:
time: 282 us; the launch traced here: 280 us
  waiting for transfers between devices  97.3 us (35%)
  blocking collectives  76.3 us (27%)
  starting transfers between devices  66.2 us (23%)
  Pallas kernels  30.1 us (11%)
  other arithmetic  5.07 us (2%)
  local copies, waits for them, and re-layouts  3.98 us (1%)
    ppermute x37, waiting for transfers between devices, send(): return lax.ppermute(value, AXES, pairs)  88.1 us
    ppermute x37, starting transfers between devices, send(): return lax.ppermute(value, AXES, pairs)  55.7 us
    all_to_all x3, blocking collectives, col_spread(): return lax.all_to_all(value, 'col', 0, 0, tiled=True)  33.4 us
    pallas_call x9, Pallas kernels, product(): pl.pallas_call(functools.partial(product_kernel, odd, choose), out_shape=...  30.1 us
    all_to_all x2, blocking collectives, col_sum(): terms = lax.all_to_all(terms, 'col', 0, 0, tiled=True)  25.1 us
    all_to_all x1, blocking collectives, on_device(): lax.all_to_all(jnp.concatenate(terms, axis=1), 'col', 0, 0, tiled=True)  17.8 us
    all_to_all x1, waiting for transfers between devices, col_spread(): return lax.all_to_all(value, 'col', 0, 0, tiled=True)  9.17 us
    all_to_all x1, starting transfers between devices, col_spread(): return lax.all_to_all(value, 'col', 0, 0, tiled=True)  6.37 us
  transfers between devices with their start and end apart: 39, of which 23 were waited for; matrix products, arithmetic and copies ran while one was open for 1% of the time, Pallas kernels for 1%

profile of v4, /device:TPU:1, one launch (start us, length us, event | category | flops | bytes accessed | tf_op | source)
XLA Modules:
  0.0 280.4 jit_solution(2269668172535724051)
XLA Ops:
  2.6 6.4 %all-to-all-start = ((bf16[8,256,128]{2,1,0:T(8,128)(2,1)}), bf16[8,256,128]{2,1,0:T(8,128)(2,1)S(1)}, u32[]{:S(2)}, u32[]{:S(2)}) async-start(bf16[8,256,128]{2,1,0:T(8,128)(2,1)} %broadcast_in_dim.126), calls=%async_computation | async-start | bytes 1048576 | tf_op jit(solution)/shard_map/all_to_all | solution.py:249
  9.0 9.2 %all-to-all-done.refs_0_ = bf16[8,256,128]{2,1,0:T(8,128)(2,1)S(1)} async-done(((bf16[8,256,128]{2,1,0:T(8,128)(2,1)}), bf16[8,256,128]{2,1,0:T(8,128)(2,1)S(1)}, u32[]{:S(2)}, u32[]{:S(2)}) %all-to-all-start) | async-done | bytes 524320 | tf_op jit(solution)/shard_map/all_to_all | solution.py:249
  18.2 4.4 %odd_product.4 = (f32[4,256,128]{2,1,0:T(8,128)S(1)}, bf16[4,256,128]{2,1,0:T(8,128)(2,1)S(1)}) custom-call(s32[2,1,4,4]{3,2,1,0:T(4,128)S(1)} %copy-done.2, bf16[8,256,128]{2,1,0:T(8,128)(2,1)S(1)} %all-to-all-done.refs_0_, bf16[2,16,256,128]{3,2,1,0:T(8,128)(2,1)} %bitcast.88, bf16[2,16,256,128]{3,2,1,0:T(8,128)(2,1)} %bitcast.92), custom_call_target="tpu_custom_call" | custom-call | flops 536870912 | bytes 3145728 | tf_op jit(solution)/shard_map/odd_product/pallas_call | solution.py:154
  22.6 1.9 collective-permute-start
  25.9 3.1 %collective-permute-start.1 = (bf16[2,256,128]{2,1,0:T(8,128)(2,1)S(1)}, bf16[2,256,128]{2,1,0:T(8,128)(2,1)S(1)}, u32[]{:S(2)}, u32[]{:S(2)}) collective-permute-start(bf16[2,256,128]{2,1,0:T(8,128)(2,1)S(1)} %get-tuple-element.47), channel_id=1, source_target_pairs={{0,16},{1,17},{2,18},{3,19},{4,20},{5,21},{6,22},{7,23},{8,24},{9,... | collective-permute-start | bytes 393224 | tf_op jit(solution)/shard_map/ppermute | solution.py:44
  28.9 3.3 %collective-permute-start.4 = (bf16[2,256,128]{2,1,0:T(8,128)(2,1)S(1)}, bf16[2,256,128]{2,1,0:T(8,128)(2,1)S(1)}, u32[]{:S(2)}, u32[]{:S(2)}) collective-permute-start(bf16[2,256,128]{2,1,0:T(8,128)(2,1)S(1)} %get-tuple-element.48), channel_id=1, source_target_pairs={{0,48},{1,49},{2,50},{3,51},{4,52},{5,53},{6,54},{7,55},{8,56},{9,... | collective-permute-start | bytes 393224 | tf_op jit(solution)/shard_map/ppermute | solution.py:44
  32.2 3.2 %collective-permute-done.1 = bf16[2,256,128]{2,1,0:T(8,128)(2,1)S(1)} collective-permute-done((bf16[2,256,128]{2,1,0:T(8,128)(2,1)S(1)}, bf16[2,256,128]{2,1,0:T(8,128)(2,1)S(1)}, u32[]{:S(2)}, u32[]{:S(2)}) %collective-permute-start.1) | collective-permute-done | bytes 131104 | tf_op jit(solution)/shard_map/ppermute | solution.py:44
  35.5 1.4 collective-permute-done.4
  36.9 4.9 %collective-permute-start.2 = (bf16[2,256,128]{2,1,0:T(8,128)(2,1)S(1)}, bf16[2,256,128]{2,1,0:T(8,128)(2,1)S(1)}, u32[]{:S(2)}, u32[]{:S(2)}) collective-permute-start(bf16[2,256,128]{2,1,0:T(8,128)(2,1)S(1)} %get-tuple-element.45), channel_id=1, source_target_pairs={{0,112},{1,113},{2,114},{3,115},{4,116},{5,117},{6,118},{7,119},{8... | collective-permute-start | bytes 393224 | tf_op jit(solution)/shard_map/ppermute | solution.py:44
  41.8 1.3 collective-permute-start.3
  43.1 2.3 collective-permute-start.5
  45.4 1.3 collective-permute-start.6
  47.8 3.8 %collective-permute-done.6 = bf16[2,256,128]{2,1,0:T(8,128)(2,1)S(1)} collective-permute-done((bf16[2,256,128]{2,1,0:T(8,128)(2,1)S(1)}, bf16[2,256,128]{2,1,0:T(8,128)(2,1)S(1)}, u32[]{:S(2)}, u32[]{:S(2)}) %collective-permute-start.6) | collective-permute-done | bytes 131104 | tf_op jit(solution)/shard_map/ppermute | solution.py:44
  51.7 3.7 %collective-permute-start.7 = (bf16[4,256,128]{2,1,0:T(8,128)(2,1)S(1)}, bf16[4,256,128]{2,1,0:T(8,128)(2,1)S(1)}, u32[]{:S(2)}, u32[]{:S(2)}) collective-permute-start(bf16[4,256,128]{2,1,0:T(8,128)(2,1)S(1)} %fusion.4.refs_0_), channel_id=1, source_target_pairs={{0,8},{1,9},{2,10},{3,11},{4,12},{5,13},{6,14},{7,15},{8,0},{9,1},... | collective-permute-start | bytes 786440 | tf_op jit(solution)/shard_map/ppermute | solution.py:44
  56.6 2.4 even_product.5
  59.0 13.3 %all_to_all.40 = bf16[8,256,128]{2,1,0:T(8,128)(2,1)S(1)} all-to-all(bf16[8,256,128]{2,1,0:T(8,128)(2,1)S(1)} %even_product.5), channel_id=1, replica_groups=mesh['layer'=4,'row'=8,'col'=8] {'col'}, dimensions={0} | all-to-all | bytes 1048576 | tf_op jit(solution)/shard_map/all_to_all | solution.py:244
  73.1 11.6 %all_to_all.41.refs_0_ = bf16[8,256,128]{2,1,0:T(8,128)(2,1)S(1)} all-to-all(bf16[8,256,128]{2,1,0:T(8,128)(2,1)S(1)} %broadcast_in_dim.129), channel_id=1, replica_groups=mesh['layer'=4,'row'=8,'col'=8] {'col'}, dimensions={0} | all-to-all | bytes 1048576 | tf_op jit(solution)/shard_map/all_to_all | solution.py:249
  84.7 4.4 %odd_product.5 = (f32[4,256,128]{2,1,0:T(8,128)S(1)}, bf16[4,256,128]{2,1,0:T(8,128)(2,1)S(1)}) custom-call(s32[2,1,4,4]{3,2,1,0:T(4,128)S(1)} %copy-done.2, bf16[8,256,128]{2,1,0:T(8,128)(2,1)S(1)} %all_to_all.41.refs_0_, bf16[2,16,256,128]{3,2,1,0:T(8,128)(2,1)} %bitcast.89, bf16[2,16,256,128]{3,2,1,0:T(8,128)(2,1)} %bitcast.93), custom_call_target="tpu_custom_call" | custom-call | flops 536870912 | bytes 3145728 | tf_op jit(solution)/shard_map/odd_product/pallas_call | solution.py:154
  89.1 2.4 collective-permute-start.9
  92.8 2.3 collective-permute-start.10
  96.1 5.8 %collective-permute-done.10 = bf16[2,256,128]{2,1,0:T(8,128)(2,1)S(1)} collective-permute-done((bf16[2,256,128]{2,1,0:T(8,128)(2,1)S(1)}, bf16[2,256,128]{2,1,0:T(8,128)(2,1)S(1)}, u32[]{:S(2)}, u32[]{:S(2)}) %collective-permute-start.10) | collective-permute-done | bytes 131104 | tf_op jit(solution)/shard_map/ppermute | solution.py:44
  101.8 2.2 collective-permute-done.13
  108.3 1.3 collective-permute-start.16
  110.8 2.3 even_product.6
  113.2 2.3 even_product.7
  115.6 17.8 %all_to_all.42 = bf16[8,512,128]{2,1,0:T(8,128)(2,1)S(1)} all-to-all(bf16[8,512,128]{2,1,0:T(8,128)(2,1)S(1)} %pad_maximum_fusion), channel_id=1, replica_groups=mesh['layer'=4,'row'=8,'col'=8] {'col'}, dimensions={0} | all-to-all | bytes 2097152 | tf_op jit(solution)/shard_map/all_to_all | solution.py:269
  134.4 11.5 %all_to_all.43.refs_0_ = bf16[8,256,128]{2,1,0:T(8,128)(2,1)S(1)} all-to-all(bf16[8,256,128]{2,1,0:T(8,128)(2,1)S(1)} %broadcast_in_dim.131), channel_id=1, replica_groups=mesh['layer'=4,'row'=8,'col'=8] {'col'}, dimensions={0} | all-to-all | bytes 1048576 | tf_op jit(solution)/shard_map/all_to_all | solution.py:249
  145.9 4.4 %odd_product.6 = (f32[4,256,128]{2,1,0:T(8,128)S(1)}, bf16[4,256,128]{2,1,0:T(8,128)(2,1)S(1)}) custom-call(s32[2,1,4,4]{3,2,1,0:T(4,128)S(1)} %copy-done.2, bf16[8,256,128]{2,1,0:T(8,128)(2,1)S(1)} %all_to_all.43.refs_0_, bf16[2,16,256,128]{3,2,1,0:T(8,128)(2,1)} %bitcast.90, bf16[2,16,256,128]{3,2,1,0:T(8,128)(2,1)} %bitcast.94), custom_call_target="tpu_custom_call" | custom-call | flops 536870912 | bytes 3145728 | tf_op jit(solution)/shard_map/odd_product/pallas_call | solution.py:154
  150.3 2.4 collective-permute-start.21
  154.2 1.8 collective-permute-start.25
  155.9 7.1 %collective-permute-done.22 = bf16[2,256,128]{2,1,0:T(8,128)(2,1)S(1)} collective-permute-done((bf16[2,256,128]{2,1,0:T(8,128)(2,1)S(1)}, bf16[2,256,128]{2,1,0:T(8,128)(2,1)S(1)}, u32[]{:S(2)}, u32[]{:S(2)}) %collective-permute-start.22) | collective-permute-done | bytes 131104 | tf_op jit(solution)/shard_map/ppermute | solution.py:44
  166.2 1.4 collective-permute-start.28
  168.7 2.4 even_product.8
  171.1 11.8 %all_to_all.44 = bf16[8,256,128]{2,1,0:T(8,128)(2,1)S(1)} all-to-all(bf16[8,256,128]{2,1,0:T(8,128)(2,1)S(1)} %even_product.8), channel_id=1, replica_groups=mesh['layer'=4,'row'=8,'col'=8] {'col'}, dimensions={0} | all-to-all | bytes 1048576 | tf_op jit(solution)/shard_map/all_to_all | solution.py:244
  183.0 1.3 collective-permute-start.29
  184.3 35.4 %collective-permute-done.29 = bf16[256,128]{1,0:T(8,128)(2,1)S(1)} collective-permute-done((bf16[256,128]{1,0:T(8,128)(2,1)S(1)}, bf16[256,128]{1,0:T(8,128)(2,1)S(1)}, u32[]{:S(2)}, u32[]{:S(2)}) %collective-permute-start.29) | collective-permute-done | bytes 65568 | tf_op jit(solution)/shard_map/ppermute | solution.py:44
  219.8 10.4 %all_to_all.45.refs_0_ = bf16[8,256,128]{2,1,0:T(8,128)(2,1)S(1)} all-to-all(bf16[8,256,128]{2,1,0:T(8,128)(2,1)S(1)} %broadcast_in_dim.133), channel_id=1, replica_groups=mesh['layer'=4,'row'=8,'col'=8] {'col'}, dimensions={0} | all-to-all | bytes 1048576 | tf_op jit(solution)/shard_map/all_to_all | solution.py:249
  230.1 4.4 %odd_product.7 = (f32[4,256,128]{2,1,0:T(8,128)S(1)}, bf16[4,256,128]{2,1,0:T(8,128)(2,1)S(1)}) custom-call(s32[2,1,4,4]{3,2,1,0:T(4,128)S(1)} %copy-done.2, bf16[8,256,128]{2,1,0:T(8,128)(2,1)S(1)} %all_to_all.45.refs_0_, bf16[2,16,256,128]{3,2,1,0:T(8,128)(2,1)} %bitcast.91, bf16[2,16,256,128]{3,2,1,0:T(8,128)(2,1)} %bitcast.95), custom_call_target="tpu_custom_call" | custom-call | flops 536870912 | bytes 3145728 | tf_op jit(solution)/shard_map/odd_product/pallas_call | solution.py:154
  234.5 3.2 %collective-permute-start.30 = (bf16[4,256,128]{2,1,0:T(8,128)(2,1)S(1)}, bf16[4,256,128]{2,1,0:T(8,128)(2,1)S(1)}, u32[]{:S(2)}, u32[]{:S(2)}) collective-permute-start(bf16[4,256,128]{2,1,0:T(8,128)(2,1)S(1)} %get-tuple-element.17), channel_id=1, source_target_pairs={{0,8},{1,9},{2,10},{3,11},{4,12},{5,13},{6,14},{7,15},{8,0},{9,1},... | collective-permute-start | bytes 786440 | tf_op jit(solution)/shard_map/ppermute | solution.py:44
  241.5 6.7 %collective-permute-done.31 = bf16[2,256,128]{2,1,0:T(8,128)(2,1)S(1)} collective-permute-done((bf16[2,256,128]{2,1,0:T(8,128)(2,1)S(1)}, bf16[2,256,128]{2,1,0:T(8,128)(2,1)S(1)}, u32[]{:S(2)}, u32[]{:S(2)}) %collective-permute-start.31) | collective-permute-done | bytes 131104 | tf_op jit(solution)/shard_map/ppermute | solution.py:44
  248.2 3.4 %collective-permute-start.32 = (bf16[2,256,128]{2,1,0:T(8,128)(2,1)S(1)}, bf16[2,256,128]{2,1,0:T(8,128)(2,1)S(1)}, u32[]{:S(2)}, u32[]{:S(2)}) collective-permute-start(bf16[2,256,128]{2,1,0:T(8,128)(2,1)S(1)} %get-tuple-element.27), channel_id=1, source_target_pairs={{0,48},{1,49},{2,50},{3,51},{4,52},{5,53},{6,54},{7,55},{8,56},{9,... | collective-permute-start | bytes 393224 | tf_op jit(solution)/shard_map/ppermute | solution.py:44
  251.6 4.2 %collective-permute-done.32 = bf16[2,256,128]{2,1,0:T(8,128)(2,1)S(1)} collective-permute-done((bf16[2,256,128]{2,1,0:T(8,128)(2,1)S(1)}, bf16[2,256,128]{2,1,0:T(8,128)(2,1)S(1)}, u32[]{:S(2)}, u32[]{:S(2)}) %collective-permute-start.32) | collective-permute-done | bytes 131104 | tf_op jit(solution)/shard_map/ppermute | solution.py:44
  255.8 3.1 %collective-permute-done.34 = bf16[2,256,128]{2,1,0:T(8,128)(2,1)S(1)} collective-permute-done((bf16[2,256,128]{2,1,0:T(8,128)(2,1)S(1)}, bf16[2,256,128]{2,1,0:T(8,128)(2,1)S(1)}, u32[]{:S(2)}, u32[]{:S(2)}) %collective-permute-start.34) | collective-permute-done | bytes 131104 | tf_op jit(solution)/shard_map/ppermute | solution.py:44
  259.1 1.3 collective-permute-start.35
  261.5 3.2 %even_product.9 = bf16[8,256,128]{2,1,0:T(8,128)(2,1)} custom-call(s32[2,1,4,4]{3,2,1,0:T(4,128)S(1)} %copy-done.1, bf16[4,256,128]{2,1,0:T(8,128)(2,1)S(1)} %fusion.refs_0_, bf16[4,256,128]{2,1,0:T(8,128)(2,1)S(1)} %collective-permute-done.35.refs_1_, bf16[2,16,256,128]{3,2,1,0:T(8,128)(2,1)S(1)} %bitcast.82, bf16[2,16,256,128]{3,2,1,0:T(8,128)(2,1)} %bitcast.87), custom_call_target="tpu_custom_call" | custom-call | flops 536870912 | bytes 3145728 | tf_op jit(solution)/shard_map/even_product/pallas_call | solution.py:154
  264.7 4.2 %all-to-all-start.7 = ((bf16[8,256,128]{2,1,0:T(8,128)(2,1)}), bf16[8,256,128]{2,1,0:T(8,128)(2,1)}, u32[]{:S(2)}, u32[]{:S(2)}) async-start(bf16[8,256,128]{2,1,0:T(8,128)(2,1)} %even_product.9), calls=%async_computation.7 | async-start | bytes 1048576 | tf_op jit(solution)/shard_map/all_to_all | solution.py:244
  269.9 1.3 collective-permute-start.36
  271.2 5.4 %collective-permute-done.36 = f32[256,128]{1,0:T(8,128)S(1)} collective-permute-done((f32[256,128]{1,0:T(8,128)S(1)}, f32[256,128]{1,0:T(8,128)S(1)}, u32[]{:S(2)}, u32[]{:S(2)}) %collective-permute-start.36) | collective-permute-done | bytes 131104 | tf_op jit(solution)/shard_map/ppermute | solution.py:44
  (103 shorter events, 30.8 us)
Async XLA Ops:
  0.6 17.6 %copy-start.2 = (s32[2,1,4,4]{3,2,1,0:T(4,128)S(1)}, s32[2,1,4,4]{3,2,1,0:T(4,128)}, u32[]{:S(2)}) copy-start(s32[2,1,4,4]{3,2,1,0:T(4,128)} %ranks.16) | copy-start | bytes 388
  2.6 15.5 %all-to-all-start = ((bf16[8,256,128]{2,1,0:T(8,128)(2,1)}), bf16[8,256,128]{2,1,0:T(8,128)(2,1)S(1)}, u32[]{:S(2)}, u32[]{:S(2)}) async-start(bf16[8,256,128]{2,1,0:T(8,128)(2,1)} %broadcast_in_dim.126), calls=%async_computation | async-start | bytes 1048576 | tf_op jit(solution)/shard_map/all_to_all | solution.py:249
  18.2 6.3 %copy-start.3 = (f32[2,1,2,128,128]{4,3,2,1,0:T(8,128)S(1)}, f32[2,1,2,128,128]{4,3,2,1,0:T(8,128)}, u32[]{:S(2)}) copy-start(f32[2,1,2,128,128]{4,3,2,1,0:T(8,128)} %param.15) | copy-start | bytes 786436
  22.6 3.1 %collective-permute-start = (bf16[4,256,128]{2,1,0:T(8,128)(2,1)S(1)}, bf16[4,256,128]{2,1,0:T(8,128)(2,1)S(1)}, u32[]{:S(2)}, u32[]{:S(2)}) collective-permute-start(bf16[4,256,128]{2,1,0:T(8,128)(2,1)S(1)} %get-tuple-element.11), channel_id=1, source_target_pairs={{0,8},{1,9},{2,10},{3,11},{4,12},{5,13},{6,14},{7,15},{8,0},{9,1},... | collective-permute-start | bytes 786440 | tf_op jit(solution)/shard_map/ppermute | solution.py:44
  25.8 30.8 %copy-start = (bf16[2,1,4,4,256,128]{5,4,3,2,1,0:T(8,128)(2,1)S(1)}, bf16[2,1,4,4,256,128]{5,4,3,2,1,0:T(8,128)(2,1)}, u32[]{:S(2)}) copy-start(bf16[2,1,4,4,256,128]{5,4,3,2,1,0:T(8,128)(2,1)} %param.9) | copy-start | bytes 6291460
  25.8 30.8 %copy-start.1 = (s32[2,1,4,4]{3,2,1,0:T(4,128)S(1)}, s32[2,1,4,4]{3,2,1,0:T(4,128)}, u32[]{:S(2)}) copy-start(s32[2,1,4,4]{3,2,1,0:T(4,128)} %ranks.17) | copy-start | bytes 388
  25.9 9.6 %collective-permute-start.1 = (bf16[2,256,128]{2,1,0:T(8,128)(2,1)S(1)}, bf16[2,256,128]{2,1,0:T(8,128)(2,1)S(1)}, u32[]{:S(2)}, u32[]{:S(2)}) collective-permute-start(bf16[2,256,128]{2,1,0:T(8,128)(2,1)S(1)} %get-tuple-element.47), channel_id=1, source_target_pairs={{0,16},{1,17},{2,18},{3,19},{4,20},{5,21},{6,22},{7,23},{8,24},{9,... | collective-permute-start | bytes 393224 | tf_op jit(solution)/shard_map/ppermute | solution.py:44
  28.9 7.9 %collective-permute-start.4 = (bf16[2,256,128]{2,1,0:T(8,128)(2,1)S(1)}, bf16[2,256,128]{2,1,0:T(8,128)(2,1)S(1)}, u32[]{:S(2)}, u32[]{:S(2)}) collective-permute-start(bf16[2,256,128]{2,1,0:T(8,128)(2,1)S(1)} %get-tuple-element.48), channel_id=1, source_target_pairs={{0,48},{1,49},{2,50},{3,51},{4,52},{5,53},{6,54},{7,55},{8,56},{9,... | collective-permute-start | bytes 393224 | tf_op jit(solution)/shard_map/ppermute | solution.py:44
  36.9 9.8 %collective-permute-start.2 = (bf16[2,256,128]{2,1,0:T(8,128)(2,1)S(1)}, bf16[2,256,128]{2,1,0:T(8,128)(2,1)S(1)}, u32[]{:S(2)}, u32[]{:S(2)}) collective-permute-start(bf16[2,256,128]{2,1,0:T(8,128)(2,1)S(1)} %get-tuple-element.45), channel_id=1, source_target_pairs={{0,112},{1,113},{2,114},{3,115},{4,116},{5,117},{6,118},{7,119},{8... | collective-permute-start | bytes 393224 | tf_op jit(solution)/shard_map/ppermute | solution.py:44
  41.8 5.9 %collective-permute-start.3 = (bf16[2,256,128]{2,1,0:T(8,128)(2,1)S(1)}, bf16[2,256,128]{2,1,0:T(8,128)(2,1)S(1)}, u32[]{:S(2)}, u32[]{:S(2)}) collective-permute-start(bf16[2,256,128]{2,1,0:T(8,128)(2,1)S(1)} %get-tuple-element.45), channel_id=1, source_target_pairs={{0,64},{1,65},{2,66},{3,67},{4,68},{5,69},{6,70},{7,71},{8,72},{9,... | collective-permute-start | bytes 393224 | tf_op jit(solution)/shard_map/ppermute | solution.py:44
  43.1 4.6 %collective-permute-start.5 = (bf16[2,256,128]{2,1,0:T(8,128)(2,1)S(1)}, bf16[2,256,128]{2,1,0:T(8,128)(2,1)S(1)}, u32[]{:S(2)}, u32[]{:S(2)}) collective-permute-start(bf16[2,256,128]{2,1,0:T(8,128)(2,1)S(1)} %get-tuple-element.46), channel_id=1, source_target_pairs={{0,80},{1,81},{2,82},{3,83},{4,84},{5,85},{6,86},{7,87},{8,88},{9,... | collective-permute-start | bytes 393224 | tf_op jit(solution)/shard_map/ppermute | solution.py:44
  45.4 6.1 %collective-permute-start.6 = (bf16[2,256,128]{2,1,0:T(8,128)(2,1)S(1)}, bf16[2,256,128]{2,1,0:T(8,128)(2,1)S(1)}, u32[]{:S(2)}, u32[]{:S(2)}) collective-permute-start(bf16[2,256,128]{2,1,0:T(8,128)(2,1)S(1)} %get-tuple-element.46), channel_id=1, source_target_pairs={{0,64},{1,65},{2,66},{3,67},{4,68},{5,69},{6,70},{7,71},{8,72},{9,... | collective-permute-start | bytes 393224 | tf_op jit(solution)/shard_map/ppermute | solution.py:44
  51.7 4.9 %collective-permute-start.7 = (bf16[4,256,128]{2,1,0:T(8,128)(2,1)S(1)}, bf16[4,256,128]{2,1,0:T(8,128)(2,1)S(1)}, u32[]{:S(2)}, u32[]{:S(2)}) collective-permute-start(bf16[4,256,128]{2,1,0:T(8,128)(2,1)S(1)} %fusion.4.refs_0_), channel_id=1, source_target_pairs={{0,8},{1,9},{2,10},{3,11},{4,12},{5,13},{6,14},{7,15},{8,0},{9,1},... | collective-permute-start | bytes 786440 | tf_op jit(solution)/shard_map/ppermute | solution.py:44
  72.4 0.7 collective-permute-start.8
  89.1 3.6 %collective-permute-start.9 = (bf16[4,256,128]{2,1,0:T(8,128)(2,1)S(1)}, bf16[4,256,128]{2,1,0:T(8,128)(2,1)S(1)}, u32[]{:S(2)}, u32[]{:S(2)}) collective-permute-start(bf16[4,256,128]{2,1,0:T(8,128)(2,1)S(1)} %get-tuple-element.13), channel_id=1, source_target_pairs={{0,8},{1,9},{2,10},{3,11},{4,12},{5,13},{6,14},{7,15},{8,0},{9,1},... | collective-permute-start | bytes 786440 | tf_op jit(solution)/shard_map/ppermute | solution.py:44
  92.8 9.0 %collective-permute-start.10 = (bf16[2,256,128]{2,1,0:T(8,128)(2,1)S(1)}, bf16[2,256,128]{2,1,0:T(8,128)(2,1)S(1)}, u32[]{:S(2)}, u32[]{:S(2)}) collective-permute-start(bf16[2,256,128]{2,1,0:T(8,128)(2,1)S(1)} %get-tuple-element.41), channel_id=1, source_target_pairs={{0,16},{1,17},{2,18},{3,19},{4,20},{5,21},{6,22},{7,23},{8,24},{9,... | collective-permute-start | bytes 393224 | tf_op jit(solution)/shard_map/ppermute | solution.py:44
  95.2 8.9 %collective-permute-start.13 = (bf16[2,256,128]{2,1,0:T(8,128)(2,1)S(1)}, bf16[2,256,128]{2,1,0:T(8,128)(2,1)S(1)}, u32[]{:S(2)}, u32[]{:S(2)}) collective-permute-start(bf16[2,256,128]{2,1,0:T(8,128)(2,1)S(1)} %get-tuple-element.42), channel_id=1, source_target_pairs={{0,48},{1,49},{2,50},{3,51},{4,52},{5,53},{6,54},{7,55},{8,56},{9,... | collective-permute-start | bytes 393224 | tf_op jit(solution)/shard_map/ppermute | solution.py:44
  104.1 3.4 %collective-permute-start.11 = (bf16[2,256,128]{2,1,0:T(8,128)(2,1)S(1)}, bf16[2,256,128]{2,1,0:T(8,128)(2,1)S(1)}, u32[]{:S(2)}, u32[]{:S(2)}) collective-permute-start(bf16[2,256,128]{2,1,0:T(8,128)(2,1)S(1)} %get-tuple-element.39), channel_id=1, source_target_pairs={{64,176},{65,177},{66,178},{67,179},{68,180},{69,181},{70,182},{71... | collective-permute-start | bytes 393224 | tf_op jit(solution)/shard_map/ppermute | solution.py:44
  104.8 3.4 %collective-permute-start.12 = (bf16[2,256,128]{2,1,0:T(8,128)(2,1)S(1)}, bf16[2,256,128]{2,1,0:T(8,128)(2,1)S(1)}, u32[]{:S(2)}, u32[]{:S(2)}) collective-permute-start(bf16[2,256,128]{2,1,0:T(8,128)(2,1)S(1)} %get-tuple-element.39), channel_id=1, source_target_pairs={{64,128},{65,129},{66,130},{67,131},{68,132},{69,133},{70,134},{71... | collective-permute-start | bytes 393224 | tf_op jit(solution)/shard_map/ppermute | solution.py:44
  105.5 2.8 collective-permute-start.14
  106.2 2.1 collective-permute-start.15
  106.8 2.8 %collective-permute-start.17 = (bf16[2,256,128]{2,1,0:T(8,128)(2,1)S(1)}, bf16[2,256,128]{2,1,0:T(8,128)(2,1)S(1)}, u32[]{:S(2)}, u32[]{:S(2)}) collective-permute-start(bf16[2,256,128]{2,1,0:T(8,128)(2,1)S(1)} %get-tuple-element.39), channel_id=1, source_target_pairs={{128,176},{129,177},{130,178},{131,179},{132,180},{133,181},{134,1... | collective-permute-start | bytes 393224 | tf_op jit(solution)/shard_map/ppermute | solution.py:44
  107.5 2.2 collective-permute-start.18
  108.3 2.5 collective-permute-start.16
  109.8 3.4 %collective-permute-start.19 = (bf16[4,256,128]{2,1,0:T(8,128)(2,1)S(1)}, bf16[4,256,128]{2,1,0:T(8,128)(2,1)S(1)}, u32[]{:S(2)}, u32[]{:S(2)}) collective-permute-start(bf16[4,256,128]{2,1,0:T(8,128)(2,1)S(1)} %fusion.2.refs_0_), channel_id=1, source_target_pairs={{0,8},{1,9},{2,10},{3,11},{4,12},{5,13},{6,14},{7,15},{8,0},{9,1},... | collective-permute-start | bytes 786440 | tf_op jit(solution)/shard_map/ppermute | solution.py:44
  133.6 0.7 collective-permute-start.20
  150.3 3.6 %collective-permute-start.21 = (bf16[4,256,128]{2,1,0:T(8,128)(2,1)S(1)}, bf16[4,256,128]{2,1,0:T(8,128)(2,1)S(1)}, u32[]{:S(2)}, u32[]{:S(2)}) collective-permute-start(bf16[4,256,128]{2,1,0:T(8,128)(2,1)S(1)} %get-tuple-element.15), channel_id=1, source_target_pairs={{0,8},{1,9},{2,10},{3,11},{4,12},{5,13},{6,14},{7,15},{8,0},{9,1},... | collective-permute-start | bytes 786440 | tf_op jit(solution)/shard_map/ppermute | solution.py:44
  154.1 8.9 %collective-permute-start.22 = (bf16[2,256,128]{2,1,0:T(8,128)(2,1)S(1)}, bf16[2,256,128]{2,1,0:T(8,128)(2,1)S(1)}, u32[]{:S(2)}, u32[]{:S(2)}) collective-permute-start(bf16[2,256,128]{2,1,0:T(8,128)(2,1)S(1)} %get-tuple-element.35), channel_id=1, source_target_pairs={{0,16},{1,17},{2,18},{3,19},{4,20},{5,21},{6,22},{7,23},{8,24},{9,... | collective-permute-start | bytes 393224 | tf_op jit(solution)/shard_map/ppermute | solution.py:44
  154.2 9.0 %collective-permute-start.25 = (bf16[2,256,128]{2,1,0:T(8,128)(2,1)S(1)}, bf16[2,256,128]{2,1,0:T(8,128)(2,1)S(1)}, u32[]{:S(2)}, u32[]{:S(2)}) collective-permute-start(bf16[2,256,128]{2,1,0:T(8,128)(2,1)S(1)} %get-tuple-element.36), channel_id=1, source_target_pairs={{0,48},{1,49},{2,50},{3,51},{4,52},{5,53},{6,54},{7,55},{8,56},{9,... | collective-permute-start | bytes 393224 | tf_op jit(solution)/shard_map/ppermute | solution.py:44
  163.3 2.7 collective-permute-start.23
  163.9 2.0 collective-permute-start.24
  164.6 1.4 collective-permute-start.26
  165.3 0.7 collective-permute-start.27
  166.2 2.5 collective-permute-start.28
  183.0 36.7 %collective-permute-start.29 = (bf16[256,128]{1,0:T(8,128)(2,1)S(1)}, bf16[256,128]{1,0:T(8,128)(2,1)S(1)}, u32[]{:S(2)}, u32[]{:S(2)}) collective-permute-start(bf16[256,128]{1,0:T(8,128)(2,1)S(1)} %fusion.21), channel_id=1, source_target_pairs={{64,0},{65,1},{66,2},{67,3},{68,4},{69,5},{70,6},{71,7},{72,8},{73... | collective-permute-start | bytes 196616 | tf_op jit(solution)/shard_map/ppermute | solution.py:44
  234.5 4.3 %collective-permute-start.30 = (bf16[4,256,128]{2,1,0:T(8,128)(2,1)S(1)}, bf16[4,256,128]{2,1,0:T(8,128)(2,1)S(1)}, u32[]{:S(2)}, u32[]{:S(2)}) collective-permute-start(bf16[4,256,128]{2,1,0:T(8,128)(2,1)S(1)} %get-tuple-element.17), channel_id=1, source_target_pairs={{0,8},{1,9},{2,10},{3,11},{4,12},{5,13},{6,14},{7,15},{8,0},{9,1},... | collective-permute-start | bytes 786440 | tf_op jit(solution)/shard_map/ppermute | solution.py:44
  239.0 9.2 %collective-permute-start.31 = (bf16[2,256,128]{2,1,0:T(8,128)(2,1)S(1)}, bf16[2,256,128]{2,1,0:T(8,128)(2,1)S(1)}, u32[]{:S(2)}, u32[]{:S(2)}) collective-permute-start(bf16[2,256,128]{2,1,0:T(8,128)(2,1)S(1)} %get-tuple-element.29), channel_id=1, source_target_pairs={{0,16},{1,17},{2,18},{3,19},{4,20},{5,21},{6,22},{7,23},{8,24},{9,... | collective-permute-start | bytes 393224 | tf_op jit(solution)/shard_map/ppermute | solution.py:44
  240.3 7.9 %collective-permute-start.33 = (bf16[2,256,128]{2,1,0:T(8,128)(2,1)S(1)}, bf16[2,256,128]{2,1,0:T(8,128)(2,1)S(1)}, u32[]{:S(2)}, u32[]{:S(2)}) collective-permute-start(bf16[2,256,128]{2,1,0:T(8,128)(2,1)S(1)} %get-tuple-element.30), channel_id=1, source_target_pairs={{0,48},{1,49},{2,50},{3,51},{4,52},{5,53},{6,54},{7,55},{8,56},{9,... | collective-permute-start | bytes 393224 | tf_op jit(solution)/shard_map/ppermute | solution.py:44
  248.2 7.6 %collective-permute-start.32 = (bf16[2,256,128]{2,1,0:T(8,128)(2,1)S(1)}, bf16[2,256,128]{2,1,0:T(8,128)(2,1)S(1)}, u32[]{:S(2)}, u32[]{:S(2)}) collective-permute-start(bf16[2,256,128]{2,1,0:T(8,128)(2,1)S(1)} %get-tuple-element.27), channel_id=1, source_target_pairs={{0,48},{1,49},{2,50},{3,51},{4,52},{5,53},{6,54},{7,55},{8,56},{9,... | collective-permute-start | bytes 393224 | tf_op jit(solution)/shard_map/ppermute | solution.py:44
  251.6 7.3 %collective-permute-start.34 = (bf16[2,256,128]{2,1,0:T(8,128)(2,1)S(1)}, bf16[2,256,128]{2,1,0:T(8,128)(2,1)S(1)}, u32[]{:S(2)}, u32[]{:S(2)}) collective-permute-start(bf16[2,256,128]{2,1,0:T(8,128)(2,1)S(1)} %get-tuple-element.28), channel_id=1, source_target_pairs={{0,16},{1,17},{2,18},{3,19},{4,20},{5,21},{6,22},{7,23},{8,24},{9,... | collective-permute-start | bytes 393224 | tf_op jit(solution)/shard_map/ppermute | solution.py:44
  259.1 2.4 collective-permute-start.35
  264.7 13.7 %all-to-all-start.7 = ((bf16[8,256,128]{2,1,0:T(8,128)(2,1)}), bf16[8,256,128]{2,1,0:T(8,128)(2,1)}, u32[]{:S(2)}, u32[]{:S(2)}) async-start(bf16[8,256,128]{2,1,0:T(8,128)(2,1)} %even_product.9), calls=%async_computation.7 | async-start | bytes 1048576 | tf_op jit(solution)/shard_map/all_to_all | solution.py:244
  269.9 6.7 %collective-permute-start.36 = (f32[256,128]{1,0:T(8,128)S(1)}, f32[256,128]{1,0:T(8,128)S(1)}, u32[]{:S(2)}, u32[]{:S(2)}) collective-permute-start(f32[256,128]{1,0:T(8,128)S(1)} %select_add_fusion.8), channel_id=1, source_target_pairs={{64,0},{65,1},{66,2},{67,3},{68,4},{69,5},{70,6},{71,7},{72,8},{73... | collective-permute-start | bytes 393224 | tf_op jit(solution)/shard_map/ppermute | solution.py:44

commit v5 on v4

--- a/solution.py
+++ b/solution.py
@@ -53,19 +53,15 @@
     direction = choose if isinstance(choose, int) else (section == choose[0]).astype(jnp.int32)
 
     def piece(index):
-        source, kept = ((left, lefts), (right, rights))[index // 2]
-        start, size = index % 2 * 8, 8
-        return pltpu.make_async_copy(
-            source.at[direction, pl.ds(start, size)], kept.at[pl.ds(start, size)], sems.at[index]
-        )
-
-    if odd:
-        piece(2).start()
-        piece(3).start()
-    else:
+        source, kept = ((left, lefts), (right, rights))[index // 4]
+        size = 4 if odd else 8
+        tiles = pl.ds(index % 4 * size, size)
+        return pltpu.make_async_copy(source.at[direction, tiles], kept.at[tiles], sems.at[index])
+
+    if not odd:
         rights = None
-        piece(0).start()
-        piece(1).start()
+    for index in (4, 5, 6, 7, 0, 1, 2, 3) if odd else (0, 1):
+        piece(index).start()
 
     for chunk in range(8):
         lanes = slice(chunk % 2 * 128, chunk % 2 * 128 + 128)
@@ -86,8 +82,8 @@
     sign = jnp.where(lane < 64, 1.0, -1.0)
     for a_pair in range(2):
         if odd:
-            piece(2 + a_pair).wait()
-            piece(a_pair).start()
+            piece(4 + a_pair * 2).wait()
+            piece(5 + a_pair * 2).wait()
         for c in range(4):
             tiles = (a_pair * 8 + c, a_pair * 8 + 4 + c)
             joined = jnp.concatenate([rights[tile] if odd else right[direction, tile] for tile in tiles], axis=1)
@@ -105,8 +101,8 @@
                     value = part[imag] + turned[real]
                     stacked[a_pair * 2 + side, imag, lanes] = value.astype(BF)
     for a in range(4):
-        if a % 2 == 0:
-            piece(a // 2).wait()
+        if odd or a % 2 == 0:
+            piece(a if odd else a // 2).wait()
         total = None
         for c_pair in range(2):
             joined = jnp.concatenate(
@@ -161,7 +157,7 @@
             pltpu.VMEM((4, 256, 512), BF),
         ]
         + [pltpu.VMEM((16, 256, 128), BF)] * (2 if odd else 1)
-        + [pltpu.SemaphoreType.DMA((4,))],
+        + [pltpu.SemaphoreType.DMA((8,))],
         compiler_params=pltpu.CompilerParams(vmem_limit_bytes=20 * 2**20),
         cost_estimate=pl.CostEstimate(
             flops=16 * 2 * 256**3, bytes_accessed=3 * 2**20, transcendentals=0

time: 282 us -> 280 us (level)
  transfers between devices with their start and end apart: 39 -> 39, of which waited for: 23 -> 22; matrix products, arithmetic and copies ran while one was open for 1% -> 1% of each run, Pallas kernels for 1% -> 1%
where the time goes in v5:
time: 280 us; the launch traced here: 279 us
  waiting for transfers between devices  97.1 us (35%)
  blocking collectives  75.9 us (27%)
  starting transfers between devices  66.9 us (24%)
  Pallas kernels  29.1 us (10%)
  other arithmetic  5.07 us (2%)
  local copies, waits for them, and re-layouts  3.98 us (1%)
    ppermute x37, waiting for transfers between devices, send(): return lax.ppermute(value, AXES, pairs)  87.9 us
    ppermute x37, starting transfers between devices, send(): return lax.ppermute(value, AXES, pairs)  56.4 us
    all_to_all x3, blocking collectives, col_spread(): return lax.all_to_all(value, 'col', 0, 0, tiled=True)  33.5 us
    pallas_call x9, Pallas kernels, product(): pl.pallas_call(functools.partial(product_kernel, odd, choose), out_shape=...  29.1 us
    all_to_all x2, blocking collectives, col_sum(): terms = lax.all_to_all(terms, 'col', 0, 0, tiled=True)  25.1 us
    all_to_all x1, blocking collectives, on_device(): lax.all_to_all(jnp.concatenate(terms, axis=1), 'col', 0, 0, tiled=True)  17.3 us
    all_to_all x1, waiting for transfers between devices, col_spread(): return lax.all_to_all(value, 'col', 0, 0, tiled=True)  9.17 us
    all_to_all x1, starting transfers between devices, col_spread(): return lax.all_to_all(value, 'col', 0, 0, tiled=True)  6.37 us
  transfers between devices with their start and end apart: 39, of which 22 were waited for; matrix products, arithmetic and copies ran while one was open for 1% of the time, Pallas kernels for 1%

profile of v5, /device:TPU:1, one launch (start us, length us, event | category | flops | bytes accessed | tf_op | source)
XLA Modules:
  0.0 279.4 jit_solution(14397448694992428635)
XLA Ops:
  2.6 6.4 %all-to-all-start = ((bf16[8,256,128]{2,1,0:T(8,128)(2,1)}), bf16[8,256,128]{2,1,0:T(8,128)(2,1)S(1)}, u32[]{:S(2)}, u32[]{:S(2)}) async-start(bf16[8,256,128]{2,1,0:T(8,128)(2,1)} %broadcast_in_dim.126), calls=%async_computation | async-start | bytes 1048576 | tf_op jit(solution)/shard_map/all_to_all | solution.py:245
  9.0 9.2 %all-to-all-done.refs_0_ = bf16[8,256,128]{2,1,0:T(8,128)(2,1)S(1)} async-done(((bf16[8,256,128]{2,1,0:T(8,128)(2,1)}), bf16[8,256,128]{2,1,0:T(8,128)(2,1)S(1)}, u32[]{:S(2)}, u32[]{:S(2)}) %all-to-all-start) | async-done | bytes 524320 | tf_op jit(solution)/shard_map/all_to_all | solution.py:245
  18.2 4.1 %odd_product.4 = (f32[4,256,128]{2,1,0:T(8,128)S(1)}, bf16[4,256,128]{2,1,0:T(8,128)(2,1)S(1)}) custom-call(s32[2,1,4,4]{3,2,1,0:T(4,128)S(1)} %copy-done.2, bf16[8,256,128]{2,1,0:T(8,128)(2,1)S(1)} %all-to-all-done.refs_0_, bf16[2,16,256,128]{3,2,1,0:T(8,128)(2,1)} %bitcast.88, bf16[2,16,256,128]{3,2,1,0:T(8,128)(2,1)} %bitcast.92), custom_call_target="tpu_custom_call" | custom-call | flops 536870912 | bytes 3145728 | tf_op jit(solution)/shard_map/odd_product/pallas_call | solution.py:150
  22.3 1.9 collective-permute-start
  25.5 3.1 %collective-permute-start.1 = (bf16[2,256,128]{2,1,0:T(8,128)(2,1)S(1)}, bf16[2,256,128]{2,1,0:T(8,128)(2,1)S(1)}, u32[]{:S(2)}, u32[]{:S(2)}) collective-permute-start(bf16[2,256,128]{2,1,0:T(8,128)(2,1)S(1)} %get-tuple-element.47), channel_id=1, source_target_pairs={{0,16},{1,17},{2,18},{3,19},{4,20},{5,21},{6,22},{7,23},{8,24},{9,... | collective-permute-start | bytes 393224 | tf_op jit(solution)/shard_map/ppermute | solution.py:44
  28.6 3.3 %collective-permute-start.4 = (bf16[2,256,128]{2,1,0:T(8,128)(2,1)S(1)}, bf16[2,256,128]{2,1,0:T(8,128)(2,1)S(1)}, u32[]{:S(2)}, u32[]{:S(2)}) collective-permute-start(bf16[2,256,128]{2,1,0:T(8,128)(2,1)S(1)} %get-tuple-element.48), channel_id=1, source_target_pairs={{0,48},{1,49},{2,50},{3,51},{4,52},{5,53},{6,54},{7,55},{8,56},{9,... | collective-permute-start | bytes 393224 | tf_op jit(solution)/shard_map/ppermute | solution.py:44
  31.9 3.2 %collective-permute-done.1 = bf16[2,256,128]{2,1,0:T(8,128)(2,1)S(1)} collective-permute-done((bf16[2,256,128]{2,1,0:T(8,128)(2,1)S(1)}, bf16[2,256,128]{2,1,0:T(8,128)(2,1)S(1)}, u32[]{:S(2)}, u32[]{:S(2)}) %collective-permute-start.1) | collective-permute-done | bytes 131104 | tf_op jit(solution)/shard_map/ppermute | solution.py:44
  35.1 1.4 collective-permute-done.4
  36.6 4.9 %collective-permute-start.2 = (bf16[2,256,128]{2,1,0:T(8,128)(2,1)S(1)}, bf16[2,256,128]{2,1,0:T(8,128)(2,1)S(1)}, u32[]{:S(2)}, u32[]{:S(2)}) collective-permute-start(bf16[2,256,128]{2,1,0:T(8,128)(2,1)S(1)} %get-tuple-element.45), channel_id=1, source_target_pairs={{0,112},{1,113},{2,114},{3,115},{4,116},{5,117},{6,118},{7,119},{8... | collective-permute-start | bytes 393224 | tf_op jit(solution)/shard_map/ppermute | solution.py:44
  41.5 1.3 collective-permute-start.3
  42.8 2.3 collective-permute-start.5
  45.1 1.3 collective-permute-start.6
  47.4 3.8 %collective-permute-done.6 = bf16[2,256,128]{2,1,0:T(8,128)(2,1)S(1)} collective-permute-done((bf16[2,256,128]{2,1,0:T(8,128)(2,1)S(1)}, bf16[2,256,128]{2,1,0:T(8,128)(2,1)S(1)}, u32[]{:S(2)}, u32[]{:S(2)}) %collective-permute-start.6) | collective-permute-done | bytes 131104 | tf_op jit(solution)/shard_map/ppermute | solution.py:44
  51.3 3.7 %collective-permute-start.7 = (bf16[4,256,128]{2,1,0:T(8,128)(2,1)S(1)}, bf16[4,256,128]{2,1,0:T(8,128)(2,1)S(1)}, u32[]{:S(2)}, u32[]{:S(2)}) collective-permute-start(bf16[4,256,128]{2,1,0:T(8,128)(2,1)S(1)} %fusion.4.refs_0_), channel_id=1, source_target_pairs={{0,8},{1,9},{2,10},{3,11},{4,12},{5,13},{6,14},{7,15},{8,0},{9,1},... | collective-permute-start | bytes 786440 | tf_op jit(solution)/shard_map/ppermute | solution.py:44
  56.2 2.4 even_product.5
  58.7 13.3 %all_to_all.40 = bf16[8,256,128]{2,1,0:T(8,128)(2,1)S(1)} all-to-all(bf16[8,256,128]{2,1,0:T(8,128)(2,1)S(1)} %even_product.5), channel_id=1, replica_groups=mesh['layer'=4,'row'=8,'col'=8] {'col'}, dimensions={0} | all-to-all | bytes 1048576 | tf_op jit(solution)/shard_map/all_to_all | solution.py:240
  72.8 11.6 %all_to_all.41.refs_0_ = bf16[8,256,128]{2,1,0:T(8,128)(2,1)S(1)} all-to-all(bf16[8,256,128]{2,1,0:T(8,128)(2,1)S(1)} %broadcast_in_dim.129), channel_id=1, replica_groups=mesh['layer'=4,'row'=8,'col'=8] {'col'}, dimensions={0} | all-to-all | bytes 1048576 | tf_op jit(solution)/shard_map/all_to_all | solution.py:245
  84.4 4.1 %odd_product.5 = (f32[4,256,128]{2,1,0:T(8,128)S(1)}, bf16[4,256,128]{2,1,0:T(8,128)(2,1)S(1)}) custom-call(s32[2,1,4,4]{3,2,1,0:T(4,128)S(1)} %copy-done.2, bf16[8,256,128]{2,1,0:T(8,128)(2,1)S(1)} %all_to_all.41.refs_0_, bf16[2,16,256,128]{3,2,1,0:T(8,128)(2,1)} %bitcast.89, bf16[2,16,256,128]{3,2,1,0:T(8,128)(2,1)} %bitcast.93), custom_call_target="tpu_custom_call" | custom-call | flops 536870912 | bytes 3145728 | tf_op jit(solution)/shard_map/odd_product/pallas_call | solution.py:150
  88.5 2.4 collective-permute-start.9
  92.2 2.3 collective-permute-start.10
  95.4 5.8 %collective-permute-done.10 = bf16[2,256,128]{2,1,0:T(8,128)(2,1)S(1)} collective-permute-done((bf16[2,256,128]{2,1,0:T(8,128)(2,1)S(1)}, bf16[2,256,128]{2,1,0:T(8,128)(2,1)S(1)}, u32[]{:S(2)}, u32[]{:S(2)}) %collective-permute-start.10) | collective-permute-done | bytes 131104 | tf_op jit(solution)/shard_map/ppermute | solution.py:44
  101.2 2.2 collective-permute-done.13
  107.7 1.3 collective-permute-start.16
  110.2 2.4 even_product.6
  112.6 2.4 even_product.7
  115.1 17.3 %all_to_all.42 = bf16[8,512,128]{2,1,0:T(8,128)(2,1)S(1)} all-to-all(bf16[8,512,128]{2,1,0:T(8,128)(2,1)S(1)} %pad_maximum_fusion), channel_id=1, replica_groups=mesh['layer'=4,'row'=8,'col'=8] {'col'}, dimensions={0} | all-to-all | bytes 2097152 | tf_op jit(solution)/shard_map/all_to_all | solution.py:265
  133.4 11.6 %all_to_all.43.refs_0_ = bf16[8,256,128]{2,1,0:T(8,128)(2,1)S(1)} all-to-all(bf16[8,256,128]{2,1,0:T(8,128)(2,1)S(1)} %broadcast_in_dim.131), channel_id=1, replica_groups=mesh['layer'=4,'row'=8,'col'=8] {'col'}, dimensions={0} | all-to-all | bytes 1048576 | tf_op jit(solution)/shard_map/all_to_all | solution.py:245
  145.0 4.1 %odd_product.6 = (f32[4,256,128]{2,1,0:T(8,128)S(1)}, bf16[4,256,128]{2,1,0:T(8,128)(2,1)S(1)}) custom-call(s32[2,1,4,4]{3,2,1,0:T(4,128)S(1)} %copy-done.2, bf16[8,256,128]{2,1,0:T(8,128)(2,1)S(1)} %all_to_all.43.refs_0_, bf16[2,16,256,128]{3,2,1,0:T(8,128)(2,1)} %bitcast.90, bf16[2,16,256,128]{3,2,1,0:T(8,128)(2,1)} %bitcast.94), custom_call_target="tpu_custom_call" | custom-call | flops 536870912 | bytes 3145728 | tf_op jit(solution)/shard_map/odd_product/pallas_call | solution.py:150
  149.1 2.3 collective-permute-start.21
  153.1 1.9 collective-permute-start.25
  155.0 6.7 %collective-permute-done.22 = bf16[2,256,128]{2,1,0:T(8,128)(2,1)S(1)} collective-permute-done((bf16[2,256,128]{2,1,0:T(8,128)(2,1)S(1)}, bf16[2,256,128]{2,1,0:T(8,128)(2,1)S(1)}, u32[]{:S(2)}, u32[]{:S(2)}) %collective-permute-start.22) | collective-permute-done | bytes 131104 | tf_op jit(solution)/shard_map/ppermute | solution.py:44
  164.6 1.8 collective-permute-start.28
  167.6 2.4 even_product.8
  170.0 11.8 %all_to_all.44 = bf16[8,256,128]{2,1,0:T(8,128)(2,1)S(1)} all-to-all(bf16[8,256,128]{2,1,0:T(8,128)(2,1)S(1)} %even_product.8), channel_id=1, replica_groups=mesh['layer'=4,'row'=8,'col'=8] {'col'}, dimensions={0} | all-to-all | bytes 1048576 | tf_op jit(solution)/shard_map/all_to_all | solution.py:240
  181.9 1.3 collective-permute-start.29
  183.2 35.8 %collective-permute-done.29 = bf16[256,128]{1,0:T(8,128)(2,1)S(1)} collective-permute-done((bf16[256,128]{1,0:T(8,128)(2,1)S(1)}, bf16[256,128]{1,0:T(8,128)(2,1)S(1)}, u32[]{:S(2)}, u32[]{:S(2)}) %collective-permute-start.29) | collective-permute-done | bytes 65568 | tf_op jit(solution)/shard_map/ppermute | solution.py:44
  219.1 10.3 %all_to_all.45.refs_0_ = bf16[8,256,128]{2,1,0:T(8,128)(2,1)S(1)} all-to-all(bf16[8,256,128]{2,1,0:T(8,128)(2,1)S(1)} %broadcast_in_dim.133), channel_id=1, replica_groups=mesh['layer'=4,'row'=8,'col'=8] {'col'}, dimensions={0} | all-to-all | bytes 1048576 | tf_op jit(solution)/shard_map/all_to_all | solution.py:245
  229.5 4.1 %odd_product.7 = (f32[4,256,128]{2,1,0:T(8,128)S(1)}, bf16[4,256,128]{2,1,0:T(8,128)(2,1)S(1)}) custom-call(s32[2,1,4,4]{3,2,1,0:T(4,128)S(1)} %copy-done.2, bf16[8,256,128]{2,1,0:T(8,128)(2,1)S(1)} %all_to_all.45.refs_0_, bf16[2,16,256,128]{3,2,1,0:T(8,128)(2,1)} %bitcast.91, bf16[2,16,256,128]{3,2,1,0:T(8,128)(2,1)} %bitcast.95), custom_call_target="tpu_custom_call" | custom-call | flops 536870912 | bytes 3145728 | tf_op jit(solution)/shard_map/odd_product/pallas_call | solution.py:150
  233.6 3.1 %collective-permute-start.30 = (bf16[4,256,128]{2,1,0:T(8,128)(2,1)S(1)}, bf16[4,256,128]{2,1,0:T(8,128)(2,1)S(1)}, u32[]{:S(2)}, u32[]{:S(2)}) collective-permute-start(bf16[4,256,128]{2,1,0:T(8,128)(2,1)S(1)} %get-tuple-element.17), channel_id=1, source_target_pairs={{0,8},{1,9},{2,10},{3,11},{4,12},{5,13},{6,14},{7,15},{8,0},{9,1},... | collective-permute-start | bytes 786440 | tf_op jit(solution)/shard_map/ppermute | solution.py:44
  239.2 1.3 collective-permute-start.33
  240.5 6.7 %collective-permute-done.31 = bf16[2,256,128]{2,1,0:T(8,128)(2,1)S(1)} collective-permute-done((bf16[2,256,128]{2,1,0:T(8,128)(2,1)S(1)}, bf16[2,256,128]{2,1,0:T(8,128)(2,1)S(1)}, u32[]{:S(2)}, u32[]{:S(2)}) %collective-permute-start.31) | collective-permute-done | bytes 131104 | tf_op jit(solution)/shard_map/ppermute | solution.py:44
  247.3 3.4 %collective-permute-start.32 = (bf16[2,256,128]{2,1,0:T(8,128)(2,1)S(1)}, bf16[2,256,128]{2,1,0:T(8,128)(2,1)S(1)}, u32[]{:S(2)}, u32[]{:S(2)}) collective-permute-start(bf16[2,256,128]{2,1,0:T(8,128)(2,1)S(1)} %get-tuple-element.27), channel_id=1, source_target_pairs={{0,48},{1,49},{2,50},{3,51},{4,52},{5,53},{6,54},{7,55},{8,56},{9,... | collective-permute-start | bytes 393224 | tf_op jit(solution)/shard_map/ppermute | solution.py:44
  250.7 4.3 %collective-permute-done.32 = bf16[2,256,128]{2,1,0:T(8,128)(2,1)S(1)} collective-permute-done((bf16[2,256,128]{2,1,0:T(8,128)(2,1)S(1)}, bf16[2,256,128]{2,1,0:T(8,128)(2,1)S(1)}, u32[]{:S(2)}, u32[]{:S(2)}) %collective-permute-start.32) | collective-permute-done | bytes 131104 | tf_op jit(solution)/shard_map/ppermute | solution.py:44
  255.0 2.9 %collective-permute-done.34 = bf16[2,256,128]{2,1,0:T(8,128)(2,1)S(1)} collective-permute-done((bf16[2,256,128]{2,1,0:T(8,128)(2,1)S(1)}, bf16[2,256,128]{2,1,0:T(8,128)(2,1)S(1)}, u32[]{:S(2)}, u32[]{:S(2)}) %collective-permute-start.34) | collective-permute-done | bytes 131104 | tf_op jit(solution)/shard_map/ppermute | solution.py:44
  260.5 3.2 %even_product.9 = bf16[8,256,128]{2,1,0:T(8,128)(2,1)} custom-call(s32[2,1,4,4]{3,2,1,0:T(4,128)S(1)} %copy-done.1, bf16[4,256,128]{2,1,0:T(8,128)(2,1)S(1)} %fusion.refs_0_, bf16[4,256,128]{2,1,0:T(8,128)(2,1)S(1)} %collective-permute-done.35.refs_1_, bf16[2,16,256,128]{3,2,1,0:T(8,128)(2,1)S(1)} %bitcast.82, bf16[2,16,256,128]{3,2,1,0:T(8,128)(2,1)} %bitcast.87), custom_call_target="tpu_custom_call" | custom-call | flops 536870912 | bytes 3145728 | tf_op jit(solution)/shard_map/even_product/pallas_call | solution.py:150
  263.7 4.2 %all-to-all-start.7 = ((bf16[8,256,128]{2,1,0:T(8,128)(2,1)}), bf16[8,256,128]{2,1,0:T(8,128)(2,1)}, u32[]{:S(2)}, u32[]{:S(2)}) async-start(bf16[8,256,128]{2,1,0:T(8,128)(2,1)} %even_product.9), calls=%async_computation.7 | async-start | bytes 1048576 | tf_op jit(solution)/shard_map/all_to_all | solution.py:240
  268.9 1.3 collective-permute-start.36
  270.2 5.4 %collective-permute-done.36 = f32[256,128]{1,0:T(8,128)S(1)} collective-permute-done((f32[256,128]{1,0:T(8,128)S(1)}, f32[256,128]{1,0:T(8,128)S(1)}, u32[]{:S(2)}, u32[]{:S(2)}) %collective-permute-start.36) | collective-permute-done | bytes 131104 | tf_op jit(solution)/shard_map/ppermute | solution.py:44
  (103 shorter events, 30.9 us)
Async XLA Ops:
  0.6 17.6 %copy-start.2 = (s32[2,1,4,4]{3,2,1,0:T(4,128)S(1)}, s32[2,1,4,4]{3,2,1,0:T(4,128)}, u32[]{:S(2)}) copy-start(s32[2,1,4,4]{3,2,1,0:T(4,128)} %ranks.16) | copy-start | bytes 388
  2.6 15.5 %all-to-all-start = ((bf16[8,256,128]{2,1,0:T(8,128)(2,1)}), bf16[8,256,128]{2,1,0:T(8,128)(2,1)S(1)}, u32[]{:S(2)}, u32[]{:S(2)}) async-start(bf16[8,256,128]{2,1,0:T(8,128)(2,1)} %broadcast_in_dim.126), calls=%async_computation | async-start | bytes 1048576 | tf_op jit(solution)/shard_map/all_to_all | solution.py:245
  18.2 6.0 %copy-start.3 = (f32[2,1,2,128,128]{4,3,2,1,0:T(8,128)S(1)}, f32[2,1,2,128,128]{4,3,2,1,0:T(8,128)}, u32[]{:S(2)}) copy-start(f32[2,1,2,128,128]{4,3,2,1,0:T(8,128)} %param.15) | copy-start | bytes 786436
  22.3 3.1 %collective-permute-start = (bf16[4,256,128]{2,1,0:T(8,128)(2,1)S(1)}, bf16[4,256,128]{2,1,0:T(8,128)(2,1)S(1)}, u32[]{:S(2)}, u32[]{:S(2)}) collective-permute-start(bf16[4,256,128]{2,1,0:T(8,128)(2,1)S(1)} %get-tuple-element.11), channel_id=1, source_target_pairs={{0,8},{1,9},{2,10},{3,11},{4,12},{5,13},{6,14},{7,15},{8,0},{9,1},... | collective-permute-start | bytes 786440 | tf_op jit(solution)/shard_map/ppermute | solution.py:44
  25.4 30.8 %copy-start = (bf16[2,1,4,4,256,128]{5,4,3,2,1,0:T(8,128)(2,1)S(1)}, bf16[2,1,4,4,256,128]{5,4,3,2,1,0:T(8,128)(2,1)}, u32[]{:S(2)}) copy-start(bf16[2,1,4,4,256,128]{5,4,3,2,1,0:T(8,128)(2,1)} %param.9) | copy-start | bytes 6291460
  25.5 30.8 %copy-start.1 = (s32[2,1,4,4]{3,2,1,0:T(4,128)S(1)}, s32[2,1,4,4]{3,2,1,0:T(4,128)}, u32[]{:S(2)}) copy-start(s32[2,1,4,4]{3,2,1,0:T(4,128)} %ranks.17) | copy-start | bytes 388
  25.5 9.6 %collective-permute-start.1 = (bf16[2,256,128]{2,1,0:T(8,128)(2,1)S(1)}, bf16[2,256,128]{2,1,0:T(8,128)(2,1)S(1)}, u32[]{:S(2)}, u32[]{:S(2)}) collective-permute-start(bf16[2,256,128]{2,1,0:T(8,128)(2,1)S(1)} %get-tuple-element.47), channel_id=1, source_target_pairs={{0,16},{1,17},{2,18},{3,19},{4,20},{5,21},{6,22},{7,23},{8,24},{9,... | collective-permute-start | bytes 393224 | tf_op jit(solution)/shard_map/ppermute | solution.py:44
  28.6 7.9 %collective-permute-start.4 = (bf16[2,256,128]{2,1,0:T(8,128)(2,1)S(1)}, bf16[2,256,128]{2,1,0:T(8,128)(2,1)S(1)}, u32[]{:S(2)}, u32[]{:S(2)}) collective-permute-start(bf16[2,256,128]{2,1,0:T(8,128)(2,1)S(1)} %get-tuple-element.48), channel_id=1, source_target_pairs={{0,48},{1,49},{2,50},{3,51},{4,52},{5,53},{6,54},{7,55},{8,56},{9,... | collective-permute-start | bytes 393224 | tf_op jit(solution)/shard_map/ppermute | solution.py:44
  36.6 9.8 %collective-permute-start.2 = (bf16[2,256,128]{2,1,0:T(8,128)(2,1)S(1)}, bf16[2,256,128]{2,1,0:T(8,128)(2,1)S(1)}, u32[]{:S(2)}, u32[]{:S(2)}) collective-permute-start(bf16[2,256,128]{2,1,0:T(8,128)(2,1)S(1)} %get-tuple-element.45), channel_id=1, source_target_pairs={{0,112},{1,113},{2,114},{3,115},{4,116},{5,117},{6,118},{7,119},{8... | collective-permute-start | bytes 393224 | tf_op jit(solution)/shard_map/ppermute | solution.py:44
  41.5 5.9 %collective-permute-start.3 = (bf16[2,256,128]{2,1,0:T(8,128)(2,1)S(1)}, bf16[2,256,128]{2,1,0:T(8,128)(2,1)S(1)}, u32[]{:S(2)}, u32[]{:S(2)}) collective-permute-start(bf16[2,256,128]{2,1,0:T(8,128)(2,1)S(1)} %get-tuple-element.45), channel_id=1, source_target_pairs={{0,64},{1,65},{2,66},{3,67},{4,68},{5,69},{6,70},{7,71},{8,72},{9,... | collective-permute-start | bytes 393224 | tf_op jit(solution)/shard_map/ppermute | solution.py:44
  42.8 4.6 %collective-permute-start.5 = (bf16[2,256,128]{2,1,0:T(8,128)(2,1)S(1)}, bf16[2,256,128]{2,1,0:T(8,128)(2,1)S(1)}, u32[]{:S(2)}, u32[]{:S(2)}) collective-permute-start(bf16[2,256,128]{2,1,0:T(8,128)(2,1)S(1)} %get-tuple-element.46), channel_id=1, source_target_pairs={{0,80},{1,81},{2,82},{3,83},{4,84},{5,85},{6,86},{7,87},{8,88},{9,... | collective-permute-start | bytes 393224 | tf_op jit(solution)/shard_map/ppermute | solution.py:44
  45.1 6.1 %collective-permute-start.6 = (bf16[2,256,128]{2,1,0:T(8,128)(2,1)S(1)}, bf16[2,256,128]{2,1,0:T(8,128)(2,1)S(1)}, u32[]{:S(2)}, u32[]{:S(2)}) collective-permute-start(bf16[2,256,128]{2,1,0:T(8,128)(2,1)S(1)} %get-tuple-element.46), channel_id=1, source_target_pairs={{0,64},{1,65},{2,66},{3,67},{4,68},{5,69},{6,70},{7,71},{8,72},{9,... | collective-permute-start | bytes 393224 | tf_op jit(solution)/shard_map/ppermute | solution.py:44
  51.3 4.9 %collective-permute-start.7 = (bf16[4,256,128]{2,1,0:T(8,128)(2,1)S(1)}, bf16[4,256,128]{2,1,0:T(8,128)(2,1)S(1)}, u32[]{:S(2)}, u32[]{:S(2)}) collective-permute-start(bf16[4,256,128]{2,1,0:T(8,128)(2,1)S(1)} %fusion.4.refs_0_), channel_id=1, source_target_pairs={{0,8},{1,9},{2,10},{3,11},{4,12},{5,13},{6,14},{7,15},{8,0},{9,1},... | collective-permute-start | bytes 786440 | tf_op jit(solution)/shard_map/ppermute | solution.py:44
  72.1 0.7 collective-permute-start.8
  88.5 3.6 %collective-permute-start.9 = (bf16[4,256,128]{2,1,0:T(8,128)(2,1)S(1)}, bf16[4,256,128]{2,1,0:T(8,128)(2,1)S(1)}, u32[]{:S(2)}, u32[]{:S(2)}) collective-permute-start(bf16[4,256,128]{2,1,0:T(8,128)(2,1)S(1)} %get-tuple-element.13), channel_id=1, source_target_pairs={{0,8},{1,9},{2,10},{3,11},{4,12},{5,13},{6,14},{7,15},{8,0},{9,1},... | collective-permute-start | bytes 786440 | tf_op jit(solution)/shard_map/ppermute | solution.py:44
  92.2 9.0 %collective-permute-start.10 = (bf16[2,256,128]{2,1,0:T(8,128)(2,1)S(1)}, bf16[2,256,128]{2,1,0:T(8,128)(2,1)S(1)}, u32[]{:S(2)}, u32[]{:S(2)}) collective-permute-start(bf16[2,256,128]{2,1,0:T(8,128)(2,1)S(1)} %get-tuple-element.41), channel_id=1, source_target_pairs={{0,16},{1,17},{2,18},{3,19},{4,20},{5,21},{6,22},{7,23},{8,24},{9,... | collective-permute-start | bytes 393224 | tf_op jit(solution)/shard_map/ppermute | solution.py:44
  94.5 8.9 %collective-permute-start.13 = (bf16[2,256,128]{2,1,0:T(8,128)(2,1)S(1)}, bf16[2,256,128]{2,1,0:T(8,128)(2,1)S(1)}, u32[]{:S(2)}, u32[]{:S(2)}) collective-permute-start(bf16[2,256,128]{2,1,0:T(8,128)(2,1)S(1)} %get-tuple-element.42), channel_id=1, source_target_pairs={{0,48},{1,49},{2,50},{3,51},{4,52},{5,53},{6,54},{7,55},{8,56},{9,... | collective-permute-start | bytes 393224 | tf_op jit(solution)/shard_map/ppermute | solution.py:44
  103.5 3.4 %collective-permute-start.11 = (bf16[2,256,128]{2,1,0:T(8,128)(2,1)S(1)}, bf16[2,256,128]{2,1,0:T(8,128)(2,1)S(1)}, u32[]{:S(2)}, u32[]{:S(2)}) collective-permute-start(bf16[2,256,128]{2,1,0:T(8,128)(2,1)S(1)} %get-tuple-element.39), channel_id=1, source_target_pairs={{64,176},{65,177},{66,178},{67,179},{68,180},{69,181},{70,182},{71... | collective-permute-start | bytes 393224 | tf_op jit(solution)/shard_map/ppermute | solution.py:44
  104.2 3.4 %collective-permute-start.12 = (bf16[2,256,128]{2,1,0:T(8,128)(2,1)S(1)}, bf16[2,256,128]{2,1,0:T(8,128)(2,1)S(1)}, u32[]{:S(2)}, u32[]{:S(2)}) collective-permute-start(bf16[2,256,128]{2,1,0:T(8,128)(2,1)S(1)} %get-tuple-element.39), channel_id=1, source_target_pairs={{64,128},{65,129},{66,130},{67,131},{68,132},{69,133},{70,134},{71... | collective-permute-start | bytes 393224 | tf_op jit(solution)/shard_map/ppermute | solution.py:44
  104.9 2.8 collective-permute-start.14
  105.5 2.1 collective-permute-start.15
  106.2 2.8 %collective-permute-start.17 = (bf16[2,256,128]{2,1,0:T(8,128)(2,1)S(1)}, bf16[2,256,128]{2,1,0:T(8,128)(2,1)S(1)}, u32[]{:S(2)}, u32[]{:S(2)}) collective-permute-start(bf16[2,256,128]{2,1,0:T(8,128)(2,1)S(1)} %get-tuple-element.39), channel_id=1, source_target_pairs={{128,176},{129,177},{130,178},{131,179},{132,180},{133,181},{134,1... | collective-permute-start | bytes 393224 | tf_op jit(solution)/shard_map/ppermute | solution.py:44
  106.9 2.1 collective-permute-start.18
  107.7 2.5 collective-permute-start.16
  109.2 3.4 %collective-permute-start.19 = (bf16[4,256,128]{2,1,0:T(8,128)(2,1)S(1)}, bf16[4,256,128]{2,1,0:T(8,128)(2,1)S(1)}, u32[]{:S(2)}, u32[]{:S(2)}) collective-permute-start(bf16[4,256,128]{2,1,0:T(8,128)(2,1)S(1)} %fusion.2.refs_0_), channel_id=1, source_target_pairs={{0,8},{1,9},{2,10},{3,11},{4,12},{5,13},{6,14},{7,15},{8,0},{9,1},... | collective-permute-start | bytes 786440 | tf_op jit(solution)/shard_map/ppermute | solution.py:44
  132.6 0.7 collective-permute-start.20
  149.1 3.5 %collective-permute-start.21 = (bf16[4,256,128]{2,1,0:T(8,128)(2,1)S(1)}, bf16[4,256,128]{2,1,0:T(8,128)(2,1)S(1)}, u32[]{:S(2)}, u32[]{:S(2)}) collective-permute-start(bf16[4,256,128]{2,1,0:T(8,128)(2,1)S(1)} %get-tuple-element.15), channel_id=1, source_target_pairs={{0,8},{1,9},{2,10},{3,11},{4,12},{5,13},{6,14},{7,15},{8,0},{9,1},... | collective-permute-start | bytes 786440 | tf_op jit(solution)/shard_map/ppermute | solution.py:44
  152.7 9.0 %collective-permute-start.22 = (bf16[2,256,128]{2,1,0:T(8,128)(2,1)S(1)}, bf16[2,256,128]{2,1,0:T(8,128)(2,1)S(1)}, u32[]{:S(2)}, u32[]{:S(2)}) collective-permute-start(bf16[2,256,128]{2,1,0:T(8,128)(2,1)S(1)} %get-tuple-element.35), channel_id=1, source_target_pairs={{0,16},{1,17},{2,18},{3,19},{4,20},{5,21},{6,22},{7,23},{8,24},{9,... | collective-permute-start | bytes 393224 | tf_op jit(solution)/shard_map/ppermute | solution.py:44
  153.1 8.5 %collective-permute-start.25 = (bf16[2,256,128]{2,1,0:T(8,128)(2,1)S(1)}, bf16[2,256,128]{2,1,0:T(8,128)(2,1)S(1)}, u32[]{:S(2)}, u32[]{:S(2)}) collective-permute-start(bf16[2,256,128]{2,1,0:T(8,128)(2,1)S(1)} %get-tuple-element.36), channel_id=1, source_target_pairs={{0,48},{1,49},{2,50},{3,51},{4,52},{5,53},{6,54},{7,55},{8,56},{9,... | collective-permute-start | bytes 393224 | tf_op jit(solution)/shard_map/ppermute | solution.py:44
  161.7 2.7 collective-permute-start.23
  162.4 2.0 collective-permute-start.24
  163.1 1.4 collective-permute-start.26
  163.8 0.7 collective-permute-start.27
  164.6 2.9 %collective-permute-start.28 = (bf16[4,256,128]{2,1,0:T(8,128)(2,1)S(1)}, bf16[4,256,128]{2,1,0:T(8,128)(2,1)S(1)}, u32[]{:S(2)}, u32[]{:S(2)}) collective-permute-start(bf16[4,256,128]{2,1,0:T(8,128)(2,1)S(1)} %fusion.1.refs_0_), channel_id=1, source_target_pairs={{0,8},{1,9},{2,10},{3,11},{4,12},{5,13},{6,14},{7,15},{8,0},{9,1},... | collective-permute-start | bytes 786440 | tf_op jit(solution)/shard_map/ppermute | solution.py:44
  181.9 37.1 %collective-permute-start.29 = (bf16[256,128]{1,0:T(8,128)(2,1)S(1)}, bf16[256,128]{1,0:T(8,128)(2,1)S(1)}, u32[]{:S(2)}, u32[]{:S(2)}) collective-permute-start(bf16[256,128]{1,0:T(8,128)(2,1)S(1)} %fusion.21), channel_id=1, source_target_pairs={{64,0},{65,1},{66,2},{67,3},{68,4},{69,5},{70,6},{71,7},{72,8},{73... | collective-permute-start | bytes 196616 | tf_op jit(solution)/shard_map/ppermute | solution.py:44
  233.6 4.3 %collective-permute-start.30 = (bf16[4,256,128]{2,1,0:T(8,128)(2,1)S(1)}, bf16[4,256,128]{2,1,0:T(8,128)(2,1)S(1)}, u32[]{:S(2)}, u32[]{:S(2)}) collective-permute-start(bf16[4,256,128]{2,1,0:T(8,128)(2,1)S(1)} %get-tuple-element.17), channel_id=1, source_target_pairs={{0,8},{1,9},{2,10},{3,11},{4,12},{5,13},{6,14},{7,15},{8,0},{9,1},... | collective-permute-start | bytes 786440 | tf_op jit(solution)/shard_map/ppermute | solution.py:44
  238.0 9.2 %collective-permute-start.31 = (bf16[2,256,128]{2,1,0:T(8,128)(2,1)S(1)}, bf16[2,256,128]{2,1,0:T(8,128)(2,1)S(1)}, u32[]{:S(2)}, u32[]{:S(2)}) collective-permute-start(bf16[2,256,128]{2,1,0:T(8,128)(2,1)S(1)} %get-tuple-element.29), channel_id=1, source_target_pairs={{0,16},{1,17},{2,18},{3,19},{4,20},{5,21},{6,22},{7,23},{8,24},{9,... | collective-permute-start | bytes 393224 | tf_op jit(solution)/shard_map/ppermute | solution.py:44
  239.2 8.0 %collective-permute-start.33 = (bf16[2,256,128]{2,1,0:T(8,128)(2,1)S(1)}, bf16[2,256,128]{2,1,0:T(8,128)(2,1)S(1)}, u32[]{:S(2)}, u32[]{:S(2)}) collective-permute-start(bf16[2,256,128]{2,1,0:T(8,128)(2,1)S(1)} %get-tuple-element.30), channel_id=1, source_target_pairs={{0,48},{1,49},{2,50},{3,51},{4,52},{5,53},{6,54},{7,55},{8,56},{9,... | collective-permute-start | bytes 393224 | tf_op jit(solution)/shard_map/ppermute | solution.py:44
  247.3 7.7 %collective-permute-start.32 = (bf16[2,256,128]{2,1,0:T(8,128)(2,1)S(1)}, bf16[2,256,128]{2,1,0:T(8,128)(2,1)S(1)}, u32[]{:S(2)}, u32[]{:S(2)}) collective-permute-start(bf16[2,256,128]{2,1,0:T(8,128)(2,1)S(1)} %get-tuple-element.27), channel_id=1, source_target_pairs={{0,48},{1,49},{2,50},{3,51},{4,52},{5,53},{6,54},{7,55},{8,56},{9,... | collective-permute-start | bytes 393224 | tf_op jit(solution)/shard_map/ppermute | solution.py:44
  250.7 7.2 %collective-permute-start.34 = (bf16[2,256,128]{2,1,0:T(8,128)(2,1)S(1)}, bf16[2,256,128]{2,1,0:T(8,128)(2,1)S(1)}, u32[]{:S(2)}, u32[]{:S(2)}) collective-permute-start(bf16[2,256,128]{2,1,0:T(8,128)(2,1)S(1)} %get-tuple-element.28), channel_id=1, source_target_pairs={{0,16},{1,17},{2,18},{3,19},{4,20},{5,21},{6,22},{7,23},{8,24},{9,... | collective-permute-start | bytes 393224 | tf_op jit(solution)/shard_map/ppermute | solution.py:44
  258.1 2.4 collective-permute-start.35
  263.7 13.7 %all-to-all-start.7 = ((bf16[8,256,128]{2,1,0:T(8,128)(2,1)}), bf16[8,256,128]{2,1,0:T(8,128)(2,1)}, u32[]{:S(2)}, u32[]{:S(2)}) async-start(bf16[8,256,128]{2,1,0:T(8,128)(2,1)} %even_product.9), calls=%async_computation.7 | async-start | bytes 1048576 | tf_op jit(solution)/shard_map/all_to_all | solution.py:240
  268.9 6.7 %collective-permute-start.36 = (f32[256,128]{1,0:T(8,128)S(1)}, f32[256,128]{1,0:T(8,128)S(1)}, u32[]{:S(2)}, u32[]{:S(2)}) collective-permute-start(f32[256,128]{1,0:T(8,128)S(1)} %select_add_fusion.8), channel_id=1, source_target_pairs={{64,0},{65,1},{66,2},{67,3},{68,4},{69,5},{70,6},{71,7},{72,8},{73... | collective-permute-start | bytes 393224 | tf_op jit(solution)/shard_map/ppermute | solution.py:44
